TPU v7x, 32 devices: a whole 2x2x4 slice. The times are simulated.
32 devices in a mesh: panel: 8 (over y, x, core), rep: 4 (over z).
Axes of the slice: x: 2, y: 2, z: 4, core: 2. Of those that a mesh axis runs over, the one named last changes fastest.
Arguments:
- user_cot: float32 [4096, 256], P('rep'), may hold values from -6 to 6
- item_cot: float32 [8192, 256], P('panel'), may hold values from -6 to 6
- tile_vals: float32 [8, 4, 40, 128, 128], P('panel', 'rep'), may hold values from 0 to 0.0191815, as said below
- tile_rows: int32 [8, 4, 40], P('panel', 'rep'), may hold values from 0 to 7
- tile_cols: int32 [8, 4, 40], P('panel', 'rep'), may hold values from 0 to 7
- tile_count: int32 [8, 4], P('panel', 'rep'), may hold values from 1 to 40, as said below
Outputs:
- grad_user: float32 [4096, 256], P(('rep', 'panel'))
- grad_item: float32 [8192, 256], P(('panel', 'rep'))
Inputs may be any that keep to these rules, and one draw needn't show every extreme that they name: `tile_count`: at least one block has all 40 slots live. `tile_vals`: each tile has 2 to 10 percent nonzero entries; entries are nonnegative, near the inverse square root of a typical user degree times a typical item degree.
All inputs are finite; a program needn't handle non-finite values.
Results may differ from a plain program's by a relative error of at most 0.0001.
Values sent between devices are 32-bit elements; how exact they have to be, the bound alone decides.
No kernel may reach another device: no remote copies, remote signals or barrier semaphores. Data moves between devices by JAX's collectives and lax.ppermute only.
A program may use at most 64 MiB of HBM per device.

v0:
```python
import jax
import jax.numpy as jnp
from jax import lax
from jax.sharding import PartitionSpec as P

TILE = 128


exact_mode = lax.Precision.HIGHEST


def own_rows(full_rows, position, row_count):
    return lax.dynamic_slice_in_dim(full_rows, position * row_count, row_count, 0)


def per_device(user_cot, item_cot, tile_vals, tile_rows, tile_cols, tile_count):
    blocks = tile_vals[0, 0]
    row_ids = tile_rows[0, 0]
    col_ids = tile_cols[0, 0]
    feature = user_cot.shape[1]
    user_blocks = user_cot.shape[0] // TILE
    item_blocks = item_cot.shape[0] // TILE
    alive_mask = (jnp.arange(blocks.shape[0], dtype=jnp.int32) < tile_count[0, 0]).astype(
        jnp.float32
    )
    row_hits = (row_ids[None, :] == jnp.arange(user_blocks, dtype=jnp.int32)[:, None]).astype(
        jnp.float32
    ) * alive_mask[None, :]
    col_hits = (col_ids[None, :] == jnp.arange(item_blocks, dtype=jnp.int32)[:, None]).astype(
        jnp.float32
    ) * alive_mask[None, :]

    def to_users(items):
        picked = jnp.take(items.reshape(item_blocks, TILE, feature), col_ids, axis=0)
        product = jnp.einsum("tjk,tkw->tjw", blocks, picked, precision=exact_mode)
        summed = jnp.einsum("ut,tjw->ujw", row_hits, product, precision=exact_mode)
        return summed.reshape(user_blocks * TILE, feature)

    def to_items(users):
        picked = jnp.take(users.reshape(user_blocks, TILE, feature), row_ids, axis=0)
        product = jnp.einsum("tkj,tkw->tjw", blocks, picked, precision=exact_mode)
        summed = jnp.einsum("it,tjw->ijw", col_hits, product, precision=exact_mode)
        return summed.reshape(item_blocks * TILE, feature)

    user_third = user_cot / 3.0
    item_third = item_cot / 3.0
    item_terms = to_items(user_third)
    user_terms = to_users(item_third)
    user_part = user_cot.shape[0] // lax.axis_size("panel")
    item_part = item_cot.shape[0] // lax.axis_size("rep")
    item_mid = item_third + lax.psum(item_terms, "rep")
    user_mid = user_third + lax.psum(user_terms, "panel")
    grad_user = own_rows(user_third, lax.axis_index("panel"), user_part) + lax.psum_scatter(
        to_users(item_mid), "panel", scatter_dimension=0, tiled=True
    )
    grad_item = own_rows(item_third, lax.axis_index("rep"), item_part) + lax.psum_scatter(
        to_items(user_mid), "rep", scatter_dimension=0, tiled=True
    )
    return (grad_user, grad_item)


def solution(mesh):
    return jax.shard_map(
        per_device,
        mesh=mesh,
        in_specs=(
            P("rep", None),
            P("panel", None),
            P("panel", "rep", None, None, None),
            P("panel", "rep", None),
            P("panel", "rep", None),
            P("panel", "rep"),
        ),
        out_specs=(P(("rep", "panel"), None), P(("panel", "rep"), None)),
        check_vma=False,
    )
```

profile of v0, /device:TPU:0, one launch (start us, length us, event | category | flops | bytes accessed | tf_op | source)
XLA Modules:
  0.0 259.0 jit_solution(9302449628497952198)
XLA Ops:
  9.4 2.3 broadcast_multiply_fusion
  11.7 4.4 %gather_fusion.2 = f32[40,128,256]{2,1,0:T(8,128)} fusion(f32[8,128,256]{2,1,0:T(8,128)} %bitcast.49, s32[1024]{0:T(1024)S(1)} %pad_clamp_fusion), kind=kCustom, calls=%fused_computation.2.clone | custom fusion | bytes 10485920 | tf_op jit(solution)/shard_map/jit(_take)/gather | solution.py:34
  16.1 12.6 %fusion.10 = f32[40,256,128]{2,1,0:T(8,128)} fusion(f32[40,128,256]{2,1,0:T(8,128)} %gather_fusion.2, f32[1,1,40,128,128]{4,3,2,1,0:T(8,128)S(1)} %copy-done, pred[40]{0:T(512)(128)(4,1)S(1)} %get-tuple-element.5), kind=kOutput, calls=%fused_computation.14 | convolution fusion | flops 2014576640 | bytes 13107240 | tf_op jit(solution)/shard_map/tjk,tkw->tjw/dot_general | solution.py:35
  28.8 6.2 %copy.14 = f32[40,256,128]{1,0,2:T(8,128)} copy(f32[40,256,128]{2,1,0:T(8,128)} %fusion.10) | data formatting | bytes 10485760 | tf_op jit(solution)/shard_map/tjk,tkw->tjw/dot_general | solution.py:35
  34.9 4.5 %fusion.2 = f32[8,128,256]{2,0,1:T(8,128)S(1)} fusion(f32[40,256,128]{1,0,2:T(8,128)} %copy.14, f32[40]{0:T(128)S(1)} %compare_convert_fusion, s32[40]{0:T(128)S(1)} %bitcast.59), kind=kOutput, calls=%fused_computation.6 | convolution fusion | flops 125829760 | bytes 6291776 | tf_op jit(solution)/shard_map/ut,tjw->ujw/dot_general | solution.py:36
  41.0 59.2 %all-reduce.5.cloned.1.call-done = f32[1024,256]{1,0:T(8,128)} async-done(((f32[1024,256]{1,0:T(8,128)}), f32[1024,256]{1,0:T(8,128)}) %all-reduce.5.cloned.1.call-update) | async-done | bytes 1048592 | tf_op jit(solution)/shard_map/psum | solution.py:52
  100.3 3.1 %fusion.56 = (f32[1024,256]{1,0:T(8,128)}, f32[1024,256]{1,0:T(8,128)}) fusion(f32[1024,256]{1,0:T(8,128)} %all-reduce.5.cloned.1.call-done, f32[1024,256]{1,0:T(8,128)} %param.8), kind=kLoop, calls=%fused_computation.73 | loop fusion | flops 524288 | bytes 4194304 | tf_op jit(solution)/shard_map/add | solution.py:52
  103.4 4.4 %gather_fusion = f32[40,128,256]{2,1,0:T(8,128)} fusion(f32[8,128,256]{2,1,0:T(8,128)} %bitcast.50, s32[1024]{0:T(1024)S(1)} %pad_clamp_fusion.1), kind=kCustom, calls=%fused_computation.clone | custom fusion | bytes 10485920 | tf_op jit(solution)/shard_map/jit(_take)/gather | solution.py:40
  107.8 12.6 %fusion.14 = f32[40,256,128]{2,1,0:T(8,128)} fusion(f32[40,128,256]{2,1,0:T(8,128)} %gather_fusion, f32[1,1,40,128,128]{4,3,2,1,0:T(8,128)S(1)} %copy-done, pred[40]{0:T(512)(128)(4,1)S(1)} %get-tuple-element.6), kind=kOutput, calls=%fused_computation.18 | convolution fusion | flops 2014576640 | bytes 13107240 | tf_op jit(solution)/shard_map/tkj,tkw->tjw/dot_general | solution.py:41
  120.4 6.2 %copy.12 = f32[40,256,128]{1,0,2:T(8,128)} copy(f32[40,256,128]{2,1,0:T(8,128)} %fusion.14) | data formatting | bytes 10485760 | tf_op jit(solution)/shard_map/tkj,tkw->tjw/dot_general | solution.py:41
  126.6 4.5 %fusion.6 = f32[8,128,256]{2,0,1:T(8,128)S(1)} fusion(f32[40,256,128]{1,0,2:T(8,128)} %copy.12, s32[40]{0:T(128)S(1)} %bitcast.57, f32[40]{0:T(128)S(1)} %compare_convert_fusion), kind=kOutput, calls=%fused_computation.10 | convolution fusion | flops 125829760 | bytes 6291776 | tf_op jit(solution)/shard_map/it,tjw->ijw/dot_general | solution.py:42
  132.7 4.4 %gather_fusion.3 = f32[40,128,256]{2,1,0:T(8,128)} fusion(f32[8,128,256]{2,1,0:T(8,128)} %bitcast.52, s32[1024]{0:T(1024)S(1)} %pad_clamp_fusion.1), kind=kCustom, calls=%fused_computation.3.clone | custom fusion | bytes 10485920 | tf_op jit(solution)/shard_map/jit(_take)/gather | solution.py:40
  137.1 12.7 %fusion.8 = f32[40,256,128]{2,1,0:T(8,128)} fusion(f32[40,128,256]{2,1,0:T(8,128)} %gather_fusion.3, f32[1,1,40,128,128]{4,3,2,1,0:T(8,128)S(1)} %copy-done, pred[40]{0:T(512)(128)(4,1)S(1)} %get-tuple-element.6), kind=kOutput, calls=%fused_computation.12 | convolution fusion | flops 2014576640 | bytes 13107240 | tf_op jit(solution)/shard_map/tkj,tkw->tjw/dot_general | solution.py:41
  149.8 6.2 %copy.15 = f32[40,256,128]{1,0,2:T(8,128)} copy(f32[40,256,128]{2,1,0:T(8,128)} %fusion.8) | data formatting | bytes 10485760 | tf_op jit(solution)/shard_map/tkj,tkw->tjw/dot_general | solution.py:41
  156.0 4.5 %fusion = f32[8,128,256]{2,0,1:T(8,128)S(1)} fusion(f32[40,256,128]{1,0,2:T(8,128)} %copy.15, s32[40]{0:T(128)S(1)} %bitcast.58, f32[40]{0:T(128)S(1)} %compare_convert_fusion), kind=kOutput, calls=%fused_computation.4 | convolution fusion | flops 125829760 | bytes 6291776 | tf_op jit(solution)/shard_map/it,tjw->ijw/dot_general | solution.py:42
  162.2 21.3 %all-reduce.3.cloned.1.call-done = f32[1024,256]{1,0:T(8,128)} async-done(((f32[1024,256]{1,0:T(8,128)}), f32[1024,256]{1,0:T(8,128)}) %all-reduce.3.cloned.1.call-update) | async-done | bytes 1048592 | tf_op jit(solution)/shard_map/psum | solution.py:51
  183.5 2.7 %fusion.57 = f32[1024,256]{1,0:T(8,128)} fusion(f32[1024,256]{1,0:T(8,128)} %all-reduce.3.cloned.1.call-done, f32[1024,256]{1,0:T(8,128)} %param.9), kind=kLoop, calls=%fused_computation.74 | loop fusion | flops 524288 | bytes 3145728 | tf_op jit(solution)/shard_map/add | solution.py:51
  186.2 4.4 %gather_fusion.1 = f32[40,128,256]{2,1,0:T(8,128)} fusion(f32[8,128,256]{2,1,0:T(8,128)} %bitcast.51, s32[1024]{0:T(1024)S(1)} %pad_clamp_fusion), kind=kCustom, calls=%fused_computation.1.clone | custom fusion | bytes 10485920 | tf_op jit(solution)/shard_map/jit(_take)/gather | solution.py:34
  190.6 12.8 %fusion.12 = f32[40,256,128]{2,1,0:T(8,128)} fusion(f32[40,128,256]{2,1,0:T(8,128)} %gather_fusion.1, f32[1,1,40,128,128]{4,3,2,1,0:T(8,128)S(1)} %copy-done, pred[40]{0:T(512)(128)(4,1)S(1)} %get-tuple-element.5), kind=kOutput, calls=%fused_computation.16 | convolution fusion | flops 2014576640 | bytes 13107240 | tf_op jit(solution)/shard_map/tjk,tkw->tjw/dot_general | solution.py:35
  203.4 6.2 %copy.13 = f32[40,256,128]{1,0,2:T(8,128)} copy(f32[40,256,128]{2,1,0:T(8,128)} %fusion.12) | data formatting | bytes 10485760 | tf_op jit(solution)/shard_map/tjk,tkw->tjw/dot_general | solution.py:35
  209.5 4.5 %fusion.4 = f32[8,128,256]{2,0,1:T(8,128)S(1)} fusion(f32[40,256,128]{1,0,2:T(8,128)} %copy.13, f32[40]{0:T(128)S(1)} %compare_convert_fusion, s32[40]{0:T(128)S(1)} %bitcast.60), kind=kOutput, calls=%fused_computation.8 | convolution fusion | flops 125829760 | bytes 6291776 | tf_op jit(solution)/shard_map/ut,tjw->ujw/dot_general | solution.py:36
  215.4 1.8 dynamic-slice_add_fusion
  217.2 33.7 %reduce-scatter.3.cloned.1.call-done = f32[128,256]{1,0:T(8,128)} async-done(((f32[1024,256]{1,0:T(8,128)}), f32[128,256]{1,0:T(8,128)}) %reduce-scatter.3.cloned.1.call-update) | async-done | bytes 131088 | tf_op jit(solution)/shard_map/reduce_scatter | solution.py:53
  250.9 1.6 dynamic-slice_add_fusion.1
  (25 shorter events, 7.6 us)
Async XLA Ops:
  7.2 9.0 %copy-start = (f32[1,1,40,128,128]{4,3,2,1,0:T(8,128)S(1)}, f32[1,1,40,128,128]{4,3,2,1,0:T(8,128)}, u32[]{:S(2)}) copy-start(f32[1,1,40,128,128]{4,3,2,1,0:T(8,128)} %param.10) | copy-start | bytes 7864324
  7.2 93.1 %all-reduce.5.cloned.1.call-start = ((), (), s32[]{:S(2)}) async-start(), calls=%async_computation.4 | async-start | bytes 2097152 | tf_op jit(solution)/shard_map/psum | solution.py:52
  28.8 6.2 %copy-start.2 = (s32[1,1,40]{2,1,0:T(1,128)S(1)}, s32[1,1,40]{2,1,0:T(1,128)}, u32[]{:S(2)}) copy-start(s32[1,1,40]{2,1,0:T(1,128)} %param.11) | copy-start | bytes 484
  40.8 142.7 %all-reduce.3.cloned.1.call-start = ((), (), s32[]{:S(2)}) async-start(), calls=%async_computation.2 | async-start | bytes 2097152 | tf_op jit(solution)/shard_map/psum | solution.py:51
  120.4 6.2 %copy-start.1 = (s32[1,1,40]{2,1,0:T(1,128)S(1)}, s32[1,1,40]{2,1,0:T(1,128)}, u32[]{:S(2)}) copy-start(s32[1,1,40]{2,1,0:T(1,128)} %param.12) | copy-start | bytes 484
  132.4 82.9 %reduce-scatter.5.cloned.1.call-start = ((), (), s32[]{:S(2)}) async-start(), calls=%async_computation.5 | async-start | bytes 1310720 | tf_op jit(solution)/shard_map/reduce_scatter | solution.py:56
  161.9 89.0 %reduce-scatter.3.cloned.1.call-start = ((), (), s32[]{:S(2)}) async-start(), calls=%async_computation.3 | async-start | bytes 1179648 | tf_op jit(solution)/shard_map/reduce_scatter | solution.py:53
Sparse Core Ops, SparseCore 0:
  40.9 59.3 all-reduce.4
  132.6 50.8 all-reduce.2
  185.9 26.5 reduce-scatter.4
  215.5 35.3 reduce-scatter.2
where the time goes:
time: 260 us; the launch traced here: 259 us
  waiting for transfers between devices  114 us (44%)
  matrix products  68.7 us (26%)
  local copies, waits for them, and re-layouts  47.7 us (18%)
  between operations  14.6 us (6%)
  other arithmetic  12.9 us (5%)
    psum x1, waiting for transfers between devices, per_device(): user_mid = user_third + lax.psum(user_terms, 'panel')  59.2 us
    reduce_scatter x1, waiting for transfers between devices, per_device(): lax.psum_scatter(to_users(item_mid), 'panel', scatter_dimension=0, tiled=...  33.7 us
    dot_general x2, matrix products, to_users(): product = jnp.einsum('tjk,tkw->tjw', blocks, picked, precision=exact_mode)  25.5 us
    dot_general x2, matrix products, to_items(): product = jnp.einsum('tkj,tkw->tjw', blocks, picked, precision=exact_mode)  25.3 us
    psum x1, waiting for transfers between devices, per_device(): item_mid = item_third + lax.psum(item_terms, 'rep')  21.3 us
    dot_general x2, local copies, waits for them, and re-layouts, to_items(): product = jnp.einsum('tkj,tkw->tjw', blocks, picked, precision=exact_mode)  12.3 us
    dot_general x2, local copies, waits for them, and re-layouts, to_users(): product = jnp.einsum('tjk,tkw->tjw', blocks, picked, precision=exact_mode)  12.3 us
    dot_general x2, matrix products, to_items(): summed = jnp.einsum('it,tjw->ijw', col_hits, product, precision=exact_mode)  8.97 us
  transfers between devices with their start and end apart: 4, of which 3 were waited for; matrix products, arithmetic and copies ran while one was open for 24% of the time, Pallas kernels for 0%

commit v1 on v0

v1 whole, which is shorter than its diff:
```python
import jax
import jax.numpy as jnp
from jax import lax
from jax.experimental import pallas as pl
from jax.experimental.pallas import tpu as pltpu
from jax.sharding import PartitionSpec as P

TILE = 128
BLOCK = 256
CHUNKS = 2
VMEM_BYTES = 48 * 1024 * 1024
THIRD = 1.0 / 3.0
NEAR = (((1,), (0,)), ((), ()))


def halves(values):
    high = values.astype(jnp.bfloat16)
    low = (values - high.astype(jnp.float32)).astype(jnp.bfloat16)
    return high, low


def product(left, right):
    dot = lambda a, b: lax.dot_general(a, b, NEAR, preferred_element_type=jnp.float32)
    return dot(left[0], right[0]) + (dot(left[0], right[1]) + dot(left[1], right[0]))


def add_to_items(high_ref, low_ref, users, items_ref):
    users_t = halves(users.T)
    step = min(BLOCK, high_ref.shape[1])
    for start in range(0, high_ref.shape[1], step):
        here = pl.ds(start, step)
        items_ref[here, :] = product(users_t, (high_ref[:, here], low_ref[:, here])).T


def build_kernel(count_ref, rows_ref, cols_ref, tiles_ref, users_ref, high_ref, low_ref, items_ref, whole_ref):
    whole_ref[...] = jnp.zeros_like(whole_ref)

    @pl.loop(0, count_ref[0, 0])
    def _(t):
        row = pl.ds(pl.multiple_of(rows_ref[0, t] * TILE, TILE), TILE)
        col = pl.ds(pl.multiple_of(cols_ref[0, t] * TILE, TILE), TILE)
        whole_ref[row, col] += tiles_ref[t]

    step = min(BLOCK, whole_ref.shape[0])
    for start in range(0, whole_ref.shape[0], step):
        here = pl.ds(start, step)
        high_ref[here, :], low_ref[here, :] = halves(whole_ref[here, :])
    add_to_items(high_ref, low_ref, users_ref[...] * THIRD, items_ref)


def items_kernel(high_ref, low_ref, users_ref, items_ref):
    add_to_items(high_ref, low_ref, users_ref[...], items_ref)


def users_kernel(scale, high_ref, low_ref, items_ref, users_ref):
    items = halves(items_ref[...] * scale)
    step = min(BLOCK, high_ref.shape[0])
    for start in range(0, high_ref.shape[0], step):
        here = pl.ds(start, step)
        users_ref[here, :] = product((high_ref[here, :], low_ref[here, :]), items)


def call(kernel, out_shape, ins, scratch=(), smem=0, flops=0, moved=0):
    vmem = pl.BlockSpec(memory_space=pltpu.VMEM)
    return pl.pallas_call(
        kernel,
        out_shape=out_shape,
        in_specs=[pl.BlockSpec(memory_space=pltpu.SMEM)] * smem + [vmem] * (len(ins) - smem),
        out_specs=jax.tree.map(lambda _: vmem, out_shape),
        scratch_shapes=list(scratch),
        compiler_params=pltpu.CompilerParams(vmem_limit_bytes=VMEM_BYTES),
        cost_estimate=pl.CostEstimate(flops=flops, bytes_accessed=moved, transcendentals=0),
    )(*ins)


def swap(values, n_panel):
    return lax.ppermute(values, "panel", [(i, i ^ 1) for i in range(n_panel)])


def line_ring(values, n_panel, n_rep):
    at = lambda p, r: p * n_rep + r
    pairs = []
    for p in range(0, n_panel, 2):
        for r in range(n_rep):
            pairs.append((at(p, r), at(p, r + 1) if r < n_rep - 1 else at(p + 1, r)))
            pairs.append((at(p + 1, r), at(p + 1, r - 1) if r > 0 else at(p, r)))
    return lax.ppermute(values, ("panel", "rep"), pairs)


def bits_of(n_panel):
    count = (n_panel // 2).bit_length() - 1
    turned = [(k + count // 2) % count for k in range(count)]
    return [(k + 1, turned[k] + 1) for k in range(count)]


def across(values, n_panel, bits):
    return lax.ppermute(values, "panel", [(i, i ^ (1 << bits[i & 1])) for i in range(n_panel)])


def pick(values, index, axis=0):
    return lax.dynamic_index_in_dim(values, index, axis, keepdims=False)


def per_device(user_cot, item_cot, tile_vals, tile_rows, tile_cols, tile_count):
    n_panel, n_rep = lax.axis_size("panel"), lax.axis_size("rep")
    panel, rep = lax.axis_index("panel"), lax.axis_index("rep")
    core = panel & 1
    place = jnp.where(core == 0, rep, n_rep - 1 - rep)
    real = lambda q: jnp.where(core == 0, q, n_rep - 1 - q)
    n_user, feature = user_cot.shape
    n_item = item_cot.shape[0]
    tiles = tile_vals[0, 0]
    f32 = lambda *shape: jax.ShapeDtypeStruct(shape, jnp.float32)
    b16 = lambda *shape: jax.ShapeDtypeStruct(shape, jnp.bfloat16)
    flops = 6 * n_user * n_item * feature
    moved = 4 * (n_user * n_item + 2 * n_user * feature)

    high, low, item_part = call(
        build_kernel,
        (b16(n_user, n_item), b16(n_user, n_item), f32(n_item, feature)),
        (tile_count, tile_rows[0], tile_cols[0], tiles, user_cot),
        [pltpu.VMEM((n_user, n_item), jnp.float32)],
        smem=3,
        flops=flops,
        moved=moved,
    )

    def to_items(users):
        return call(items_kernel, f32(n_item, feature), (high, low, users), flops=flops, moved=moved)

    def to_users(items, scale):
        kernel = lambda *refs: users_kernel(scale, *refs)
        return call(kernel, f32(n_user, feature), (high, low, items), flops=flops, moved=moved)

    chunk = n_item // n_rep // CHUNKS

    def slices(values):
        return values.reshape(n_rep, CHUNKS, chunk, feature)

    def both(mine, theirs, q, c):
        at = real(jnp.clip(q, 0, n_rep - 1))
        return jnp.stack([pick(mine, at)[c], pick(theirs, at)[c]])

    mine = slices(item_part)
    theirs = slices(swap(item_part, n_panel))
    held = [None] * CHUNKS
    for t in range(1, n_rep):
        for c in range(CHUNKS):
            sent = both(mine, theirs, place + n_rep - t, c)
            if t > 1:
                sent += jnp.where(place > 0, held[c], 0.0)
            held[c] = line_ring(sent, n_panel, n_rep)
    total = []
    for c in range(CHUNKS):
        part = jnp.where(place > 0, held[c], 0.0)
        total.append(part + swap(part, n_panel)[::-1] + both(mine, theirs, place, c))

    user_part = to_users(item_cot, THIRD).reshape(2, n_user // 2, feature)
    user_half = pick(user_part, core) + swap(pick(user_part, 1 - core), n_panel)
    for bits in bits_of(n_panel):
        user_half += across(user_half, n_panel, bits)
    other_half = swap(user_half, n_panel)
    user_sum = jnp.where(
        core == 0, jnp.concatenate([user_half, other_half]), jnp.concatenate([other_half, user_half])
    )

    again = to_items(user_sum)
    mine2 = slices(again)
    theirs2 = slices(swap(again, n_panel))
    came = [[] for _ in range(CHUNKS)]
    for t in range(1, n_rep + 1):
        for c in range(CHUNKS):
            if t == 1:
                sent = total[c]
            else:
                sent = jnp.where(place > 0, came[c][-1], 0.0) + jnp.where(
                    place >= t - 1, 0.0, both(mine2, theirs2, place + n_rep - (t - 1), c)
                )
            came[c].append(line_ring(sent, n_panel, n_rep))

    gathered = []
    for c in range(CHUNKS):
        near = jnp.stack([came[c][t][0] for t in range(n_rep - 1)])
        far = swap(jnp.stack([came[c][t][1] for t in range(n_rep - 1)]), n_panel)
        below, above = jnp.where(core == 0, near, far), jnp.where(core == 0, far, near)
        line = jnp.concatenate([below[::-1], total[c][:1], above])
        gathered.append(lax.dynamic_slice_in_dim(line, n_rep - 1 - rep, n_rep, 0))
    item_sum = jnp.stack(gathered, 1).reshape(n_item, feature)

    parts = to_users(item_sum, 1.0)
    bits = bits_of(n_panel)
    width = n_user // n_panel
    count = len(bits)
    parts = parts.reshape((n_panel // 2, 2, width, feature))
    scattered = pick(parts, core, 1) + swap(pick(parts, 1 - core, 1), n_panel)
    scattered = scattered.reshape((2,) * count + (width, feature))
    orders = [[count - b[k] for b in bits] for k in (0, 1)]
    scattered = jnp.where(
        core == 0,
        scattered.transpose(orders[0] + [count, count + 1]),
        scattered.transpose(orders[1] + [count, count + 1]),
    )
    for pair in bits:
        own = (panel >> jnp.where(core == 0, pair[0], pair[1])) & 1
        scattered = pick(scattered, own) + across(pick(scattered, 1 - own), n_panel, pair)

    own_users = lambda values: lax.dynamic_slice_in_dim(values, panel * width, width, 0)
    grad_user = own_users(user_cot) * THIRD + own_users(user_sum) + scattered

    pieces = []
    own_items = pick(slices(item_cot), rep)
    own_again = pick(mine2, rep)
    for c in range(CHUNKS):
        part = jnp.where(place > 0, came[c][-1], 0.0)
        pieces.append(
            own_items[c] * THIRD + total[c][0] + own_again[c] + part[0] + swap(part[1], n_panel)
        )
    grad_item = jnp.concatenate(pieces)
    return (grad_user, grad_item)


def solution(mesh):
    return jax.shard_map(
        per_device,
        mesh=mesh,
        in_specs=(
            P("rep", None),
            P("panel", None),
            P("panel", "rep", None, None, None),
            P("panel", "rep", None),
            P("panel", "rep", None),
            P("panel", "rep"),
        ),
        out_specs=(P(("rep", "panel"), None), P(("panel", "rep"), None)),
        check_vma=False,
    )
```

time: 260 us -> 117 us (0.45)
  waiting for transfers between devices: 114 us -> 17.4 us
  matrix products: 68.7 us -> 0 us
  starting transfers between devices: 0.83 us -> 38.3 us
  local copies, waits for them, and re-layouts: 47.7 us -> 21.4 us
  Pallas kernels: 0 us -> 16.9 us
  between operations: 14.6 us -> 1.66 us
  other arithmetic: 12.9 us -> 20.7 us
    psum x2 -> x0, waiting for transfers between devices: 80.5 us -> none  [the longest x1 59.2 us: per_device(): user_mid = user_third + lax.psum(user_terms, 'panel')]
    dot_general x8 -> x0, matrix products: 68.7 us -> none  [the longest x2 25.5 us: to_users(): product = jnp.einsum('tjk,tkw->tjw', blocks, picked, precision=exact_mode)]
    ppermute x0 -> x29, starting transfers between devices: none -> 38.3 us  [the longest x14 29.1 us: line_ring(): return lax.ppermute(values, ('panel', 'rep'), pairs)]
    reduce_scatter x2 -> x0, waiting for transfers between devices: 33.7 us -> none  [the longest x1 33.7 us: per_device(): lax.psum_scatter(to_users(item_mid), 'panel', scatter_dimension=0, tiled=...]
    dot_general x8 -> x0, local copies, waits for them, and re-layouts: 30 us -> none  [the longest x2 12.3 us: to_items(): product = jnp.einsum('tkj,tkw->tjw', blocks, picked, precision=exact_mode)]
    gather x4 -> x0, local copies, waits for them, and re-layouts: 17.7 us -> none  [the longest x2 8.85 us: to_items(): jnp.take(users.reshape(user_blocks, TILE, feature), row_ids, axis=0)]
    ppermute x0 -> x29, waiting for transfers between devices: none -> 17.4 us  [the longest x14 9.81 us: line_ring(): return lax.ppermute(values, ('panel', 'rep'), pairs)]
    pallas_call x0 -> x4, Pallas kernels: none -> 16.9 us  [call(): pl.pallas_call(kernel, out_shape=out_shape, in_specs=[pl.BlockSpec(memory...]
  transfers between devices with their start and end apart: 4 -> 29, of which waited for: 3 -> 11; matrix products, arithmetic and copies ran while one was open for 24% -> 32% of each run, Pallas kernels for 0% -> 10%
where the time goes in v1:
time: 117 us; the launch traced here: 116 us
  starting transfers between devices  38.3 us (33%)
  local copies, waits for them, and re-layouts  21.4 us (18%)
  other arithmetic  20.7 us (18%)
  waiting for transfers between devices  17.4 us (15%)
  Pallas kernels  16.9 us (14%)
  between operations  1.66 us (1%)
    ppermute x14, starting transfers between devices, line_ring(): return lax.ppermute(values, ('panel', 'rep'), pairs)  29.1 us
    pallas_call x4, Pallas kernels, call(): pl.pallas_call(kernel, out_shape=out_shape, in_specs=[pl.BlockSpec(memory...  16.9 us
    ppermute x14, waiting for transfers between devices, line_ring(): return lax.ppermute(values, ('panel', 'rep'), pairs)  9.81 us
    slice x4, local copies, waits for them, and re-layouts, both(): return jnp.stack([pick(mine, at)[c], pick(theirs, at)[c]])  8.14 us
    ppermute x4, starting transfers between devices, across(): lax.ppermute(values, 'panel', [(i, i ^ 1 << bits[i & 1]) for i in range(n...  7 us
    ppermute x4, waiting for transfers between devices, across(): lax.ppermute(values, 'panel', [(i, i ^ 1 << bits[i & 1]) for i in range(n...  5.47 us
    slice x6, local copies, waits for them, and re-layouts, per_device(): near = jnp.stack([came[c][t][0] for t in range(n_rep - 1)])  4.01 us
    unnamed x30, local copies, waits for them, and re-layouts  3.34 us
  transfers between devices with their start and end apart: 29, of which 11 were waited for; matrix products, arithmetic and copies ran while one was open for 32% of the time, Pallas kernels for 10%

profile of v1, /device:TPU:0, one launch (start us, length us, event | category | flops | bytes accessed | tf_op | source)
XLA Modules:
  0.0 116.4 jit_solution(7364560734602682937)
XLA Ops:
  3.8 5.5 %shard_map.77 = (bf16[1024,1024]{1,0:T(8,128)(2,1)S(1)}, bf16[1024,1024]{1,0:T(8,128)(2,1)}, f32[1024,256]{1,0:T(8,128)}) custom-call(s32[1,1]{1,0:T(1,128)S(6)} %copy.10.count_ref, s32[1,40]{1,0:T(1,128)S(1)} %bitcast.142, s32[1,40]{1,0:T(1,128)S(1)} %bitcast.143, f32[40,128,128]{2,1,0:T(8,128)} %bitcast.146, f32[1024,256]{1,0:T(8,128)S(1)} %copy-done.1), custom_call_target="tpu_custom_call" | custom-call | flops 1610612736 | bytes 6291456 | tf_op jit(solution)/shard_map/pallas_call | solution.py:65
  9.7 3.4 %shard_map.78 = f32[1024,256]{1,0:T(8,128)S(1)} custom-call(bf16[1024,1024]{1,0:T(8,128)(2,1)S(1)} %get-tuple-element.5.refs_0_.high_ref, bf16[1024,1024]{1,0:T(8,128)(2,1)} %get-tuple-element.6.refs_1_.low_ref, f32[1024,256]{1,0:T(8,128)S(1)} %copy-done), custom_call_target="tpu_custom_call" | custom-call | flops 1610612736 | bytes 6291456 | tf_op jit(solution)/shard_map/pallas_call | solution.py:65
  14.1 2.1 %collective-permute-done = f32[512,256]{1,0:T(8,128)} collective-permute-done((f32[512,256]{1,0:T(8,128)}, f32[512,256]{1,0:T(8,128)}, u32[]{:S(2)}, u32[]{:S(2)}) %collective-permute-start) | collective-permute-done | bytes 524320 | tf_op jit(solution)/shard_map/ppermute | solution.py:77
  17.4 2.9 %collective-permute-start.1 = (f32[512,256]{1,0:T(8,128)S(1)}, f32[512,256]{1,0:T(8,128)S(1)}, u32[]{:S(2)}, u32[]{:S(2)}) collective-permute-start(f32[512,256]{1,0:T(8,128)S(1)} %bitcast_add_fusion.1), channel_id=1, source_target_pairs={{0,8},{4,20},{8,0},{12,28},{16,24},{20,4},{24,16},{28,12},{1,9},{5... | collective-permute-start | bytes 1572872 | tf_op jit(solution)/shard_map/ppermute | solution.py:97
  20.2 2.1 %dynamic-slice_bitcast_fusion.28 = (f32[1,128,256]{2,1,0:T(8,128)S(1)}, f32[1,128,256]{2,1,0:T(8,128)}, f32[1,128,256]{2,1,0:T(8,128)}, f32[1,128,256]{2,1,0:T(8...) fusion(f32[4,2,128,256]{3,2,1,0:T(8,128)} %bitcast.6, ...), kind=kLoop, calls=%fused_computation.91 | loop fusion | bytes 2097172 | tf_op jit(solution)/shard_map/slice | solution.py:142
  22.3 2.2 %dynamic-slice_bitcast_fusion.27 = (f32[1,128,256]{2,1,0:T(8,128)S(1)}, f32[1,128,256]{2,1,0:T(8,128)}, f32[1,128,256]{2,1,0:T(8,128)}, f32[1,128,256]{2,1,0:T(8...) fusion(f32[4,2,128,256]{3,2,1,0:T(8,128)} %bitcast.8, ...), kind=kLoop, calls=%fused_computation.90 | loop fusion | bytes 2097172 | tf_op jit(solution)/shard_map/slice | solution.py:142
  27.4 1.9 %collective-permute-start.2 = (f32[512,256]{1,0:T(8,128)S(1)}, f32[512,256]{1,0:T(8,128)S(1)}, u32[]{:S(2)}, u32[]{:S(2)}) collective-permute-start(f32[512,256]{1,0:T(8,128)S(1)} %add.192), channel_id=1, source_target_pairs={{0,16},{4,12},{8,24},{12,4},{16,0},{20,28},{24,8},{28,20},{1,17},{... | collective-permute-start | bytes 1572872 | tf_op jit(solution)/shard_map/ppermute | solution.py:97
  36.9 2.6 %collective-permute-start.15 = (f32[2,128,256]{2,1,0:T(8,128)S(1)}, f32[2,128,256]{2,1,0:T(8,128)S(1)}, u32[]{:S(2)}, u32[]{:S(2)}) collective-permute-start(f32[2,128,256]{2,1,0:T(8,128)S(1)} %maximum_add_fusion.4), channel_id=1, source_target_pairs={{0,1},{4,0},{1,2},{5,4},{2,3},{6,5},{3,7},{7,6},{8,9},{12,8},{9,10... | collective-permute-start | bytes 786440 | tf_op jit(solution)/shard_map/ppermute | solution.py:87
  41.5 1.9 %collective-permute-done.15 = f32[2,128,256]{2,1,0:T(8,128)S(1)} collective-permute-done((f32[2,128,256]{2,1,0:T(8,128)S(1)}, f32[2,128,256]{2,1,0:T(8,128)S(1)}, u32[]{:S(2)}, u32[]{:S(2)}) %collective-permute-start.15) | collective-permute-done | bytes 262176 | tf_op jit(solution)/shard_map/ppermute | solution.py:87
  43.5 2.5 %collective-permute-start.16 = (f32[2,128,256]{2,1,0:T(8,128)S(1)}, f32[2,128,256]{2,1,0:T(8,128)S(1)}, u32[]{:S(2)}, u32[]{:S(2)}) collective-permute-start(f32[2,128,256]{2,1,0:T(8,128)S(1)} %maximum_add_fusion.3), channel_id=1, source_target_pairs={{0,1},{4,0},{1,2},{5,4},{2,3},{6,5},{3,7},{7,6},{8,9},{12,8},{9,10... | collective-permute-start | bytes 786440 | tf_op jit(solution)/shard_map/ppermute | solution.py:87
  47.2 4.6 %shard_map.79 = f32[1024,256]{1,0:T(8,128)} custom-call(bf16[1024,1024]{1,0:T(8,128)(2,1)S(1)} %get-tuple-element.5.refs_0_.high_ref, bf16[1024,1024]{1,0:T(8,128)(2,1)} %get-tuple-element.6.refs_1_.low_ref, f32[1024,256]{1,0:T(8,128)S(1)} %maximum_select_fusion.users_ref), custom_call_target="tpu_custom_call" | custom-call | flops 1610612736 | bytes 6291456 | tf_op jit(solution)/shard_map/pallas_call | solution.py:65
  54.1 2.6 %collective-permute-start.9 = (f32[2,128,256]{2,1,0:T(8,128)S(1)}, f32[2,128,256]{2,1,0:T(8,128)S(1)}, u32[]{:S(2)}, u32[]{:S(2)}) collective-permute-start(f32[2,128,256]{2,1,0:T(8,128)S(1)} %maximum_add_fusion.2), channel_id=1, source_target_pairs={{0,1},{4,0},{1,2},{5,4},{2,3},{6,5},{3,7},{7,6},{8,9},{12,8},{9,10... | collective-permute-start | bytes 786440 | tf_op jit(solution)/shard_map/ppermute | solution.py:87
  59.6 1.9 %dynamic-slice_bitcast_fusion.7 = (f32[1,128,256]{2,1,0:T(8,128)}, f32[1,128,256]{2,1,0:T(8,128)S(1)}, f32[1,128,256]{2,1,0:T(8,128)S(1)}, f32[1,128,256]{2,1,0:...) fusion(f32[4,2,128,256]{3,2,1,0:T(8,128)} %bitcast.16, s32[]{:T(128)S(6)} %select_n.244, ...), kind=kLoop, calls=%fused_computation.66 | loop fusion | bytes 1572880 | tf_op jit(solution)/shard_map/slice | solution.py:142
  62.2 2.0 %dynamic-slice_bitcast_fusion.6 = (f32[1,128,256]{2,1,0:T(8,128)}, f32[1,128,256]{2,1,0:T(8,128)S(1)}, f32[1,128,256]{2,1,0:T(8,128)S(1)}, f32[1,128,256]{2,1,0:...) fusion(f32[4,2,128,256]{3,2,1,0:T(8,128)} %bitcast.18, s32[]{:T(128)S(6)} %select_n.244, ...), kind=kLoop, calls=%fused_computation.65 | loop fusion | bytes 1572880 | tf_op jit(solution)/shard_map/slice | solution.py:142
  64.2 1.9 %collective-permute-start.19 = (f32[2,128,256]{2,1,0:T(8,128)S(1)}, f32[2,128,256]{2,1,0:T(8,128)S(1)}, u32[]{:S(2)}, u32[]{:S(2)}) collective-permute-start(f32[2,128,256]{2,1,0:T(8,128)S(1)} %fusion.12), channel_id=1, source_target_pairs={{0,1},{4,0},{1,2},{5,4},{2,3},{6,5},{3,7},{7,6},{8,9},{12,8},{9,10... | collective-permute-start | bytes 786440 | tf_op jit(solution)/shard_map/ppermute | solution.py:87
  70.0 2.5 %collective-permute-start.20 = (f32[2,128,256]{2,1,0:T(8,128)S(1)}, f32[2,128,256]{2,1,0:T(8,128)S(1)}, u32[]{:S(2)}, u32[]{:S(2)}) collective-permute-start(f32[2,128,256]{2,1,0:T(8,128)S(1)} %fusion.13), channel_id=1, source_target_pairs={{0,1},{4,0},{1,2},{5,4},{2,3},{6,5},{3,7},{7,6},{8,9},{12,8},{9,10... | collective-permute-start | bytes 786440 | tf_op jit(solution)/shard_map/ppermute | solution.py:87
  72.8 2.5 %collective-permute-start.12 = (f32[2,128,256]{2,1,0:T(8,128)S(1)}, f32[2,128,256]{2,1,0:T(8,128)S(1)}, u32[]{:S(2)}, u32[]{:S(2)}) collective-permute-start(f32[2,128,256]{2,1,0:T(8,128)S(1)} %fusion.11), channel_id=1, source_target_pairs={{0,1},{4,0},{1,2},{5,4},{2,3},{6,5},{3,7},{7,6},{8,9},{12,8},{9,10... | collective-permute-start | bytes 786440 | tf_op jit(solution)/shard_map/ppermute | solution.py:87
  76.7 2.6 %collective-permute-done.12 = f32[2,128,256]{2,1,0:T(8,128)S(1)} collective-permute-done((f32[2,128,256]{2,1,0:T(8,128)S(1)}, f32[2,128,256]{2,1,0:T(8,128)S(1)}, u32[]{:S(2)}, u32[]{:S(2)}) %collective-permute-start.12) | collective-permute-done | bytes 262176 | tf_op jit(solution)/shard_map/ppermute | solution.py:87
  88.2 2.5 %collective-permute-start.27 = (f32[2,128,256]{2,1,0:T(8,128)}, f32[2,128,256]{2,1,0:T(8,128)}, u32[]{:S(2)}, u32[]{:S(2)}) collective-permute-start(f32[2,128,256]{2,1,0:T(8,128)} %fusion.15), channel_id=1, source_target_pairs={{0,1},{4,0},{1,2},{5,4},{2,3},{6,5},{3,7},{7,6},{8,9},{12,8},{9,10... | collective-permute-start | bytes 786440 | tf_op jit(solution)/shard_map/ppermute | solution.py:87
  90.7 2.6 %fusion.6 = (f32[3,128,256]{2,1,0:T(8,128)}, f32[3,128,256]{2,1,0:T(8,128)}, f32[3,128,256]{2,1,0:T(8,128)S(1)}, f32[3,128,256]{2,1,0:T(8,128)}) fusion(f32[3,128,256]{2,1,0:T(8,128)} %collective-permute-done.21, f32[1,128,256]{2,1,0:T(8,128)} %get-tuple-element.52, f32[1,128,256]{2,1,0:T(8,128)} %get-tuple-element.50, f32[1,128,256]{2,1,0:T(8,128)} %get-tuple-element.48, ...), kind=kLoop, calls=%fused_computation.23 | loop fusion | flops 786432 | bytes 3145729 | tf_op jit(solution)/shard_map/jit(_where)/select_n | solution.py:185
  97.5 3.4 %shard_map.80 = f32[1024,256]{1,0:T(8,128)S(1)} custom-call(bf16[1024,1024]{1,0:T(8,128)(2,1)S(1)} %get-tuple-element.5.refs_0_.high_ref, bf16[1024,1024]{1,0:T(8,128)(2,1)} %get-tuple-element.6.refs_1_.low_ref, f32[1024,256]{1,0:T(8,128)S(1)} %bitcast.140), custom_call_target="tpu_custom_call" | custom-call | flops 1610612736 | bytes 6291456 | tf_op jit(solution)/shard_map/pallas_call | solution.py:65
  104.7 2.1 %collective-permute-done.25 = f32[2,128,256]{2,1,0:T(8,128)S(1)} collective-permute-done((f32[2,128,256]{2,1,0:T(8,128)S(1)}, f32[2,128,256]{2,1,0:T(8,128)S(1)}, u32[]{:S(2)}, u32[]{:S(2)}) %collective-permute-start.25) | collective-permute-done | bytes 262176 | tf_op jit(solution)/shard_map/ppermute | solution.py:87
  107.3 2.4 %collective-permute-done.23 = f32[2,128,256]{2,1,0:T(8,128)S(1)} collective-permute-done((f32[2,128,256]{2,1,0:T(8,128)S(1)}, f32[2,128,256]{2,1,0:T(8,128)S(1)}, u32[]{:S(2)}, u32[]{:S(2)}) %collective-permute-start.23) | collective-permute-done | bytes 262176 | tf_op jit(solution)/shard_map/ppermute | solution.py:97
  112.5 2.3 %collective-permute-done.24 = f32[128,256]{1,0:T(8,128)S(1)} collective-permute-done((f32[128,256]{1,0:T(8,128)S(1)}, f32[128,256]{1,0:T(8,128)S(1)}, u32[]{:S(2)}, u32[]{:S(2)}) %collective-permute-start.24) | collective-permute-done | bytes 131104 | tf_op jit(solution)/shard_map/ppermute | solution.py:97
  (122 shorter events, 51.8 us)
Async XLA Ops:
  9.4 13.0 %collective-permute-start.4 = (f32[1024,256]{1,0:T(8,128)}, f32[1024,256]{1,0:T(8,128)}, u32[]{:S(2)}, u32[]{:S(2)}) collective-permute-start(f32[1024,256]{1,0:T(8,128)} %get-tuple-element.7), channel_id=1, source_target_pairs={{0,4},{4,0},{8,12},{12,8},{16,20},{20,16},{24,28},{28,24},{1,5},{5... | collective-permute-start | bytes 3145736 | tf_op jit(solution)/shard_map/ppermute | solution.py:77
  17.4 10.0 %collective-permute-start.1 = (f32[512,256]{1,0:T(8,128)S(1)}, f32[512,256]{1,0:T(8,128)S(1)}, u32[]{:S(2)}, u32[]{:S(2)}) collective-permute-start(f32[512,256]{1,0:T(8,128)S(1)} %bitcast_add_fusion.1), channel_id=1, source_target_pairs={{0,8},{4,20},{8,0},{12,28},{16,24},{20,4},{24,16},{28,12},{1,9},{5... | collective-permute-start | bytes 1572872 | tf_op jit(solution)/shard_map/ppermute | solution.py:97
  25.2 6.5 %collective-permute-start.5 = (f32[2,128,256]{2,1,0:T(8,128)}, f32[2,128,256]{2,1,0:T(8,128)}, u32[]{:S(2)}, u32[]{:S(2)}) collective-permute-start(f32[2,128,256]{2,1,0:T(8,128)} %pad_maximum_fusion.5), channel_id=1, source_target_pairs={{0,1},{4,0},{1,2},{5,4},{2,3},{6,5},{3,7},{7,6},{8,9},{12,8},{9,10... | collective-permute-start | bytes 786440 | tf_op jit(solution)/shard_map/ppermute | solution.py:87
  27.4 12.1 %collective-permute-start.2 = (f32[512,256]{1,0:T(8,128)S(1)}, f32[512,256]{1,0:T(8,128)S(1)}, u32[]{:S(2)}, u32[]{:S(2)}) collective-permute-start(f32[512,256]{1,0:T(8,128)S(1)} %add.192), channel_id=1, source_target_pairs={{0,16},{4,12},{8,24},{12,4},{16,0},{20,28},{24,8},{28,20},{1,17},{... | collective-permute-start | bytes 1572872 | tf_op jit(solution)/shard_map/ppermute | solution.py:97
  30.1 5.8 %collective-permute-start.14 = (f32[2,128,256]{2,1,0:T(8,128)}, f32[2,128,256]{2,1,0:T(8,128)}, u32[]{:S(2)}, u32[]{:S(2)}) collective-permute-start(f32[2,128,256]{2,1,0:T(8,128)} %pad_maximum_fusion.6), channel_id=1, source_target_pairs={{0,1},{4,0},{1,2},{5,4},{2,3},{6,5},{3,7},{7,6},{8,9},{12,8},{9,10... | collective-permute-start | bytes 786440 | tf_op jit(solution)/shard_map/ppermute | solution.py:87
  32.8 6.9 %collective-permute-start.6 = (f32[2,128,256]{2,1,0:T(8,128)S(1)}, f32[2,128,256]{2,1,0:T(8,128)S(1)}, u32[]{:S(2)}, u32[]{:S(2)}) collective-permute-start(f32[2,128,256]{2,1,0:T(8,128)S(1)} %maximum_add_fusion.1), channel_id=1, source_target_pairs={{0,1},{4,0},{1,2},{5,4},{2,3},{6,5},{3,7},{7,6},{8,9},{12,8},{9,10... | collective-permute-start | bytes 786440 | tf_op jit(solution)/shard_map/ppermute | solution.py:87
  36.9 6.5 %collective-permute-start.15 = (f32[2,128,256]{2,1,0:T(8,128)S(1)}, f32[2,128,256]{2,1,0:T(8,128)S(1)}, u32[]{:S(2)}, u32[]{:S(2)}) collective-permute-start(f32[2,128,256]{2,1,0:T(8,128)S(1)} %maximum_add_fusion.4), channel_id=1, source_target_pairs={{0,1},{4,0},{1,2},{5,4},{2,3},{6,5},{3,7},{7,6},{8,9},{12,8},{9,10... | collective-permute-start | bytes 786440 | tf_op jit(solution)/shard_map/ppermute | solution.py:87
  39.6 7.4 %collective-permute-start.3 = (f32[512,256]{1,0:T(8,128)S(1)}, f32[512,256]{1,0:T(8,128)S(1)}, u32[]{:S(2)}, u32[]{:S(2)}) collective-permute-start(f32[512,256]{1,0:T(8,128)S(1)} %add.193), channel_id=1, source_target_pairs={{0,4},{4,0},{8,12},{12,8},{16,20},{20,16},{24,28},{28,24},{1,5},{5... | collective-permute-start | bytes 1572872 | tf_op jit(solution)/shard_map/ppermute | solution.py:77
  39.8 6.5 %collective-permute-start.7 = (f32[2,128,256]{2,1,0:T(8,128)S(1)}, f32[2,128,256]{2,1,0:T(8,128)S(1)}, u32[]{:S(2)}, u32[]{:S(2)}) collective-permute-start(f32[2,128,256]{2,1,0:T(8,128)S(1)} %maximum_add_fusion), channel_id=1, source_target_pairs={{0,1},{4,0},{1,2},{5,4},{2,3},{6,5},{3,7},{7,6},{8,9},{12,8},{9,10... | collective-permute-start | bytes 786440 | tf_op jit(solution)/shard_map/ppermute | solution.py:87
  43.5 8.7 %collective-permute-start.16 = (f32[2,128,256]{2,1,0:T(8,128)S(1)}, f32[2,128,256]{2,1,0:T(8,128)S(1)}, u32[]{:S(2)}, u32[]{:S(2)}) collective-permute-start(f32[2,128,256]{2,1,0:T(8,128)S(1)} %maximum_add_fusion.3), channel_id=1, source_target_pairs={{0,1},{4,0},{1,2},{5,4},{2,3},{6,5},{3,7},{7,6},{8,9},{12,8},{9,10... | collective-permute-start | bytes 786440 | tf_op jit(solution)/shard_map/ppermute | solution.py:87
  47.0 6.0 %collective-permute-start.8 = (f32[2,128,256]{2,1,0:T(8,128)}, f32[2,128,256]{2,1,0:T(8,128)}, u32[]{:S(2)}, u32[]{:S(2)}) collective-permute-start(f32[2,128,256]{2,1,0:T(8,128)} %broadcast_select_fusion.3), channel_id=1, source_target_pairs={{0,4},{4,0},{8,12},{12,8},{16,20},{20,16},{24,28},{28,24},{1,5},{5... | collective-permute-start | bytes 786440 | tf_op jit(solution)/shard_map/ppermute | solution.py:77
  51.8 10.4 %collective-permute-start.10 = (f32[1024,256]{1,0:T(8,128)}, f32[1024,256]{1,0:T(8,128)}, u32[]{:S(2)}, u32[]{:S(2)}) collective-permute-start(f32[1024,256]{1,0:T(8,128)} %shard_map.79), channel_id=1, source_target_pairs={{0,4},{4,0},{8,12},{12,8},{16,20},{20,16},{24,28},{28,24},{1,5},{5... | collective-permute-start | bytes 3145736 | tf_op jit(solution)/shard_map/ppermute | solution.py:77
  54.1 7.4 %collective-permute-start.9 = (f32[2,128,256]{2,1,0:T(8,128)S(1)}, f32[2,128,256]{2,1,0:T(8,128)S(1)}, u32[]{:S(2)}, u32[]{:S(2)}) collective-permute-start(f32[2,128,256]{2,1,0:T(8,128)S(1)} %maximum_add_fusion.2), channel_id=1, source_target_pairs={{0,1},{4,0},{1,2},{5,4},{2,3},{6,5},{3,7},{7,6},{8,9},{12,8},{9,10... | collective-permute-start | bytes 786440 | tf_op jit(solution)/shard_map/ppermute | solution.py:87
  57.8 6.3 %collective-permute-start.18 = (f32[2,128,256]{2,1,0:T(8,128)S(1)}, f32[2,128,256]{2,1,0:T(8,128)S(1)}, u32[]{:S(2)}, u32[]{:S(2)}) collective-permute-start(f32[2,128,256]{2,1,0:T(8,128)S(1)} %maximum_add_fusion.5), channel_id=1, source_target_pairs={{0,1},{4,0},{1,2},{5,4},{2,3},{6,5},{3,7},{7,6},{8,9},{12,8},{9,10... | collective-permute-start | bytes 786440 | tf_op jit(solution)/shard_map/ppermute | solution.py:87
  64.2 5.8 %collective-permute-start.19 = (f32[2,128,256]{2,1,0:T(8,128)S(1)}, f32[2,128,256]{2,1,0:T(8,128)S(1)}, u32[]{:S(2)}, u32[]{:S(2)}) collective-permute-start(f32[2,128,256]{2,1,0:T(8,128)S(1)} %fusion.12), channel_id=1, source_target_pairs={{0,1},{4,0},{1,2},{5,4},{2,3},{6,5},{3,7},{7,6},{8,9},{12,8},{9,10... | collective-permute-start | bytes 786440 | tf_op jit(solution)/shard_map/ppermute | solution.py:87
  66.1 6.7 %collective-permute-start.11 = (f32[2,128,256]{2,1,0:T(8,128)S(1)}, f32[2,128,256]{2,1,0:T(8,128)S(1)}, u32[]{:S(2)}, u32[]{:S(2)}) collective-permute-start(f32[2,128,256]{2,1,0:T(8,128)S(1)} %fusion.10), channel_id=1, source_target_pairs={{0,1},{4,0},{1,2},{5,4},{2,3},{6,5},{3,7},{7,6},{8,9},{12,8},{9,10... | collective-permute-start | bytes 786440 | tf_op jit(solution)/shard_map/ppermute | solution.py:87
  70.0 11.4 %collective-permute-start.20 = (f32[2,128,256]{2,1,0:T(8,128)S(1)}, f32[2,128,256]{2,1,0:T(8,128)S(1)}, u32[]{:S(2)}, u32[]{:S(2)}) collective-permute-start(f32[2,128,256]{2,1,0:T(8,128)S(1)} %fusion.13), channel_id=1, source_target_pairs={{0,1},{4,0},{1,2},{5,4},{2,3},{6,5},{3,7},{7,6},{8,9},{12,8},{9,10... | collective-permute-start | bytes 786440 | tf_op jit(solution)/shard_map/ppermute | solution.py:87
  72.8 6.4 %collective-permute-start.12 = (f32[2,128,256]{2,1,0:T(8,128)S(1)}, f32[2,128,256]{2,1,0:T(8,128)S(1)}, u32[]{:S(2)}, u32[]{:S(2)}) collective-permute-start(f32[2,128,256]{2,1,0:T(8,128)S(1)} %fusion.11), channel_id=1, source_target_pairs={{0,1},{4,0},{1,2},{5,4},{2,3},{6,5},{3,7},{7,6},{8,9},{12,8},{9,10... | collective-permute-start | bytes 786440 | tf_op jit(solution)/shard_map/ppermute | solution.py:87
  81.4 9.2 %collective-permute-start.13 = (f32[3,128,256]{2,1,0:T(8,128)}, f32[3,128,256]{2,1,0:T(8,128)}, u32[]{:S(2)}, u32[]{:S(2)}) collective-permute-start(f32[3,128,256]{2,1,0:T(8,128)} %pad_maximum_fusion.2), channel_id=1, source_target_pairs={{0,4},{4,0},{8,12},{12,8},{16,20},{20,16},{24,28},{28,24},{1,5},{5... | collective-permute-start | bytes 1179656 | tf_op jit(solution)/shard_map/ppermute | solution.py:77
  82.9 7.8 %collective-permute-start.21 = (f32[3,128,256]{2,1,0:T(8,128)}, f32[3,128,256]{2,1,0:T(8,128)}, u32[]{:S(2)}, u32[]{:S(2)}) collective-permute-start(f32[3,128,256]{2,1,0:T(8,128)} %pad_maximum_fusion.4), channel_id=1, source_target_pairs={{0,4},{4,0},{8,12},{12,8},{16,20},{20,16},{24,28},{28,24},{1,5},{5... | collective-permute-start | bytes 1179656 | tf_op jit(solution)/shard_map/ppermute | solution.py:77
  88.2 14.8 %collective-permute-start.27 = (f32[2,128,256]{2,1,0:T(8,128)}, f32[2,128,256]{2,1,0:T(8,128)}, u32[]{:S(2)}, u32[]{:S(2)}) collective-permute-start(f32[2,128,256]{2,1,0:T(8,128)} %fusion.15), channel_id=1, source_target_pairs={{0,1},{4,0},{1,2},{5,4},{2,3},{6,5},{3,7},{7,6},{8,9},{12,8},{9,10... | collective-permute-start | bytes 786440 | tf_op jit(solution)/shard_map/ppermute | solution.py:87
  101.1 5.7 %collective-permute-start.25 = (f32[2,128,256]{2,1,0:T(8,128)S(1)}, f32[2,128,256]{2,1,0:T(8,128)S(1)}, u32[]{:S(2)}, u32[]{:S(2)}) collective-permute-start(f32[2,128,256]{2,1,0:T(8,128)S(1)} %fusion.14), channel_id=1, source_target_pairs={{0,1},{4,0},{1,2},{5,4},{2,3},{6,5},{3,7},{7,6},{8,9},{12,8},{9,10... | collective-permute-start | bytes 786440 | tf_op jit(solution)/shard_map/ppermute | solution.py:87
  103.0 7.6 %collective-permute-start.28 = (f32[128,256]{1,0:T(8,128)S(1)}, f32[128,256]{1,0:T(8,128)S(1)}, u32[]{:S(2)}, u32[]{:S(2)}) collective-permute-start(f32[128,256]{1,0:T(8,128)S(1)} %slice_bitcast_fusion), channel_id=1, source_target_pairs={{0,4},{4,0},{8,12},{12,8},{16,20},{20,16},{24,28},{28,24},{1,5},{5... | collective-permute-start | bytes 393224 | tf_op jit(solution)/shard_map/ppermute | solution.py:77
  103.3 6.4 %collective-permute-start.23 = (f32[2,128,256]{2,1,0:T(8,128)S(1)}, f32[2,128,256]{2,1,0:T(8,128)S(1)}, u32[]{:S(2)}, u32[]{:S(2)}) collective-permute-start(f32[2,128,256]{2,1,0:T(8,128)S(1)} %dynamic-slice_bitcast_fusion.2), channel_id=1, source_target_pairs={{0,8},{4,20},{8,0},{12,28},{16,24},{20,4},{24,16},{28,12},{1,9},{5... | collective-permute-start | bytes 786440 | tf_op jit(solution)/shard_map/ppermute | solution.py:97
  (20 other events, 86.5 us)

commit v2 on v0

v2 whole, which is shorter than its diff:
```python
import jax
import jax.numpy as jnp
from jax import lax
from jax.experimental import pallas as pl
from jax.experimental.pallas import tpu as pltpu
from jax.sharding import PartitionSpec as P

TILE = 128
BLOCK = 256
VMEM_BYTES = 20 * 1024 * 1024
THIRD = 1.0 / 3.0
NEAR = (((1,), (0,)), ((), ()))


def halves(values):
    high = values.astype(jnp.bfloat16)
    low = (values - high.astype(jnp.float32)).astype(jnp.bfloat16)
    return high, low


def product(left, right):
    dot = lambda a, b: lax.dot_general(a, b, NEAR, preferred_element_type=jnp.float32)
    return dot(left[0], right[0]) + (dot(left[0], right[1]) + dot(left[1], right[0]))


def blocks_of(size):
    step = min(BLOCK, size)
    return [pl.ds(start, step) for start in range(0, size, step)]


def build(count_ref, rows_ref, cols_ref, tiles_ref, whole_ref, high_ref, low_ref):
    whole_ref[...] = jnp.zeros_like(whole_ref)

    @pl.loop(0, count_ref[0, 0])
    def _(t):
        row = pl.ds(pl.multiple_of(rows_ref[0, t] * TILE, TILE), TILE)
        col = pl.ds(pl.multiple_of(cols_ref[0, t] * TILE, TILE), TILE)
        whole_ref[row, col] += tiles_ref[t]

    for here in blocks_of(whole_ref.shape[0]):
        high_ref[here, :], low_ref[here, :] = halves(whole_ref[here, :])


def transposed_product(high_ref, low_ref, users, full_ref, slice_refs):
    users_t = halves(users.T)
    for here in blocks_of(high_ref.shape[1]):
        full_ref[here, :] = product(users_t, (high_ref[:, here], low_ref[:, here])).T
    rep = lax.axis_index("rep")
    size = slice_refs[0].shape[0]
    for m, slice_ref in enumerate(slice_refs):
        slice_ref[...] = full_ref[pl.ds(pl.multiple_of((rep ^ m) * size, size), size), :]


def first_items_kernel(count_ref, rows_ref, cols_ref, tiles_ref, users_ref, high_ref, low_ref, *rest):
    *slice_refs, whole_ref, full_ref = rest
    build(count_ref, rows_ref, cols_ref, tiles_ref, whole_ref, high_ref, low_ref)
    transposed_product(high_ref, low_ref, users_ref[...] * THIRD, full_ref, slice_refs)


def user_block(chip, core, width):
    return pl.ds(pl.multiple_of((2 * chip + core) * width, width), width)


def second_items_kernel(high_ref, low_ref, mine_ref, other_ref, *rest):
    *slice_refs, users_ref, full_ref = rest
    core = lax.axis_index("panel") & 1
    for chip in range(mine_ref.shape[0]):
        width = mine_ref.shape[1]
        users_ref[user_block(chip, core, width), :] = mine_ref[chip]
        users_ref[user_block(chip, 1 - core, width), :] = other_ref[chip]
    transposed_product(high_ref, low_ref, users_ref[...], full_ref, slice_refs)


def users_product(high_ref, low_ref, items, full_ref):
    for here in blocks_of(high_ref.shape[0]):
        full_ref[here, :] = product((high_ref[here, :], low_ref[here, :]), items)


def first_users_kernel(high_ref, low_ref, items_ref, mine_ref, other_ref, full_ref):
    users_product(high_ref, low_ref, halves(items_ref[...] * THIRD), full_ref)
    core = lax.axis_index("panel") & 1
    chips, width = mine_ref.shape[:2]
    for chip in range(chips):
        mine_ref[chip] = full_ref[user_block(chip, core, width), :]
        other_ref[chip] = full_ref[user_block(chip, 1 - core, width), :]


def second_users_kernel(high_ref, low_ref, *rest):
    *slice_refs, mine_ref, other_ref, items_ref, full_ref = rest
    rep, panel = lax.axis_index("rep"), lax.axis_index("panel")
    size = slice_refs[0].shape[0]
    for m, slice_ref in enumerate(slice_refs):
        items_ref[pl.ds(pl.multiple_of((rep ^ m) * size, size), size), :] = slice_ref[...]
    users_product(high_ref, low_ref, halves(items_ref[...]), full_ref)
    core, place = panel & 1, panel >> 1
    chips, width = mine_ref.shape[:2]
    for m in range(chips):
        mine_ref[m] = full_ref[user_block(place ^ m, core, width), :]
        other_ref[m] = full_ref[user_block(place ^ m, 1 - core, width), :]


def call(kernel, out_shape, ins, scratch=(), smem=0, flops=0, moved=0):
    vmem = pl.BlockSpec(memory_space=pltpu.VMEM)
    return pl.pallas_call(
        kernel,
        out_shape=out_shape,
        in_specs=[pl.BlockSpec(memory_space=pltpu.SMEM)] * smem + [vmem] * (len(ins) - smem),
        out_specs=[vmem] * len(out_shape),
        scratch_shapes=list(scratch),
        compiler_params=pltpu.CompilerParams(vmem_limit_bytes=VMEM_BYTES),
        cost_estimate=pl.CostEstimate(flops=flops, bytes_accessed=moved, transcendentals=0),
    )(*ins)


def across_rep(values, bit):
    count = lax.axis_size("rep")
    return lax.ppermute(values, "rep", [(i, i ^ bit) for i in range(count)])


def across_panel(values, bits):
    count = lax.axis_size("panel")
    return lax.ppermute(values, "panel", [(i, i ^ bits[i & 1]) for i in range(count)])


def swap(values):
    return across_panel(values, (1, 1))


def low_bit(m):
    return m & -m


def scatter_sum(slices):
    parts = list(slices)
    order = sorted(range(1, len(parts)), key=lambda m: (low_bit(m), low_bit(m ^ low_bit(m)) or len(parts)))
    for m in order:
        target = m ^ low_bit(m)
        parts[target] = parts[target] + across_rep(parts[m], low_bit(m))
    return parts[0]


def gather(own):
    count = lax.axis_size("rep")
    known = {0: own}
    order = sorted(range(1, count), key=lambda m: (bin(m).count("1"), -m))
    for m in order:
        known[m] = across_rep(known[m ^ low_bit(m)], low_bit(m))
    return [known[m] for m in range(count)]


def per_device(user_cot, item_cot, tile_vals, tile_rows, tile_cols, tile_count):
    n_panel, n_rep = lax.axis_size("panel"), lax.axis_size("rep")
    panel, rep = lax.axis_index("panel"), lax.axis_index("rep")
    chips = n_panel // 2
    n_user, feature = user_cot.shape
    n_item = item_cot.shape[0]
    width, size = n_user // n_panel, n_item // n_rep
    f32 = lambda *shape: jax.ShapeDtypeStruct(shape, jnp.float32)
    b16 = lambda *shape: jax.ShapeDtypeStruct(shape, jnp.bfloat16)
    space = lambda *shape: pltpu.VMEM(shape, jnp.float32)
    item_slices = [f32(size, feature)] * n_rep
    user_blocks = [f32(chips, width, feature)] * 2
    cost = dict(
        flops=6 * n_user * n_item * feature,
        moved=4 * (n_user * n_item + 2 * n_user * feature),
    )

    high, low, *item_parts = call(
        first_items_kernel,
        [b16(n_user, n_item), b16(n_user, n_item)] + item_slices,
        (tile_count, tile_rows[0], tile_cols[0], tile_vals[0, 0], user_cot),
        [space(n_user, n_item), space(n_item, feature)],
        smem=3,
        **cost,
    )
    mine, other = call(
        first_users_kernel, user_blocks, (high, low, item_cot), [space(n_user, feature)], **cost
    )

    item_sum = scatter_sum(item_parts)

    mine = mine + swap(other)
    steps = (chips - 1).bit_length()
    for k in range(steps):
        mine = mine + across_panel(mine, (2 << k, 2 << ((k + steps // 2) % steps)))

    again = call(
        second_items_kernel,
        item_slices,
        (high, low, mine, swap(mine)),
        [space(n_user, feature), space(n_item, feature)],
        **cost,
    )
    gathered = gather(item_sum)
    last_mine, last_other = call(
        second_users_kernel,
        user_blocks,
        (high, low, *gathered),
        [space(n_item, feature), space(n_user, feature)],
        **cost,
    )

    last = last_mine + swap(last_other)
    grad_user = lax.dynamic_slice_in_dim(user_cot, panel * width, width, 0) * THIRD + (
        lax.dynamic_index_in_dim(mine, panel >> 1, 0, keepdims=False) + last[0]
    )
    for m in sorted(range(1, chips), key=lambda m: -m):
        grad_user = grad_user + across_panel(last[m], (2 * m, 2 * m))

    grad_item = lax.dynamic_slice_in_dim(item_cot, rep * size, size, 0) * THIRD + (
        item_sum + scatter_sum(again)
    )
    return (grad_user, grad_item)


def solution(mesh):
    return jax.shard_map(
        per_device,
        mesh=mesh,
        in_specs=(
            P("rep", None),
            P("panel", None),
            P("panel", "rep", None, None, None),
            P("panel", "rep", None),
            P("panel", "rep", None),
            P("panel", "rep"),
        ),
        out_specs=(P(("rep", "panel"), None), P(("panel", "rep"), None)),
        check_vma=False,
    )
```

time: 260 us -> 110 us (0.42)
  matrix products: 68.7 us -> 0 us
  waiting for transfers between devices: 114 us -> 63.3 us
  local copies, waits for them, and re-layouts: 47.7 us -> 5.9 us
  starting transfers between devices: 0.83 us -> 24.6 us
  between operations: 14.6 us -> 1.4 us
  Pallas kernels: 0 us -> 9.59 us
  other arithmetic: 12.9 us -> 5.16 us
    psum x2 -> x0, waiting for transfers between devices: 80.5 us -> none  [the longest x1 59.2 us: per_device(): user_mid = user_third + lax.psum(user_terms, 'panel')]
    dot_general x8 -> x0, matrix products: 68.7 us -> none  [the longest x2 25.5 us: to_users(): product = jnp.einsum('tjk,tkw->tjw', blocks, picked, precision=exact_mode)]
    ppermute x0 -> x17, waiting for transfers between devices: none -> 63.3 us  [the longest x9 39.6 us: across_rep(): return lax.ppermute(values, 'rep', [(i, i ^ bit) for i in range(count)])]
    reduce_scatter x2 -> x0, waiting for transfers between devices: 33.7 us -> none  [the longest x1 33.7 us: per_device(): lax.psum_scatter(to_users(item_mid), 'panel', scatter_dimension=0, tiled=...]
    dot_general x8 -> x0, local copies, waits for them, and re-layouts: 30 us -> none  [the longest x2 12.3 us: to_items(): product = jnp.einsum('tkj,tkw->tjw', blocks, picked, precision=exact_mode)]
    ppermute x0 -> x17, starting transfers between devices: none -> 24.6 us  [the longest x9 15.5 us: across_rep(): return lax.ppermute(values, 'rep', [(i, i ^ bit) for i in range(count)])]
    gather x4 -> x0, local copies, waits for them, and re-layouts: 17.7 us -> none  [the longest x2 8.85 us: to_items(): jnp.take(users.reshape(user_blocks, TILE, feature), row_ids, axis=0)]
    pallas_call x0 -> x4, Pallas kernels: none -> 9.59 us  [call(): pl.pallas_call(kernel, out_shape=out_shape, in_specs=[pl.BlockSpec(memory...]
  transfers between devices with their start and end apart: 4 -> 17, of which waited for: 3 -> 12; matrix products, arithmetic and copies ran while one was open for 24% -> 1% of each run, Pallas kernels for 0% -> 2%
where the time goes in v2:
time: 110 us
  waiting for transfers between devices  63.3 us (58%)
  starting transfers between devices  24.6 us (22%)
  Pallas kernels  9.59 us (9%)
  local copies, waits for them, and re-layouts  5.9 us (5%)
  other arithmetic  5.16 us (5%)
  between operations  1.4 us (1%)
    ppermute x9, waiting for transfers between devices, across_rep(): return lax.ppermute(values, 'rep', [(i, i ^ bit) for i in range(count)])  39.6 us
    ppermute x8, waiting for transfers between devices, across_panel(): lax.ppermute(values, 'panel', [(i, i ^ bits[i & 1]) for i in range(count)])  23.6 us
    ppermute x9, starting transfers between devices, across_rep(): return lax.ppermute(values, 'rep', [(i, i ^ bit) for i in range(count)])  15.5 us
    pallas_call x4, Pallas kernels, call(): pl.pallas_call(kernel, out_shape=out_shape, in_specs=[pl.BlockSpec(memory...  9.59 us
    ppermute x8, starting transfers between devices, across_panel(): lax.ppermute(values, 'panel', [(i, i ^ bits[i & 1]) for i in range(count)])  9.09 us
    unnamed x18, local copies, waits for them, and re-layouts  5.88 us
  transfers between devices with their start and end apart: 17, of which 12 were waited for; matrix products, arithmetic and copies ran while one was open for 1% of the time, Pallas kernels for 2%

profile of v2, /device:TPU:0, one launch (start us, length us, event | category | flops | bytes accessed | tf_op | source)
XLA Modules:
  0.0 109.9 jit_solution(15987369171672764735)
XLA Ops:
  5.6 3.4 %shard_map.77 = (bf16[1024,1024]{1,0:T(8,128)(2,1)S(1)}, bf16[1024,1024]{1,0:T(8,128)(2,1)S(1)}, f32[256,256]{1,0:T(8,128)S(1)}, f32[256,256]{1,0:T(8,128)S(1)},...) custom-call(s32[1,1]{1,0:T(1,128)S(6)} %copy.8.count_ref, s32[1,40]{1,0:T(1,128)S(1)} %bitcast.20, s32[1,40]{1,0:T(1,128)S(1)} %bitcast.21, ...), custom_call_target="tpu_custom_call" | custom-call | flops 1610612736 | bytes 6291456 | tf_op jit(solution)/shard_map/pallas_call | solution.py:104
  9.0 1.9 %shard_map.78 = (f32[4,128,256]{2,1,0:T(8,128)S(1)}, f32[4,128,256]{2,1,0:T(8,128)S(1)}) custom-call(bf16[1024,1024]{1,0:T(8,128)(2,1)S(1)} %get-tuple-element.16.high_ref, bf16[1024,1024]{1,0:T(8,128)(2,1)S(1)} %get-tuple-element.17.low_ref, f32[1024,256]{1,0:T(8,128)S(1)} %copy-done), custom_call_target="tpu_custom_call" | custom-call | flops 1610612736 | bytes 6291456 | tf_op jit(solution)/shard_map/pallas_call | solution.py:104
  13.0 3.0 %collective-permute-start.1 = (f32[4,128,256]{2,1,0:T(8,128)S(1)}, f32[4,128,256]{2,1,0:T(8,128)S(1)}, u32[]{:S(2)}, u32[]{:S(2)}) collective-permute-start(f32[4,128,256]{2,1,0:T(8,128)S(1)} %add.65), channel_id=1, source_target_pairs={{0,8},{4,20},{8,0},{12,28},{16,24},{20,4},{24,16},{28,12},{1,9},{5... | collective-permute-start | bytes 1572872 | tf_op jit(solution)/shard_map/ppermute | solution.py:122
  16.0 7.2 %collective-permute-done.1 = f32[4,128,256]{2,1,0:T(8,128)S(1)} collective-permute-done((f32[4,128,256]{2,1,0:T(8,128)S(1)}, f32[4,128,256]{2,1,0:T(8,128)S(1)}, u32[]{:S(2)}, u32[]{:S(2)}) %collective-permute-start.1) | collective-permute-done | bytes 524320 | tf_op jit(solution)/shard_map/ppermute | solution.py:122
  23.3 2.0 %collective-permute-start.2 = (f32[4,128,256]{2,1,0:T(8,128)S(1)}, f32[4,128,256]{2,1,0:T(8,128)S(1)}, u32[]{:S(2)}, u32[]{:S(2)}) collective-permute-start(f32[4,128,256]{2,1,0:T(8,128)S(1)} %add.66), channel_id=1, source_target_pairs={{0,16},{4,12},{8,24},{12,4},{16,0},{20,28},{24,8},{28,20},{1,17},{... | collective-permute-start | bytes 1572872 | tf_op jit(solution)/shard_map/ppermute | solution.py:122
  25.2 7.3 %collective-permute-done.2 = f32[4,128,256]{2,1,0:T(8,128)S(1)} collective-permute-done((f32[4,128,256]{2,1,0:T(8,128)S(1)}, f32[4,128,256]{2,1,0:T(8,128)S(1)}, u32[]{:S(2)}, u32[]{:S(2)}) %collective-permute-start.2) | collective-permute-done | bytes 524320 | tf_op jit(solution)/shard_map/ppermute | solution.py:122
  32.7 2.2 %collective-permute-start.4 = (f32[256,256]{1,0:T(8,128)S(1)}, f32[256,256]{1,0:T(8,128)S(1)}, u32[]{:S(2)}, u32[]{:S(2)}) collective-permute-start(f32[256,256]{1,0:T(8,128)S(1)} %get-tuple-element.23), channel_id=1, source_target_pairs={{0,1},{1,0},{2,3},{3,2},{4,5},{5,4},{6,7},{7,6},{8,9},{9,8},{10,11... | collective-permute-start | bytes 786440 | tf_op jit(solution)/shard_map/ppermute | solution.py:117
  34.8 2.3 %shard_map.80 = (f32[256,256]{1,0:T(8,128)S(1)}, f32[256,256]{1,0:T(8,128)S(1)}, f32[256,256]{1,0:T(8,128)S(1)}, f32[256,256]{1,0:T(8,128)S(1)}) custom-call(bf16[1024,1024]{1,0:T(8,128)(2,1)S(1)} %get-tuple-element.16.high_ref, bf16[1024,1024]{1,0:T(8,128)(2,1)S(1)} %get-tuple-element.17.low_ref, f32[4,128,256]{2,1,0:T(8,128)S(1)} %add.67.mine_ref, ...), custom_call_target="tpu_custom_call" | custom-call | flops 1610612736 | bytes 6291456 | tf_op jit(solution)/shard_map/pallas_call | solution.py:104
  37.1 1.9 %collective-permute-start.15 = (f32[256,256]{1,0:T(8,128)S(1)}, f32[256,256]{1,0:T(8,128)S(1)}, u32[]{:S(2)}, u32[]{:S(2)}) collective-permute-start(f32[256,256]{1,0:T(8,128)S(1)} %get-tuple-element.29), channel_id=1, source_target_pairs={{0,1},{1,0},{2,3},{3,2},{4,5},{5,4},{6,7},{7,6},{8,9},{9,8},{10,11... | collective-permute-start | bytes 786440 | tf_op jit(solution)/shard_map/ppermute | solution.py:117
  39.2 2.8 %collective-permute-done.4 = f32[256,256]{1,0:T(8,128)S(1)} collective-permute-done((f32[256,256]{1,0:T(8,128)S(1)}, f32[256,256]{1,0:T(8,128)S(1)}, u32[]{:S(2)}, u32[]{:S(2)}) %collective-permute-start.4) | collective-permute-done | bytes 262176 | tf_op jit(solution)/shard_map/ppermute | solution.py:117
  42.7 2.8 %collective-permute-start.5 = (f32[256,256]{1,0:T(8,128)}, f32[256,256]{1,0:T(8,128)S(1)}, u32[]{:S(2)}, u32[]{:S(2)}) collective-permute-start(f32[256,256]{1,0:T(8,128)} %add.70), channel_id=1, source_target_pairs={{0,2},{1,3},{2,0},{3,1},{4,6},{5,7},{6,4},{7,5},{8,10},{9,11},{10,... | collective-permute-start | bytes 786440 | tf_op jit(solution)/shard_map/ppermute | solution.py:117
  47.1 6.1 %collective-permute-done.15 = f32[256,256]{1,0:T(8,128)S(1)} collective-permute-done((f32[256,256]{1,0:T(8,128)S(1)}, f32[256,256]{1,0:T(8,128)S(1)}, u32[]{:S(2)}, u32[]{:S(2)}) %collective-permute-start.15) | collective-permute-done | bytes 262176 | tf_op jit(solution)/shard_map/ppermute | solution.py:117
  53.9 1.9 %collective-permute-start.16 = (f32[256,256]{1,0:T(8,128)}, f32[256,256]{1,0:T(8,128)}, u32[]{:S(2)}, u32[]{:S(2)}) collective-permute-start(f32[256,256]{1,0:T(8,128)} %add.81), channel_id=1, source_target_pairs={{0,2},{1,3},{2,0},{3,1},{4,6},{5,7},{6,4},{7,5},{8,10},{9,11},{10,... | collective-permute-start | bytes 786440 | tf_op jit(solution)/shard_map/ppermute | solution.py:117
  55.9 3.0 %collective-permute-done.3 = f32[256,256]{1,0:T(8,128)S(1)} collective-permute-done((f32[256,256]{1,0:T(8,128)S(1)}, f32[256,256]{1,0:T(8,128)S(1)}, u32[]{:S(2)}, u32[]{:S(2)}) %collective-permute-start.3) | collective-permute-done | bytes 262176 | tf_op jit(solution)/shard_map/ppermute | solution.py:117
  58.9 10.9 %collective-permute-done.14 = f32[256,256]{1,0:T(8,128)S(1)} collective-permute-done((f32[256,256]{1,0:T(8,128)S(1)}, f32[256,256]{1,0:T(8,128)S(1)}, u32[]{:S(2)}, u32[]{:S(2)}) %collective-permute-start.14) | collective-permute-done | bytes 262176 | tf_op jit(solution)/shard_map/ppermute | solution.py:117
  69.8 1.8 %add_add_fusion = (f32[256,256]{1,0:T(8,128)}, f32[256,256]{1,0:T(8,128)S(1)}) fusion(f32[256,256]{1,0:T(8,128)} %collective-permute-done.16, f32[256,256]{1,0:T(8,128)S(1)} %get-tuple-element.26, f32[256,256]{1,0:T(8,128)S(1)} %collective-permute-done.14, f32[1024,256]{1,0:T(8,128)S(1)} %copy-done, s32[]{:T(128)S(6)} %select_n.12, ...), kind=kLoop, calls=%fused_computation | loop fusion | flops 458752 | bytes 2359300 | tf_op jit(solution)/shard_map/add | solution.py:210
  71.6 2.8 %collective-permute-start.7 = (f32[256,256]{1,0:T(8,128)S(1)}, f32[256,256]{1,0:T(8,128)S(1)}, u32[]{:S(2)}, u32[]{:S(2)}) collective-permute-start(f32[256,256]{1,0:T(8,128)S(1)} %get-tuple-element.31.rest_0_), channel_id=1, source_target_pairs={{0,2},{1,3},{2,0},{3,1},{4,6},{5,7},{6,4},{7,5},{8,10},{9,11},{10,... | collective-permute-start | bytes 786440 | tf_op jit(solution)/shard_map/ppermute | solution.py:117
  75.8 10.4 %collective-permute-done.7.rest_2_ = f32[256,256]{1,0:T(8,128)S(1)} collective-permute-done((f32[256,256]{1,0:T(8,128)S(1)}, f32[256,256]{1,0:T(8,128)S(1)}, u32[]{:S(2)}, u32[]{:S(2)}) %collective-permute-start.7) | collective-permute-done | bytes 262176 | tf_op jit(solution)/shard_map/ppermute | solution.py:117
  86.9 6.5 %collective-permute-done.8.rest_3_ = f32[256,256]{1,0:T(8,128)S(1)} collective-permute-done((f32[256,256]{1,0:T(8,128)S(1)}, f32[256,256]{1,0:T(8,128)S(1)}, u32[]{:S(2)}, u32[]{:S(2)}) %collective-permute-start.8) | collective-permute-done | bytes 262176 | tf_op jit(solution)/shard_map/ppermute | solution.py:117
  95.0 1.9 %shard_map.79 = (f32[4,128,256]{2,1,0:T(8,128)S(1)}, f32[4,128,256]{2,1,0:T(8,128)S(1)}) custom-call(bf16[1024,1024]{1,0:T(8,128)(2,1)S(1)} %copy-done.6, bf16[1024,1024]{1,0:T(8,128)(2,1)S(1)} %copy-done.8, f32[256,256]{1,0:T(8,128)S(1)} %get-tuple-element.31.rest_0_, f32[256,256]{1,0:T(8,128)S(1)} %collective-permute-done.6.rest_1_, ...), custom_call_target="tpu_custom_call" | custom-call | flops 1610612736 | bytes 6291456 | tf_op jit(solution)/shard_map/pallas_call | solution.py:104
  97.0 1.9 %collective-permute-done.9 = f32[4,128,256]{2,1,0:T(8,128)S(1)} collective-permute-done((f32[4,128,256]{2,1,0:T(8,128)S(1)}, f32[4,128,256]{2,1,0:T(8,128)S(1)}, u32[]{:S(2)}, u32[]{:S(2)}) %collective-permute-start.9) | collective-permute-done | bytes 524320 | tf_op jit(solution)/shard_map/ppermute | solution.py:122
  99.0 2.5 %collective-permute-start.10 = (f32[128,256]{1,0:T(8,128)S(1)}, f32[128,256]{1,0:T(8,128)S(1)}, u32[]{:S(2)}, u32[]{:S(2)}) collective-permute-start(f32[128,256]{1,0:T(8,128)S(1)} %get-tuple-element.32), channel_id=1, source_target_pairs={{0,24},{4,28},{8,16},{12,20},{16,8},{20,12},{24,0},{28,4},{1,25},{... | collective-permute-start | bytes 393224 | tf_op jit(solution)/shard_map/ppermute | solution.py:122
  102.5 3.7 %collective-permute-done.10 = f32[128,256]{1,0:T(8,128)S(1)} collective-permute-done((f32[128,256]{1,0:T(8,128)S(1)}, f32[128,256]{1,0:T(8,128)S(1)}, u32[]{:S(2)}, u32[]{:S(2)}) %collective-permute-start.10) | collective-permute-done | bytes 131104 | tf_op jit(solution)/shard_map/ppermute | solution.py:122
  106.3 2.0 %collective-permute-done.12 = f32[128,256]{1,0:T(8,128)S(1)} collective-permute-done((f32[128,256]{1,0:T(8,128)S(1)}, f32[128,256]{1,0:T(8,128)S(1)}, u32[]{:S(2)}, u32[]{:S(2)}) %collective-permute-start.12) | collective-permute-done | bytes 131104 | tf_op jit(solution)/shard_map/ppermute | solution.py:122
  (41 shorter events, 16.4 us)
Async XLA Ops:
  1.3 1.2 %copy-start.1 = (f32[1024,256]{1,0:T(8,128)S(1)}, f32[1024,256]{1,0:T(8,128)}, u32[]{:S(2)}) copy-start(f32[1024,256]{1,0:T(8,128)} %users_ref.1) | copy-start | bytes 3145732
  2.5 1.7 %copy-start.2 = (f32[1,1,40,128,128]{4,3,2,1,0:T(8,128)S(1)}, f32[1,1,40,128,128]{4,3,2,1,0:T(8,128)}, u32[]{:S(2)}) copy-start(f32[1,1,40,128,128]{4,3,2,1,0:T(8,128)} %param.8) | copy-start | bytes 7864324
  5.6 3.5 %copy-start = (f32[1024,256]{1,0:T(8,128)S(1)}, f32[1024,256]{1,0:T(8,128)}, u32[]{:S(2)}) copy-start(f32[1024,256]{1,0:T(8,128)} %items_ref.1) | copy-start | bytes 3145732
  9.0 25.8 %copy-start.5 = (bf16[1024,1024]{1,0:T(8,128)(2,1)}, bf16[1024,1024]{1,0:T(8,128)(2,1)S(1)}, u32[]{:S(2)}) copy-start(bf16[1024,1024]{1,0:T(8,128)(2,1)S(1)} %get-tuple-element.16.high_ref) | copy-start | bytes 6291460
  9.0 25.8 %copy-start.7 = (bf16[1024,1024]{1,0:T(8,128)(2,1)}, bf16[1024,1024]{1,0:T(8,128)(2,1)S(1)}, u32[]{:S(2)}) copy-start(bf16[1024,1024]{1,0:T(8,128)(2,1)S(1)} %get-tuple-element.17.low_ref) | copy-start | bytes 6291460
  11.0 2.0 %collective-permute-start = (f32[4,128,256]{2,1,0:T(8,128)S(1)}, f32[4,128,256]{2,1,0:T(8,128)S(1)}, u32[]{:S(2)}, u32[]{:S(2)}) collective-permute-start(f32[4,128,256]{2,1,0:T(8,128)S(1)} %get-tuple-element.19), channel_id=1, source_target_pairs={{0,4},{4,0},{8,12},{12,8},{16,20},{20,16},{24,28},{28,24},{1,5},{5... | collective-permute-start | bytes 1572872 | tf_op jit(solution)/shard_map/ppermute | solution.py:122
  13.0 10.2 %collective-permute-start.1 = (f32[4,128,256]{2,1,0:T(8,128)S(1)}, f32[4,128,256]{2,1,0:T(8,128)S(1)}, u32[]{:S(2)}, u32[]{:S(2)}) collective-permute-start(f32[4,128,256]{2,1,0:T(8,128)S(1)} %add.65), channel_id=1, source_target_pairs={{0,8},{4,20},{8,0},{12,28},{16,24},{20,4},{24,16},{28,12},{1,9},{5... | collective-permute-start | bytes 1572872 | tf_op jit(solution)/shard_map/ppermute | solution.py:122
  23.3 9.2 %collective-permute-start.2 = (f32[4,128,256]{2,1,0:T(8,128)S(1)}, f32[4,128,256]{2,1,0:T(8,128)S(1)}, u32[]{:S(2)}, u32[]{:S(2)}) collective-permute-start(f32[4,128,256]{2,1,0:T(8,128)S(1)} %add.66), channel_id=1, source_target_pairs={{0,16},{4,12},{8,24},{12,4},{16,0},{20,28},{24,8},{28,20},{1,17},{... | collective-permute-start | bytes 1572872 | tf_op jit(solution)/shard_map/ppermute | solution.py:122
  32.6 2.2 %collective-permute-start.13 = (f32[4,128,256]{2,1,0:T(8,128)S(1)}, f32[4,128,256]{2,1,0:T(8,128)S(1)}, u32[]{:S(2)}, u32[]{:S(2)}) collective-permute-start(f32[4,128,256]{2,1,0:T(8,128)S(1)} %add.67.mine_ref), channel_id=1, source_target_pairs={{0,4},{4,0},{8,12},{12,8},{16,20},{20,16},{24,28},{28,24},{1,5},{5... | collective-permute-start | bytes 1572872 | tf_op jit(solution)/shard_map/ppermute | solution.py:122
  32.7 9.3 %collective-permute-start.4 = (f32[256,256]{1,0:T(8,128)S(1)}, f32[256,256]{1,0:T(8,128)S(1)}, u32[]{:S(2)}, u32[]{:S(2)}) collective-permute-start(f32[256,256]{1,0:T(8,128)S(1)} %get-tuple-element.23), channel_id=1, source_target_pairs={{0,1},{1,0},{2,3},{3,2},{4,5},{5,4},{6,7},{7,6},{8,9},{9,8},{10,11... | collective-permute-start | bytes 786440 | tf_op jit(solution)/shard_map/ppermute | solution.py:117
  37.1 16.1 %collective-permute-start.15 = (f32[256,256]{1,0:T(8,128)S(1)}, f32[256,256]{1,0:T(8,128)S(1)}, u32[]{:S(2)}, u32[]{:S(2)}) collective-permute-start(f32[256,256]{1,0:T(8,128)S(1)} %get-tuple-element.29), channel_id=1, source_target_pairs={{0,1},{1,0},{2,3},{3,2},{4,5},{5,4},{6,7},{7,6},{8,9},{9,8},{10,11... | collective-permute-start | bytes 786440 | tf_op jit(solution)/shard_map/ppermute | solution.py:117
  39.0 19.9 %collective-permute-start.3 = (f32[256,256]{1,0:T(8,128)S(1)}, f32[256,256]{1,0:T(8,128)S(1)}, u32[]{:S(2)}, u32[]{:S(2)}) collective-permute-start(f32[256,256]{1,0:T(8,128)S(1)} %get-tuple-element.21), channel_id=1, source_target_pairs={{0,1},{1,0},{2,3},{3,2},{4,5},{5,4},{6,7},{7,6},{8,9},{9,8},{10,11... | collective-permute-start | bytes 786440 | tf_op jit(solution)/shard_map/ppermute | solution.py:117
  42.7 16.2 %collective-permute-start.5 = (f32[256,256]{1,0:T(8,128)}, f32[256,256]{1,0:T(8,128)S(1)}, u32[]{:S(2)}, u32[]{:S(2)}) collective-permute-start(f32[256,256]{1,0:T(8,128)} %add.70), channel_id=1, source_target_pairs={{0,2},{1,3},{2,0},{3,1},{4,6},{5,7},{6,4},{7,5},{8,10},{9,11},{10,... | collective-permute-start | bytes 786440 | tf_op jit(solution)/shard_map/ppermute | solution.py:117
  45.5 24.3 %collective-permute-start.14 = (f32[256,256]{1,0:T(8,128)S(1)}, f32[256,256]{1,0:T(8,128)S(1)}, u32[]{:S(2)}, u32[]{:S(2)}) collective-permute-start(f32[256,256]{1,0:T(8,128)S(1)} %get-tuple-element.27), channel_id=1, source_target_pairs={{0,1},{1,0},{2,3},{3,2},{4,5},{5,4},{6,7},{7,6},{8,9},{9,8},{10,11... | collective-permute-start | bytes 786440 | tf_op jit(solution)/shard_map/ppermute | solution.py:117
  53.9 15.9 %collective-permute-start.16 = (f32[256,256]{1,0:T(8,128)}, f32[256,256]{1,0:T(8,128)}, u32[]{:S(2)}, u32[]{:S(2)}) collective-permute-start(f32[256,256]{1,0:T(8,128)} %add.81), channel_id=1, source_target_pairs={{0,2},{1,3},{2,0},{3,1},{4,6},{5,7},{6,4},{7,5},{8,10},{9,11},{10,... | collective-permute-start | bytes 786440 | tf_op jit(solution)/shard_map/ppermute | solution.py:117
  55.9 37.5 %copy-start.6 = (bf16[1024,1024]{1,0:T(8,128)(2,1)S(1)}, bf16[1024,1024]{1,0:T(8,128)(2,1)}, u32[]{:S(2)}) copy-start(bf16[1024,1024]{1,0:T(8,128)(2,1)} %copy-done.5) | copy-start | bytes 6291460
  71.6 14.6 %collective-permute-start.7 = (f32[256,256]{1,0:T(8,128)S(1)}, f32[256,256]{1,0:T(8,128)S(1)}, u32[]{:S(2)}, u32[]{:S(2)}) collective-permute-start(f32[256,256]{1,0:T(8,128)S(1)} %get-tuple-element.31.rest_0_), channel_id=1, source_target_pairs={{0,2},{1,3},{2,0},{3,1},{4,6},{5,7},{6,4},{7,5},{8,10},{9,11},{10,... | collective-permute-start | bytes 786440 | tf_op jit(solution)/shard_map/ppermute | solution.py:117
  74.4 12.5 %collective-permute-start.6 = (f32[256,256]{1,0:T(8,128)S(1)}, f32[256,256]{1,0:T(8,128)S(1)}, u32[]{:S(2)}, u32[]{:S(2)}) collective-permute-start(f32[256,256]{1,0:T(8,128)S(1)} %get-tuple-element.31.rest_0_), channel_id=1, source_target_pairs={{0,1},{1,0},{2,3},{3,2},{4,5},{5,4},{6,7},{7,6},{8,9},{9,8},{10,11... | collective-permute-start | bytes 786440 | tf_op jit(solution)/shard_map/ppermute | solution.py:117
  86.2 7.2 %collective-permute-start.8 = (f32[256,256]{1,0:T(8,128)S(1)}, f32[256,256]{1,0:T(8,128)S(1)}, u32[]{:S(2)}, u32[]{:S(2)}) collective-permute-start(f32[256,256]{1,0:T(8,128)S(1)} %collective-permute-done.7.rest_2_), channel_id=1, source_target_pairs={{0,1},{1,0},{2,3},{3,2},{4,5},{5,4},{6,7},{7,6},{8,9},{9,8},{10,11... | collective-permute-start | bytes 786440 | tf_op jit(solution)/shard_map/ppermute | solution.py:117
  93.4 1.6 %copy-start.8 = (bf16[1024,1024]{1,0:T(8,128)(2,1)S(1)}, bf16[1024,1024]{1,0:T(8,128)(2,1)}, u32[]{:S(2)}) copy-start(bf16[1024,1024]{1,0:T(8,128)(2,1)} %copy-done.7) | copy-start | bytes 6291460
  96.9 2.0 %collective-permute-start.9 = (f32[4,128,256]{2,1,0:T(8,128)S(1)}, f32[4,128,256]{2,1,0:T(8,128)S(1)}, u32[]{:S(2)}, u32[]{:S(2)}) collective-permute-start(f32[4,128,256]{2,1,0:T(8,128)S(1)} %get-tuple-element.25), channel_id=1, source_target_pairs={{0,4},{4,0},{8,12},{12,8},{16,20},{20,16},{24,28},{28,24},{1,5},{5... | collective-permute-start | bytes 1572872 | tf_op jit(solution)/shard_map/ppermute | solution.py:122
  99.0 7.3 %collective-permute-start.10 = (f32[128,256]{1,0:T(8,128)S(1)}, f32[128,256]{1,0:T(8,128)S(1)}, u32[]{:S(2)}, u32[]{:S(2)}) collective-permute-start(f32[128,256]{1,0:T(8,128)S(1)} %get-tuple-element.32), channel_id=1, source_target_pairs={{0,24},{4,28},{8,16},{12,20},{16,8},{20,12},{24,0},{28,4},{1,25},{... | collective-permute-start | bytes 393224 | tf_op jit(solution)/shard_map/ppermute | solution.py:122
  101.5 6.8 %collective-permute-start.12 = (f32[128,256]{1,0:T(8,128)S(1)}, f32[128,256]{1,0:T(8,128)S(1)}, u32[]{:S(2)}, u32[]{:S(2)}) collective-permute-start(f32[128,256]{1,0:T(8,128)S(1)} %get-tuple-element.33), channel_id=1, source_target_pairs={{0,8},{4,12},{8,0},{12,4},{16,24},{20,28},{24,16},{28,20},{1,9},{5... | collective-permute-start | bytes 393224 | tf_op jit(solution)/shard_map/ppermute | solution.py:122
  102.0 6.3 %collective-permute-start.11 = (f32[128,256]{1,0:T(8,128)S(1)}, f32[128,256]{1,0:T(8,128)S(1)}, u32[]{:S(2)}, u32[]{:S(2)}) collective-permute-start(f32[128,256]{1,0:T(8,128)S(1)} %get-tuple-element.34), channel_id=1, source_target_pairs={{0,16},{4,20},{8,24},{12,28},{16,0},{20,4},{24,8},{28,12},{1,17},{... | collective-permute-start | bytes 393224 | tf_op jit(solution)/shard_map/ppermute | solution.py:122
  (2 other events, 1.3 us)

commit v3 on v0

v3 whole, which is shorter than its diff:
```python
import functools

import jax
import jax.numpy as jnp
from jax import lax
from jax.experimental import pallas as pl
from jax.experimental.pallas import tpu as pltpu
from jax.sharding import PartitionSpec as P

TILE = 128
BLOCK = 256
COPIES = 4
VMEM_BYTES = 24 * 1024 * 1024
OFFSET = 2
COLLECT = 2
THIRD = 1.0 / 3.0
NEAR = (((1,), (0,)), ((), ()))


def halves(values):
    high = values.astype(jnp.bfloat16)
    low = (values - high.astype(jnp.float32)).astype(jnp.bfloat16)
    return high, low


def product(left, right):
    dot = lambda a, b: lax.dot_general(a, b, NEAR, preferred_element_type=jnp.float32)
    return dot(left[0], right[0]) + (dot(left[0], right[1]) + dot(left[1], right[0]))


def blocks_of(size):
    step = min(BLOCK, size)
    return [pl.ds(start, step) for start in range(0, size, step)]


def rows_at(index, size):
    return pl.ds(pl.multiple_of(index * size, size), size)


def item_product(high_ref, low_ref, users, items_ref):
    users_t = halves(users.T)
    for here in blocks_of(high_ref.shape[1]):
        items_ref[here, :] = product(users_t, (high_ref[:, here], low_ref[:, here])).T


def user_product(high_ref, low_ref, items, full_ref):
    for here in blocks_of(high_ref.shape[0]):
        full_ref[here, :] = product((high_ref[here, :], low_ref[here, :]), items)


def user_blocks(full_ref, mine_ref, other_ref, place):
    core = lax.axis_index("panel") & 1
    chips, width = mine_ref.shape[:2]
    for m in range(chips):
        mine_ref[m] = full_ref[rows_at(2 * (place ^ m) + core, width), :]
        other_ref[m] = full_ref[rows_at(2 * (place ^ m) + 1 - core, width), :]


def first_kernel(count_ref, rows_hbm, cols_hbm, tiles_hbm, users_hbm, items_hbm, *rest):
    high_ref, low_ref, sums_ref, mine_ref, other_ref = rest[:5]
    whole_ref, full_ref, tiles_ref, users_ref, items_ref, rows_ref, cols_ref, sems = rest[5:]
    index_copies = [
        pltpu.make_async_copy(source, target, sems.at[COPIES + 2 + k])
        for k, (source, target) in enumerate(((rows_hbm, rows_ref), (cols_hbm, cols_ref)))
    ]
    slots = tiles_ref.shape[0]
    steps = slots // COPIES if slots % COPIES == 0 else slots
    tile_copies = []
    for k, start in enumerate(range(0, slots, steps)):
        part = pl.ds(start, steps)
        tile_copies.append(pltpu.make_async_copy(tiles_hbm.at[0, 0, part], tiles_ref.at[part], sems.at[k]))
    users_copy = pltpu.make_async_copy(users_hbm, users_ref, sems.at[COPIES])
    items_copy = pltpu.make_async_copy(items_hbm, items_ref, sems.at[COPIES + 1])
    for copy in (*index_copies, *tile_copies, users_copy, items_copy):
        copy.start()

    whole_ref[...] = jnp.zeros_like(whole_ref)
    for copy in index_copies:
        copy.wait()
    for k, copy in enumerate(tile_copies):
        copy.wait()

        @pl.loop(k * steps, jnp.minimum((k + 1) * steps, count_ref[0, 0]))
        def _(t):
            whole_ref[rows_at(rows_ref[0, 0, t], TILE), rows_at(cols_ref[0, 0, t], TILE)] += tiles_ref[t]

    for here in blocks_of(whole_ref.shape[0]):
        high_ref[here, :], low_ref[here, :] = halves(whole_ref[here, :])
    users_copy.wait()
    item_product(high_ref, low_ref, users_ref[...] * THIRD, sums_ref)
    items_copy.wait()
    user_product(high_ref, low_ref, halves(items_ref[...] * THIRD), full_ref)
    user_blocks(full_ref, mine_ref, other_ref, 0)


def items_kernel(high_ref, low_ref, mine_ref, other_ref, sums_ref, users_ref):
    core = lax.axis_index("panel") & 1
    chips, width = mine_ref.shape[:2]
    for chip in range(chips):
        users_ref[rows_at(2 * chip + core, width), :] = mine_ref[chip]
        users_ref[rows_at(2 * chip + 1 - core, width), :] = other_ref[chip]
    item_product(high_ref, low_ref, users_ref[...], sums_ref)


def after(value, *others):
    return lax.optimization_barrier((value, others))[0] if others else value


def line_place(count):
    rep = lax.axis_index("rep")
    return jnp.where(lax.axis_index("panel") & 1 == 0, rep, count - 1 - rep)


def step_kernel(step, count, has_arrival, *refs):
    arrival_ref = refs[0] if has_arrival else None
    *sources, out_ref = refs[has_arrival:]
    size = out_ref.shape[0]
    place = line_place(count)
    index = step - 2 * place

    def put(ref, block):
        out_ref[...] = ref[rows_at(block, size), :]

    pl.when(index < count)(lambda: put(sources[0], jnp.maximum(index, 0)))
    if step >= count:
        pl.when((index >= count) & (index < 2 * count))(lambda: put(sources[1], index - count))
    if step >= 2 * count + OFFSET:
        unit = index - 2 * count - OFFSET
        target = jnp.clip(count - 1 - unit // 2, 0, count - 1)
        rep = jnp.where(lax.axis_index("panel") & 1 == 0, target, count - 1 - target)
        pl.when((unit >= 0) & (unit % 2 == 0))(lambda: put(sources[2], rep))
        pl.when((unit >= 0) & (unit % 2 == 1))(lambda: put(sources[3], rep))
    if has_arrival:

        @pl.when(place > 0)
        def _():
            out_ref[...] += arrival_ref[...]


def collect_kernel(*refs):
    *arrival_refs, out_ref = refs
    size = arrival_refs[0].shape[0]
    count = out_ref.shape[0] // size
    place = line_place(count)

    @pl.when(place == 0)
    def _():
        out_ref[...] = jnp.zeros_like(out_ref)

    for step, ref in enumerate(arrival_refs):
        block = step - 2 * (place - 1)

        @pl.when((place > 0) & (block >= 0) & (block < count))
        def _():
            out_ref[rows_at(block, size), :] = ref[...]


def users_kernel(user_cot_hbm, item_cot_hbm, high_ref, low_ref, sums_ref, far_ref, again_ref, users_ref, *rest):
    *arrival_refs, mine_ref, other_ref, own_ref, items_ref, full_ref, user_cot_ref, item_cot_ref, sems = rest
    panel, rep = lax.axis_index("panel"), lax.axis_index("rep")
    size, width = item_cot_ref.shape[0], user_cot_ref.shape[0]
    copies = (
        pltpu.make_async_copy(user_cot_hbm.at[rows_at(panel, width)], user_cot_ref, sems.at[0]),
        pltpu.make_async_copy(item_cot_hbm.at[rows_at(rep, size)], item_cot_ref, sems.at[1]),
    )
    for copy in copies:
        copy.start()
    count = items_ref.shape[0] // size
    place = line_place(count)
    items_ref[...] = sums_ref[...] + far_ref[...]
    for step, ref in enumerate(arrival_refs):
        block = step - 2 * (place - 1)

        @pl.when((place > 0) & (block >= 0) & (block < count))
        def _():
            items_ref[rows_at(block, size), :] += ref[...]

    user_product(high_ref, low_ref, halves(items_ref[...]), full_ref)
    user_blocks(full_ref, mine_ref, other_ref, panel >> 1)
    for copy in copies:
        copy.wait()
    mine_ref[0] += user_cot_ref[...] * THIRD + users_ref[panel >> 1]
    own_rows = rows_at(rep, size)
    own_ref[...] = item_cot_ref[...] * THIRD + (items_ref[own_rows, :] + again_ref[own_rows, :])


def call(kernel, out_shape, ins, scratch=(), spaces=(), flops=0, moved=0):
    spaces = list(spaces) + [pltpu.VMEM] * (len(ins) - len(spaces))
    return pl.pallas_call(
        kernel,
        out_shape=out_shape,
        in_specs=[pl.BlockSpec(memory_space=space) for space in spaces],
        out_specs=[pl.BlockSpec(memory_space=pltpu.VMEM)] * len(out_shape),
        scratch_shapes=list(scratch),
        compiler_params=pltpu.CompilerParams(vmem_limit_bytes=VMEM_BYTES),
        cost_estimate=pl.CostEstimate(flops=flops, bytes_accessed=moved, transcendentals=0),
    )(*ins)


def along_line(values):
    count, panels = lax.axis_size("rep"), lax.axis_size("panel")
    at = lambda p, r: p * count + r
    pairs = []
    for p in range(0, panels, 2):
        for r in range(count):
            pairs.append((at(p, r), at(p, r + 1) if r < count - 1 else at(p + 1, r)))
            pairs.append((at(p + 1, r), at(p + 1, r - 1) if r > 0 else at(p, r)))
    return lax.ppermute(values, ("panel", "rep"), pairs)


def across_panel(values, bits):
    count = lax.axis_size("panel")
    return lax.ppermute(values, "panel", [(i, i ^ bits[i & 1]) for i in range(count)])


def swap(values):
    return across_panel(values, (1, 1))


def per_device(user_cot, item_cot, tile_vals, tile_rows, tile_cols, tile_count):
    n_panel, n_rep = lax.axis_size("panel"), lax.axis_size("rep")
    panel, rep = lax.axis_index("panel"), lax.axis_index("rep")
    chips = n_panel // 2
    n_user, feature = user_cot.shape
    n_item = item_cot.shape[0]
    width, size = n_user // n_panel, n_item // n_rep
    f32 = lambda *shape: jax.ShapeDtypeStruct(shape, jnp.float32)
    b16 = lambda *shape: jax.ShapeDtypeStruct(shape, jnp.bfloat16)
    space = lambda *shape: pltpu.VMEM(shape, jnp.float32)
    cost = dict(
        flops=6 * n_user * n_item * feature,
        moved=4 * (n_user * n_item + 2 * n_user * feature),
    )
    items = f32(n_item, feature)
    blocks = [f32(chips, width, feature)] * 2
    piece = f32(size, feature)

    arguments = (tile_rows, tile_cols, tile_vals, user_cot, item_cot)
    pinned = [pltpu.with_memory_space_constraint(array, pltpu.HBM) for array in arguments]
    high, low, sums, mine, other = call(
        first_kernel,
        [b16(n_user, n_item), b16(n_user, n_item), items] + blocks,
        (tile_count, *pinned),
        [space(n_user, n_item), space(n_user, feature), space(*tile_vals.shape[2:])]
        + [space(n_user, feature), space(n_item, feature)]
        + [pltpu.SMEM(array.shape, jnp.int32) for array in arguments[:2]]
        + [pltpu.SemaphoreType.DMA((COPIES + 4,))],
        [pltpu.SMEM] + [pltpu.HBM] * 5,
        **cost,
    )

    sources = [swap(sums), sums]
    users = mine + swap(other)
    rounds = (chips - 1).bit_length()
    arrivals = []
    for step in range(4 * n_rep - 2 + OFFSET):
        if step == 2 * n_rep + OFFSET:
            for k in range(rounds):
                users = after(users, *arrivals[max(k - 1, 0) : k])
                with jax.named_scope(f"users_{k}"):
                    users = users + across_panel(users, (2 << k, 2 << ((k + rounds // 2) % rounds)))
            users = after(users, *arrivals[rounds - 1 : rounds])
            (again,) = call(items_kernel, [items], (high, low, users, swap(users)), [space(n_user, feature)], **cost)
            sources += [swap(again), again]
        before = arrivals[step - 2 : step - 1] if step >= 2 else []
        kernel = functools.partial(step_kernel, step, n_rep, len(before))
        used = sources[: 1 + (step >= n_rep)] if step < 2 * n_rep + OFFSET else sources
        (sent,) = call(kernel, [piece], (*before, *used))
        with jax.named_scope(f"line_{step}"):
            arrivals.append(along_line(sent))
        if step == 3 * n_rep - 5 + COLLECT:
            ready = after(arrivals[: 3 * n_rep - 4], *arrivals[3 * n_rep - 4 :])
            (passed,) = call(collect_kernel, [items], ready)
            far = swap(passed)

    last_mine, last_other, own_items = call(
        users_kernel,
        blocks + [piece],
        (*pinned[3:], high, low, sums, far, again, users, *arrivals[n_rep : 4 * n_rep - 4]),
        [space(n_item, feature), space(n_user, feature), space(width, feature), space(size, feature)]
        + [pltpu.SemaphoreType.DMA((2,))],
        [pltpu.HBM] * 2,
        **cost,
    )
    last = last_mine + swap(last_other)
    grad_user = last[0]
    for m in range(chips - 1, 0, -1):
        grad_user = grad_user + across_panel(last[m], (2 * m, 2 * m))

    place = line_place(n_rep)
    grad_item = own_items + jnp.where(place > 0, arrivals[-1], 0.0)
    grad_item = grad_item + jnp.where(place < n_rep - 1, swap(arrivals[-2]), 0.0)
    return (grad_user, grad_item)


def solution(mesh):
    return jax.shard_map(
        per_device,
        mesh=mesh,
        in_specs=(
            P("rep", None),
            P("panel", None),
            P("panel", "rep", None, None, None),
            P("panel", "rep", None),
            P("panel", "rep", None),
            P("panel", "rep"),
        ),
        out_specs=(P(("rep", "panel"), None), P(("panel", "rep"), None)),
        check_vma=False,
    )
```

time: 260 us -> 82.1 us (0.32)
  waiting for transfers between devices: 114 us -> 24.5 us
  matrix products: 68.7 us -> 0 us
  local copies, waits for them, and re-layouts: 47.7 us -> 0.03 us
  starting transfers between devices: 0.83 us -> 43.4 us
  between operations: 14.6 us -> 1.5 us
  other arithmetic: 12.9 us -> 1.72 us
  Pallas kernels: 0 us -> 10.9 us
    psum x2 -> x0, waiting for transfers between devices: 80.5 us -> none  [the longest x1 59.2 us: per_device(): user_mid = user_third + lax.psum(user_terms, 'panel')]
    dot_general x8 -> x0, matrix products: 68.7 us -> none  [the longest x2 25.5 us: to_users(): product = jnp.einsum('tjk,tkw->tjw', blocks, picked, precision=exact_mode)]
    ppermute x0 -> x28, starting transfers between devices: none -> 43.4 us  [the longest x16 33.7 us: along_line(): return lax.ppermute(values, ('panel', 'rep'), pairs)]
    reduce_scatter x2 -> x0, waiting for transfers between devices: 33.7 us -> none  [the longest x1 33.7 us: per_device(): lax.psum_scatter(to_users(item_mid), 'panel', scatter_dimension=0, tiled=...]
    dot_general x8 -> x0, local copies, waits for them, and re-layouts: 30 us -> none  [the longest x2 12.3 us: to_items(): product = jnp.einsum('tkj,tkw->tjw', blocks, picked, precision=exact_mode)]
    ppermute x0 -> x28, waiting for transfers between devices: none -> 24.5 us  [the longest x16 14.1 us: along_line(): return lax.ppermute(values, ('panel', 'rep'), pairs)]
    gather x4 -> x0, local copies, waits for them, and re-layouts: 17.7 us -> none  [the longest x2 8.85 us: to_items(): jnp.take(users.reshape(user_blocks, TILE, feature), row_ids, axis=0)]
    pallas_call x0 -> x20, Pallas kernels: none -> 10.9 us  [call(): pl.pallas_call(kernel, out_shape=out_shape, in_specs=[pl.BlockSpec(memory...]
  transfers between devices with their start and end apart: 4 -> 28, of which waited for: 3 -> 17; matrix products, arithmetic and copies ran while one was open for 24% -> 1% of each run, Pallas kernels for 0% -> 3%
where the time goes in v3:
time: 82.1 us; the launch traced here: 82 us
  starting transfers between devices  43.4 us (53%)
  waiting for transfers between devices  24.5 us (30%)
  Pallas kernels  10.9 us (13%)
  other arithmetic  1.72 us (2%)
  between operations  1.5 us (2%)
    ppermute x16, starting transfers between devices, along_line(): return lax.ppermute(values, ('panel', 'rep'), pairs)  33.7 us
    ppermute x16, waiting for transfers between devices, along_line(): return lax.ppermute(values, ('panel', 'rep'), pairs)  14.1 us
    pallas_call x20, Pallas kernels, call(): pl.pallas_call(kernel, out_shape=out_shape, in_specs=[pl.BlockSpec(memory...  10.9 us
    ppermute x12, waiting for transfers between devices, across_panel(): lax.ppermute(values, 'panel', [(i, i ^ bits[i & 1]) for i in range(count)])  10.3 us
    ppermute x12, starting transfers between devices, across_panel(): lax.ppermute(values, 'panel', [(i, i ^ bits[i & 1]) for i in range(count)])  9.63 us
  transfers between devices with their start and end apart: 28, of which 17 were waited for; matrix products, arithmetic and copies ran while one was open for 1% of the time, Pallas kernels for 3%

profile of v3, /device:TPU:0, one launch (start us, length us, event | category | flops | bytes accessed | tf_op | source)
XLA Modules:
  0.0 82.0 jit_solution(13284948465497174209)
XLA Ops:
  1.3 6.2 %shard_map.77 = (bf16[1024,1024]{1,0:T(8,128)(2,1)S(1)}, bf16[1024,1024]{1,0:T(8,128)(2,1)S(1)}, f32[1024,256]{1,0:T(8,128)S(1)}, f32[4,128,256]{2,1,0:T(8,128)S(1)}, f32[4,128,256]{2,1,0:T(8,128)S(1)}) custom-call(s32[1,1]{1,0:T(1,128)S(6)} %copy.8.count_ref, s32[1,1,40]{2,1,0:T(1,128)} %rows_hbm.1, s32[1,1,40]{2,1,0:T(1,128)} %cols_hbm.1, ...), custom_call_target="tpu_custom_call" | custom-call | flops 1610612736 | bytes 6291456 | tf_op jit(solution)/shard_map/pallas_call | solution.py:189
  8.1 3.0 %collective-permute-done.12 = f32[4,128,256]{2,1,0:T(8,128)S(1)} collective-permute-done((f32[4,128,256]{2,1,0:T(8,128)S(1)}, f32[4,128,256]{2,1,0:T(8,128)S(1)}, u32[]{:S(2)}, u32[]{:S(2)}) %collective-permute-start.12) | collective-permute-done | bytes 524320 | tf_op jit(solution)/shard_map/ppermute | solution.py:213
  11.1 2.9 %collective-permute-start.13 = (f32[4,128,256]{2,1,0:T(8,128)S(1)}, f32[4,128,256]{2,1,0:T(8,128)S(1)}, u32[]{:S(2)}, u32[]{:S(2)}) collective-permute-start(f32[4,128,256]{2,1,0:T(8,128)S(1)} %add.27), channel_id=1, source_target_pairs={{0,8},{4,20},{8,0},{12,28},{16,24},{20,4},{24,16},{28,12},{1,9},{5... | collective-permute-start | bytes 1572872 | tf_op jit(solution)/shard_map/users_0/ppermute | solution.py:213
  14.1 1.8 %collective-permute-start.1 = (f32[256,256]{1,0:T(8,128)S(1)}, f32[256,256]{1,0:T(8,128)S(1)}, u32[]{:S(2)}, u32[]{:S(2)}) collective-permute-start(f32[256,256]{1,0:T(8,128)S(1)} %shard_map.78), channel_id=1, source_target_pairs={{0,1},{4,0},{1,2},{5,4},{2,3},{6,5},{3,7},{7,6},{8,9},{12,8},{9,10... | collective-permute-start | bytes 786440 | tf_op jit(solution)/shard_map/line_0/ppermute | solution.py:208
  17.3 3.9 %collective-permute-done.13 = f32[4,128,256]{2,1,0:T(8,128)S(1)} collective-permute-done((f32[4,128,256]{2,1,0:T(8,128)S(1)}, f32[4,128,256]{2,1,0:T(8,128)S(1)}, u32[]{:S(2)}, u32[]{:S(2)}) %collective-permute-start.13) | collective-permute-done | bytes 524320 | tf_op jit(solution)/shard_map/users_0/ppermute | solution.py:213
  21.3 2.1 %collective-permute-start.14 = (f32[4,128,256]{2,1,0:T(8,128)S(1)}, f32[4,128,256]{2,1,0:T(8,128)S(1)}, u32[]{:S(2)}, u32[]{:S(2)}) collective-permute-start(f32[4,128,256]{2,1,0:T(8,128)S(1)} %add.28), channel_id=1, source_target_pairs={{0,16},{4,12},{8,24},{12,4},{16,0},{20,28},{24,8},{28,20},{1,17},{... | collective-permute-start | bytes 1572872 | tf_op jit(solution)/shard_map/users_1/ppermute | solution.py:213
  25.1 1.8 %collective-permute-start.3 = (f32[256,256]{1,0:T(8,128)S(1)}, f32[256,256]{1,0:T(8,128)S(1)}, u32[]{:S(2)}, u32[]{:S(2)}) collective-permute-start(f32[256,256]{1,0:T(8,128)S(1)} %shard_map.80), channel_id=1, source_target_pairs={{0,1},{4,0},{1,2},{5,4},{2,3},{6,5},{3,7},{7,6},{8,9},{12,8},{9,10... | collective-permute-start | bytes 786440 | tf_op jit(solution)/shard_map/line_2/ppermute | solution.py:208
  26.8 2.1 %collective-permute-done.4.refs_0_.refs_3_ = f32[256,256]{1,0:T(8,128)S(1)} collective-permute-done((f32[256,256]{1,0:T(8,128)S(1)}, f32[256,256]{1,0:T(8,128)S(1)}, u32[]{:S(2)}, u32[]{:S(2)}) %collective-permute-start.4) | collective-permute-done | bytes 262176 | tf_op jit(solution)/shard_map/line_3/ppermute | solution.py:208
  29.0 2.5 %collective-permute-start.6 = (f32[256,256]{1,0:T(8,128)S(1)}, f32[256,256]{1,0:T(8,128)S(1)}, u32[]{:S(2)}, u32[]{:S(2)}) collective-permute-start(f32[256,256]{1,0:T(8,128)S(1)} %shard_map.83), channel_id=1, source_target_pairs={{0,1},{4,0},{1,2},{5,4},{2,3},{6,5},{3,7},{7,6},{8,9},{12,8},{9,10... | collective-permute-start | bytes 786440 | tf_op jit(solution)/shard_map/line_5/ppermute | solution.py:208
  31.8 2.5 %collective-permute-start.5 = (f32[256,256]{1,0:T(8,128)S(1)}, f32[256,256]{1,0:T(8,128)S(1)}, u32[]{:S(2)}, u32[]{:S(2)}) collective-permute-start(f32[256,256]{1,0:T(8,128)S(1)} %shard_map.82), channel_id=1, source_target_pairs={{0,1},{4,0},{1,2},{5,4},{2,3},{6,5},{3,7},{7,6},{8,9},{12,8},{9,10... | collective-permute-start | bytes 786440 | tf_op jit(solution)/shard_map/line_4/ppermute | solution.py:208
  35.4 2.5 %collective-permute-start.8 = (f32[256,256]{1,0:T(8,128)S(1)}, f32[256,256]{1,0:T(8,128)S(1)}, u32[]{:S(2)}, u32[]{:S(2)}) collective-permute-start(f32[256,256]{1,0:T(8,128)S(1)} %shard_map.85), channel_id=1, source_target_pairs={{0,1},{4,0},{1,2},{5,4},{2,3},{6,5},{3,7},{7,6},{8,9},{12,8},{9,10... | collective-permute-start | bytes 786440 | tf_op jit(solution)/shard_map/line_7/ppermute | solution.py:208
  38.2 2.5 %collective-permute-start.7 = (f32[256,256]{1,0:T(8,128)S(1)}, f32[256,256]{1,0:T(8,128)S(1)}, u32[]{:S(2)}, u32[]{:S(2)}) collective-permute-start(f32[256,256]{1,0:T(8,128)S(1)} %shard_map.84), channel_id=1, source_target_pairs={{0,1},{4,0},{1,2},{5,4},{2,3},{6,5},{3,7},{7,6},{8,9},{12,8},{9,10... | collective-permute-start | bytes 786440 | tf_op jit(solution)/shard_map/line_6/ppermute | solution.py:208
  41.8 2.5 %collective-permute-start.10 = (f32[256,256]{1,0:T(8,128)S(1)}, f32[256,256]{1,0:T(8,128)S(1)}, u32[]{:S(2)}, u32[]{:S(2)}) collective-permute-start(f32[256,256]{1,0:T(8,128)S(1)} %shard_map.87), channel_id=1, source_target_pairs={{0,1},{4,0},{1,2},{5,4},{2,3},{6,5},{3,7},{7,6},{8,9},{12,8},{9,10... | collective-permute-start | bytes 786440 | tf_op jit(solution)/shard_map/line_9/ppermute | solution.py:208
  44.7 2.5 %collective-permute-start.9 = (f32[256,256]{1,0:T(8,128)S(1)}, f32[256,256]{1,0:T(8,128)S(1)}, u32[]{:S(2)}, u32[]{:S(2)}) collective-permute-start(f32[256,256]{1,0:T(8,128)S(1)} %shard_map.86), channel_id=1, source_target_pairs={{0,1},{4,0},{1,2},{5,4},{2,3},{6,5},{3,7},{7,6},{8,9},{12,8},{9,10... | collective-permute-start | bytes 786440 | tf_op jit(solution)/shard_map/line_8/ppermute | solution.py:208
  47.2 2.2 %shard_map.89.refs_4_.again_ref = f32[1024,256]{1,0:T(8,128)S(1)} custom-call(bf16[1024,1024]{1,0:T(8,128)(2,1)S(1)} %get-tuple-element.20.high_ref, bf16[1024,1024]{1,0:T(8,128)(2,1)S(1)} %get-tuple-element.21.low_ref, f32[4,128,256]{2,1,0:T(8,128)S(1)} %add.29.mine_ref.users_ref, f32[4,128,256]{2,1,0:T(8,128)S(1)} %collective-permute-done.15.other_ref), custom_call_target="tpu_custom_call" | custom-call | flops 1610612736 | bytes 6291456 | tf_op jit(solution)/shard_map/pallas_call | solution.py:189
  52.1 1.7 %collective-permute-start.18 = (f32[256,256]{1,0:T(8,128)S(1)}, f32[256,256]{1,0:T(8,128)S(1)}, u32[]{:S(2)}, u32[]{:S(2)}) collective-permute-start(f32[256,256]{1,0:T(8,128)S(1)} %shard_map.91), channel_id=1, source_target_pairs={{0,1},{4,0},{1,2},{5,4},{2,3},{6,5},{3,7},{7,6},{8,9},{12,8},{9,10... | collective-permute-start | bytes 786440 | tf_op jit(solution)/shard_map/line_11/ppermute | solution.py:208
  55.7 2.1 %collective-permute-done.18.rest_7_.refs_0_ = f32[256,256]{1,0:T(8,128)S(1)} collective-permute-done((f32[256,256]{1,0:T(8,128)S(1)}, f32[256,256]{1,0:T(8,128)S(1)}, u32[]{:S(2)}, u32[]{:S(2)}) %collective-permute-start.18) | collective-permute-done | bytes 262176 | tf_op jit(solution)/shard_map/line_11/ppermute | solution.py:208
  57.8 2.8 %collective-permute-done.17.rest_6_.refs_0_ = f32[256,256]{1,0:T(8,128)S(1)} collective-permute-done((f32[256,256]{1,0:T(8,128)S(1)}, f32[256,256]{1,0:T(8,128)S(1)}, u32[]{:S(2)}, u32[]{:S(2)}) %collective-permute-start.17) | collective-permute-done | bytes 262176 | tf_op jit(solution)/shard_map/line_10/ppermute | solution.py:208
  60.6 2.1 %shard_map.92 = (f32[4,128,256]{2,1,0:T(8,128)S(1)}, f32[4,128,256]{2,1,0:T(8,128)S(1)}, f32[256,256]{1,0:T(8,128)S(1)}) custom-call(f32[1024,256]{1,0:T(8,128)} %user_cot_hbm.1, f32[1024,256]{1,0:T(8,128)} %item_cot_hbm.1, bf16[1024,1024]{1,0:T(8,128)(2,1)S(1)} %get-tuple-element.20.high_ref, bf16[1024,1024]{1,0:T(8,128)(2,1)S(1)} %get-tuple-element.21.low_ref, ...), custom_call_target="tpu_custom_call" | custom-call | flops 1610612736 | bytes 6291456 | tf_op jit(solution)/shard_map/pallas_call | solution.py:189
  62.9 2.5 %collective-permute-start.25 = (f32[256,256]{1,0:T(8,128)S(1)}, f32[256,256]{1,0:T(8,128)S(1)}, u32[]{:S(2)}, u32[]{:S(2)}) collective-permute-start(f32[256,256]{1,0:T(8,128)S(1)} %shard_map.95), channel_id=1, source_target_pairs={{0,1},{4,0},{1,2},{5,4},{2,3},{6,5},{3,7},{7,6},{8,9},{12,8},{9,10... | collective-permute-start | bytes 786440 | tf_op jit(solution)/shard_map/line_12/ppermute | solution.py:208
  65.5 1.7 %collective-permute-start.23 = (f32[256,256]{1,0:T(8,128)S(1)}, f32[256,256]{1,0:T(8,128)S(1)}, u32[]{:S(2)}, u32[]{:S(2)}) collective-permute-start(f32[256,256]{1,0:T(8,128)S(1)} %shard_map.93), channel_id=1, source_target_pairs={{0,1},{4,0},{1,2},{5,4},{2,3},{6,5},{3,7},{7,6},{8,9},{12,8},{9,10... | collective-permute-start | bytes 786440 | tf_op jit(solution)/shard_map/line_13/ppermute | solution.py:208
  67.2 2.1 %collective-permute-done.25.refs_0_ = f32[256,256]{1,0:T(8,128)S(1)} collective-permute-done((f32[256,256]{1,0:T(8,128)S(1)}, f32[256,256]{1,0:T(8,128)S(1)}, u32[]{:S(2)}, u32[]{:S(2)}) %collective-permute-start.25) | collective-permute-done | bytes 262176 | tf_op jit(solution)/shard_map/line_12/ppermute | solution.py:208
  69.4 2.5 %collective-permute-start.26 = (f32[256,256]{1,0:T(8,128)S(1)}, f32[256,256]{1,0:T(8,128)S(1)}, u32[]{:S(2)}, u32[]{:S(2)}) collective-permute-start(f32[256,256]{1,0:T(8,128)S(1)} %shard_map.96), channel_id=1, source_target_pairs={{0,1},{4,0},{1,2},{5,4},{2,3},{6,5},{3,7},{7,6},{8,9},{12,8},{9,10... | collective-permute-start | bytes 786440 | tf_op jit(solution)/shard_map/line_14/ppermute | solution.py:208
  75.6 1.7 %collective-permute-start.24 = (f32[256,256]{1,0:T(8,128)S(1)}, f32[256,256]{1,0:T(8,128)S(1)}, u32[]{:S(2)}, u32[]{:S(2)}) collective-permute-start(f32[256,256]{1,0:T(8,128)S(1)} %shard_map.94), channel_id=1, source_target_pairs={{0,1},{4,0},{1,2},{5,4},{2,3},{6,5},{3,7},{7,6},{8,9},{12,8},{9,10... | collective-permute-start | bytes 786440 | tf_op jit(solution)/shard_map/line_15/ppermute | solution.py:208
  (59 shorter events, 20.0 us)
Async XLA Ops:
  7.5 6.6 %collective-permute-start = (f32[1024,256]{1,0:T(8,128)S(1)}, f32[1024,256]{1,0:T(8,128)S(1)}, u32[]{:S(2)}, u32[]{:S(2)}) collective-permute-start(f32[1024,256]{1,0:T(8,128)S(1)} %get-tuple-element.22.refs_2_.sums_ref), channel_id=1, source_target_pairs={{0,4},{4,0},{8,12},{12,8},{16,20},{20,16},{24,28},{28,24},{1,5},{5... | collective-permute-start | bytes 3145736 | tf_op jit(solution)/shard_map/ppermute | solution.py:213
  11.1 10.1 %collective-permute-start.13 = (f32[4,128,256]{2,1,0:T(8,128)S(1)}, f32[4,128,256]{2,1,0:T(8,128)S(1)}, u32[]{:S(2)}, u32[]{:S(2)}) collective-permute-start(f32[4,128,256]{2,1,0:T(8,128)S(1)} %add.27), channel_id=1, source_target_pairs={{0,8},{4,20},{8,0},{12,28},{16,24},{20,4},{24,16},{28,12},{1,9},{5... | collective-permute-start | bytes 1572872 | tf_op jit(solution)/shard_map/users_0/ppermute | solution.py:213
  14.1 7.2 %collective-permute-start.1 = (f32[256,256]{1,0:T(8,128)S(1)}, f32[256,256]{1,0:T(8,128)S(1)}, u32[]{:S(2)}, u32[]{:S(2)}) collective-permute-start(f32[256,256]{1,0:T(8,128)S(1)} %shard_map.78), channel_id=1, source_target_pairs={{0,1},{4,0},{1,2},{5,4},{2,3},{6,5},{3,7},{7,6},{8,9},{12,8},{9,10... | collective-permute-start | bytes 786440 | tf_op jit(solution)/shard_map/line_0/ppermute | solution.py:208
  15.8 7.6 %collective-permute-start.2 = (f32[256,256]{1,0:T(8,128)S(1)}, f32[256,256]{1,0:T(8,128)S(1)}, u32[]{:S(2)}, u32[]{:S(2)}) collective-permute-start(f32[256,256]{1,0:T(8,128)S(1)} %shard_map.79), channel_id=1, source_target_pairs={{0,1},{4,0},{1,2},{5,4},{2,3},{6,5},{3,7},{7,6},{8,9},{12,8},{9,10... | collective-permute-start | bytes 786440 | tf_op jit(solution)/shard_map/line_1/ppermute | solution.py:208
  21.3 13.0 %collective-permute-start.14 = (f32[4,128,256]{2,1,0:T(8,128)S(1)}, f32[4,128,256]{2,1,0:T(8,128)S(1)}, u32[]{:S(2)}, u32[]{:S(2)}) collective-permute-start(f32[4,128,256]{2,1,0:T(8,128)S(1)} %add.28), channel_id=1, source_target_pairs={{0,16},{4,12},{8,24},{12,4},{16,0},{20,28},{24,8},{28,20},{1,17},{... | collective-permute-start | bytes 1572872 | tf_op jit(solution)/shard_map/users_1/ppermute | solution.py:213
  23.4 5.5 %collective-permute-start.4 = (f32[256,256]{1,0:T(8,128)S(1)}, f32[256,256]{1,0:T(8,128)S(1)}, u32[]{:S(2)}, u32[]{:S(2)}) collective-permute-start(f32[256,256]{1,0:T(8,128)S(1)} %shard_map.81), channel_id=1, source_target_pairs={{0,1},{4,0},{1,2},{5,4},{2,3},{6,5},{3,7},{7,6},{8,9},{12,8},{9,10... | collective-permute-start | bytes 786440 | tf_op jit(solution)/shard_map/line_3/ppermute | solution.py:208
  25.1 6.7 %collective-permute-start.3 = (f32[256,256]{1,0:T(8,128)S(1)}, f32[256,256]{1,0:T(8,128)S(1)}, u32[]{:S(2)}, u32[]{:S(2)}) collective-permute-start(f32[256,256]{1,0:T(8,128)S(1)} %shard_map.80), channel_id=1, source_target_pairs={{0,1},{4,0},{1,2},{5,4},{2,3},{6,5},{3,7},{7,6},{8,9},{12,8},{9,10... | collective-permute-start | bytes 786440 | tf_op jit(solution)/shard_map/line_2/ppermute | solution.py:208
  29.0 6.4 %collective-permute-start.6 = (f32[256,256]{1,0:T(8,128)S(1)}, f32[256,256]{1,0:T(8,128)S(1)}, u32[]{:S(2)}, u32[]{:S(2)}) collective-permute-start(f32[256,256]{1,0:T(8,128)S(1)} %shard_map.83), channel_id=1, source_target_pairs={{0,1},{4,0},{1,2},{5,4},{2,3},{6,5},{3,7},{7,6},{8,9},{12,8},{9,10... | collective-permute-start | bytes 786440 | tf_op jit(solution)/shard_map/line_5/ppermute | solution.py:208
  31.8 6.4 %collective-permute-start.5 = (f32[256,256]{1,0:T(8,128)S(1)}, f32[256,256]{1,0:T(8,128)S(1)}, u32[]{:S(2)}, u32[]{:S(2)}) collective-permute-start(f32[256,256]{1,0:T(8,128)S(1)} %shard_map.82), channel_id=1, source_target_pairs={{0,1},{4,0},{1,2},{5,4},{2,3},{6,5},{3,7},{7,6},{8,9},{12,8},{9,10... | collective-permute-start | bytes 786440 | tf_op jit(solution)/shard_map/line_4/ppermute | solution.py:208
  34.4 12.8 %collective-permute-start.15 = (f32[4,128,256]{2,1,0:T(8,128)S(1)}, f32[4,128,256]{2,1,0:T(8,128)S(1)}, u32[]{:S(2)}, u32[]{:S(2)}) collective-permute-start(f32[4,128,256]{2,1,0:T(8,128)S(1)} %add.29.mine_ref.users_ref), channel_id=1, source_target_pairs={{0,4},{4,0},{8,12},{12,8},{16,20},{20,16},{24,28},{28,24},{1,5},{5... | collective-permute-start | bytes 1572872 | tf_op jit(solution)/shard_map/ppermute | solution.py:213
  35.4 6.4 %collective-permute-start.8 = (f32[256,256]{1,0:T(8,128)S(1)}, f32[256,256]{1,0:T(8,128)S(1)}, u32[]{:S(2)}, u32[]{:S(2)}) collective-permute-start(f32[256,256]{1,0:T(8,128)S(1)} %shard_map.85), channel_id=1, source_target_pairs={{0,1},{4,0},{1,2},{5,4},{2,3},{6,5},{3,7},{7,6},{8,9},{12,8},{9,10... | collective-permute-start | bytes 786440 | tf_op jit(solution)/shard_map/line_7/ppermute | solution.py:208
  38.2 6.4 %collective-permute-start.7 = (f32[256,256]{1,0:T(8,128)S(1)}, f32[256,256]{1,0:T(8,128)S(1)}, u32[]{:S(2)}, u32[]{:S(2)}) collective-permute-start(f32[256,256]{1,0:T(8,128)S(1)} %shard_map.84), channel_id=1, source_target_pairs={{0,1},{4,0},{1,2},{5,4},{2,3},{6,5},{3,7},{7,6},{8,9},{12,8},{9,10... | collective-permute-start | bytes 786440 | tf_op jit(solution)/shard_map/line_6/ppermute | solution.py:208
  41.8 7.6 %collective-permute-start.10 = (f32[256,256]{1,0:T(8,128)S(1)}, f32[256,256]{1,0:T(8,128)S(1)}, u32[]{:S(2)}, u32[]{:S(2)}) collective-permute-start(f32[256,256]{1,0:T(8,128)S(1)} %shard_map.87), channel_id=1, source_target_pairs={{0,1},{4,0},{1,2},{5,4},{2,3},{6,5},{3,7},{7,6},{8,9},{12,8},{9,10... | collective-permute-start | bytes 786440 | tf_op jit(solution)/shard_map/line_9/ppermute | solution.py:208
  44.7 6.4 %collective-permute-start.9 = (f32[256,256]{1,0:T(8,128)S(1)}, f32[256,256]{1,0:T(8,128)S(1)}, u32[]{:S(2)}, u32[]{:S(2)}) collective-permute-start(f32[256,256]{1,0:T(8,128)S(1)} %shard_map.86), channel_id=1, source_target_pairs={{0,1},{4,0},{1,2},{5,4},{2,3},{6,5},{3,7},{7,6},{8,9},{12,8},{9,10... | collective-permute-start | bytes 786440 | tf_op jit(solution)/shard_map/line_8/ppermute | solution.py:208
  52.1 5.6 %collective-permute-start.18 = (f32[256,256]{1,0:T(8,128)S(1)}, f32[256,256]{1,0:T(8,128)S(1)}, u32[]{:S(2)}, u32[]{:S(2)}) collective-permute-start(f32[256,256]{1,0:T(8,128)S(1)} %shard_map.91), channel_id=1, source_target_pairs={{0,1},{4,0},{1,2},{5,4},{2,3},{6,5},{3,7},{7,6},{8,9},{12,8},{9,10... | collective-permute-start | bytes 786440 | tf_op jit(solution)/shard_map/line_11/ppermute | solution.py:208
  53.9 6.7 %collective-permute-start.17 = (f32[256,256]{1,0:T(8,128)S(1)}, f32[256,256]{1,0:T(8,128)S(1)}, u32[]{:S(2)}, u32[]{:S(2)}) collective-permute-start(f32[256,256]{1,0:T(8,128)S(1)} %shard_map.90), channel_id=1, source_target_pairs={{0,1},{4,0},{1,2},{5,4},{2,3},{6,5},{3,7},{7,6},{8,9},{12,8},{9,10... | collective-permute-start | bytes 786440 | tf_op jit(solution)/shard_map/line_10/ppermute | solution.py:208
  62.7 9.2 %collective-permute-start.19 = (f32[4,128,256]{2,1,0:T(8,128)S(1)}, f32[4,128,256]{2,1,0:T(8,128)S(1)}, u32[]{:S(2)}, u32[]{:S(2)}) collective-permute-start(f32[4,128,256]{2,1,0:T(8,128)S(1)} %get-tuple-element.36), channel_id=1, source_target_pairs={{0,4},{4,0},{8,12},{12,8},{16,20},{20,16},{24,28},{28,24},{1,5},{5... | collective-permute-start | bytes 1572872 | tf_op jit(solution)/shard_map/ppermute | solution.py:213
  62.9 6.4 %collective-permute-start.25 = (f32[256,256]{1,0:T(8,128)S(1)}, f32[256,256]{1,0:T(8,128)S(1)}, u32[]{:S(2)}, u32[]{:S(2)}) collective-permute-start(f32[256,256]{1,0:T(8,128)S(1)} %shard_map.95), channel_id=1, source_target_pairs={{0,1},{4,0},{1,2},{5,4},{2,3},{6,5},{3,7},{7,6},{8,9},{12,8},{9,10... | collective-permute-start | bytes 786440 | tf_op jit(solution)/shard_map/line_12/ppermute | solution.py:208
  65.5 10.1 %collective-permute-start.23 = (f32[256,256]{1,0:T(8,128)S(1)}, f32[256,256]{1,0:T(8,128)S(1)}, u32[]{:S(2)}, u32[]{:S(2)}) collective-permute-start(f32[256,256]{1,0:T(8,128)S(1)} %shard_map.93), channel_id=1, source_target_pairs={{0,1},{4,0},{1,2},{5,4},{2,3},{6,5},{3,7},{7,6},{8,9},{12,8},{9,10... | collective-permute-start | bytes 786440 | tf_op jit(solution)/shard_map/line_13/ppermute | solution.py:208
  69.4 8.0 %collective-permute-start.26 = (f32[256,256]{1,0:T(8,128)S(1)}, f32[256,256]{1,0:T(8,128)S(1)}, u32[]{:S(2)}, u32[]{:S(2)}) collective-permute-start(f32[256,256]{1,0:T(8,128)S(1)} %shard_map.96), channel_id=1, source_target_pairs={{0,1},{4,0},{1,2},{5,4},{2,3},{6,5},{3,7},{7,6},{8,9},{12,8},{9,10... | collective-permute-start | bytes 786440 | tf_op jit(solution)/shard_map/line_14/ppermute | solution.py:208
  72.0 6.0 %collective-permute-start.20 = (f32[128,256]{1,0:T(8,128)S(1)}, f32[128,256]{1,0:T(8,128)S(1)}, u32[]{:S(2)}, u32[]{:S(2)}) collective-permute-start(f32[128,256]{1,0:T(8,128)S(1)} %get-tuple-element.38), channel_id=1, source_target_pairs={{0,24},{4,28},{8,16},{12,20},{16,8},{20,12},{24,0},{28,4},{1,25},{... | collective-permute-start | bytes 393224 | tf_op jit(solution)/shard_map/ppermute | solution.py:213
  73.6 5.7 %collective-permute-start.21 = (f32[128,256]{1,0:T(8,128)S(1)}, f32[128,256]{1,0:T(8,128)S(1)}, u32[]{:S(2)}, u32[]{:S(2)}) collective-permute-start(f32[128,256]{1,0:T(8,128)S(1)} %get-tuple-element.40), channel_id=1, source_target_pairs={{0,16},{4,20},{8,24},{12,28},{16,0},{20,4},{24,8},{28,12},{1,17},{... | collective-permute-start | bytes 393224 | tf_op jit(solution)/shard_map/ppermute | solution.py:213
  75.0 5.0 %collective-permute-start.22 = (f32[128,256]{1,0:T(8,128)S(1)}, f32[128,256]{1,0:T(8,128)S(1)}, u32[]{:S(2)}, u32[]{:S(2)}) collective-permute-start(f32[128,256]{1,0:T(8,128)S(1)} %get-tuple-element.39), channel_id=1, source_target_pairs={{0,8},{4,12},{8,0},{12,4},{16,24},{20,28},{24,16},{28,20},{1,9},{5... | collective-permute-start | bytes 393224 | tf_op jit(solution)/shard_map/ppermute | solution.py:213
  75.6 5.6 %collective-permute-start.24 = (f32[256,256]{1,0:T(8,128)S(1)}, f32[256,256]{1,0:T(8,128)S(1)}, u32[]{:S(2)}, u32[]{:S(2)}) collective-permute-start(f32[256,256]{1,0:T(8,128)S(1)} %shard_map.94), channel_id=1, source_target_pairs={{0,1},{4,0},{1,2},{5,4},{2,3},{6,5},{3,7},{7,6},{8,9},{12,8},{9,10... | collective-permute-start | bytes 786440 | tf_op jit(solution)/shard_map/line_15/ppermute | solution.py:208
  (4 other events, 14.1 us)

commit v4 on v3

--- a/solution.py
+++ b/solution.py
@@ -249,17 +249,17 @@
         **cost,
     )
 
-    sources = [swap(sums), sums]
     users = mine + swap(other)
+    sources = [swap(after(sums, users)), sums]
     rounds = (chips - 1).bit_length()
     arrivals = []
     for step in range(4 * n_rep - 2 + OFFSET):
         if step == 2 * n_rep + OFFSET:
             for k in range(rounds):
-                users = after(users, *arrivals[max(k - 1, 0) : k])
+                users = after(users, *(arrivals[k : k + 1] if k else []))
                 with jax.named_scope(f"users_{k}"):
                     users = users + across_panel(users, (2 << k, 2 << ((k + rounds // 2) % rounds)))
-            users = after(users, *arrivals[rounds - 1 : rounds])
+            users = after(users, *arrivals[rounds : rounds + 1])
             (again,) = call(items_kernel, [items], (high, low, users, swap(users)), [space(n_user, feature)], **cost)
             sources += [swap(again), again]
         before = arrivals[step - 2 : step - 1] if step >= 2 else []

time: 82.1 us -> 80.6 us (0.982)
  waiting for transfers between devices: 24.5 us -> 22.6 us
    ppermute x12, waiting for transfers between devices: 10.3 us -> 8.2 us  [across_panel(): lax.ppermute(values, 'panel', [(i, i ^ bits[i & 1]) for i in range(count)])]
where the time goes in v4:
time: 80.6 us; the launch traced here: 80.5 us
  starting transfers between devices  43.8 us (54%)
  waiting for transfers between devices  22.6 us (28%)
  Pallas kernels  10.9 us (14%)
  other arithmetic  1.72 us (2%)
  between operations  1.5 us (2%)
    ppermute x16, starting transfers between devices, along_line(): return lax.ppermute(values, ('panel', 'rep'), pairs)  33.9 us
    ppermute x16, waiting for transfers between devices, along_line(): return lax.ppermute(values, ('panel', 'rep'), pairs)  14.4 us
    pallas_call x20, Pallas kernels, call(): pl.pallas_call(kernel, out_shape=out_shape, in_specs=[pl.BlockSpec(memory...  10.9 us
    ppermute x12, starting transfers between devices, across_panel(): lax.ppermute(values, 'panel', [(i, i ^ bits[i & 1]) for i in range(count)])  9.86 us
    ppermute x12, waiting for transfers between devices, across_panel(): lax.ppermute(values, 'panel', [(i, i ^ bits[i & 1]) for i in range(count)])  8.2 us
  transfers between devices with their start and end apart: 28, of which 17 were waited for; matrix products, arithmetic and copies ran while one was open for 1% of the time, Pallas kernels for 3%

profile of v4, /device:TPU:0, one launch (start us, length us, event | category | flops | bytes accessed | tf_op | source)
XLA Modules:
  0.0 80.5 jit_solution(15859297019689119050)
XLA Ops:
  1.3 6.2 %shard_map.77 = (bf16[1024,1024]{1,0:T(8,128)(2,1)S(1)}, bf16[1024,1024]{1,0:T(8,128)(2,1)S(1)}, f32[1024,256]{1,0:T(8,128)S(1)}, f32[4,128,256]{2,1,0:T(8,128)S(1)}, f32[4,128,256]{2,1,0:T(8,128)S(1)}) custom-call(s32[1,1]{1,0:T(1,128)S(6)} %copy.8.count_ref, s32[1,1,40]{2,1,0:T(1,128)} %rows_hbm.1, s32[1,1,40]{2,1,0:T(1,128)} %cols_hbm.1, ...), custom_call_target="tpu_custom_call" | custom-call | flops 1610612736 | bytes 6291456 | tf_op jit(solution)/shard_map/pallas_call | solution.py:189
  10.2 2.6 %collective-permute-start.13 = (f32[4,128,256]{2,1,0:T(8,128)S(1)}, f32[4,128,256]{2,1,0:T(8,128)S(1)}, u32[]{:S(2)}, u32[]{:S(2)}) collective-permute-start(f32[4,128,256]{2,1,0:T(8,128)S(1)} %add.27), channel_id=1, source_target_pairs={{0,8},{4,20},{8,0},{12,28},{16,24},{20,4},{24,16},{28,12},{1,9},{5... | collective-permute-start | bytes 1572872 | tf_op jit(solution)/shard_map/users_0/ppermute | solution.py:213
  12.9 2.5 %collective-permute-start.3 = (f32[256,256]{1,0:T(8,128)S(1)}, f32[256,256]{1,0:T(8,128)S(1)}, u32[]{:S(2)}, u32[]{:S(2)}) collective-permute-start(f32[256,256]{1,0:T(8,128)S(1)} %shard_map.79), channel_id=1, source_target_pairs={{0,1},{4,0},{1,2},{5,4},{2,3},{6,5},{3,7},{7,6},{8,9},{12,8},{9,10... | collective-permute-start | bytes 786440 | tf_op jit(solution)/shard_map/line_1/ppermute | solution.py:208
  16.9 3.1 %collective-permute-done.13 = f32[4,128,256]{2,1,0:T(8,128)S(1)} collective-permute-done((f32[4,128,256]{2,1,0:T(8,128)S(1)}, f32[4,128,256]{2,1,0:T(8,128)S(1)}, u32[]{:S(2)}, u32[]{:S(2)}) %collective-permute-start.13) | collective-permute-done | bytes 524320 | tf_op jit(solution)/shard_map/users_0/ppermute | solution.py:213
  20.1 2.1 %collective-permute-start.14 = (f32[4,128,256]{2,1,0:T(8,128)S(1)}, f32[4,128,256]{2,1,0:T(8,128)S(1)}, u32[]{:S(2)}, u32[]{:S(2)}) collective-permute-start(f32[4,128,256]{2,1,0:T(8,128)S(1)} %add.28), channel_id=1, source_target_pairs={{0,16},{4,12},{8,24},{12,4},{16,0},{20,28},{24,8},{28,20},{1,17},{... | collective-permute-start | bytes 1572872 | tf_op jit(solution)/shard_map/users_1/ppermute | solution.py:213
  23.7 1.6 %collective-permute-start.4 = (f32[256,256]{1,0:T(8,128)S(1)}, f32[256,256]{1,0:T(8,128)S(1)}, u32[]{:S(2)}, u32[]{:S(2)}) collective-permute-start(f32[256,256]{1,0:T(8,128)S(1)} %shard_map.80), channel_id=1, source_target_pairs={{0,1},{4,0},{1,2},{5,4},{2,3},{6,5},{3,7},{7,6},{8,9},{12,8},{9,10... | collective-permute-start | bytes 786440 | tf_op jit(solution)/shard_map/line_2/ppermute | solution.py:208
  25.3 2.2 %collective-permute-done.5.refs_0_.refs_3_ = f32[256,256]{1,0:T(8,128)S(1)} collective-permute-done((f32[256,256]{1,0:T(8,128)S(1)}, f32[256,256]{1,0:T(8,128)S(1)}, u32[]{:S(2)}, u32[]{:S(2)}) %collective-permute-start.5) | collective-permute-done | bytes 262176 | tf_op jit(solution)/shard_map/line_3/ppermute | solution.py:208
  27.6 2.5 %collective-permute-start.7 = (f32[256,256]{1,0:T(8,128)S(1)}, f32[256,256]{1,0:T(8,128)S(1)}, u32[]{:S(2)}, u32[]{:S(2)}) collective-permute-start(f32[256,256]{1,0:T(8,128)S(1)} %shard_map.83), channel_id=1, source_target_pairs={{0,1},{4,0},{1,2},{5,4},{2,3},{6,5},{3,7},{7,6},{8,9},{12,8},{9,10... | collective-permute-start | bytes 786440 | tf_op jit(solution)/shard_map/line_5/ppermute | solution.py:208
  30.4 2.5 %collective-permute-start.6 = (f32[256,256]{1,0:T(8,128)S(1)}, f32[256,256]{1,0:T(8,128)S(1)}, u32[]{:S(2)}, u32[]{:S(2)}) collective-permute-start(f32[256,256]{1,0:T(8,128)S(1)} %shard_map.82), channel_id=1, source_target_pairs={{0,1},{4,0},{1,2},{5,4},{2,3},{6,5},{3,7},{7,6},{8,9},{12,8},{9,10... | collective-permute-start | bytes 786440 | tf_op jit(solution)/shard_map/line_4/ppermute | solution.py:208
  34.0 2.5 %collective-permute-start.9 = (f32[256,256]{1,0:T(8,128)S(1)}, f32[256,256]{1,0:T(8,128)S(1)}, u32[]{:S(2)}, u32[]{:S(2)}) collective-permute-start(f32[256,256]{1,0:T(8,128)S(1)} %shard_map.85), channel_id=1, source_target_pairs={{0,1},{4,0},{1,2},{5,4},{2,3},{6,5},{3,7},{7,6},{8,9},{12,8},{9,10... | collective-permute-start | bytes 786440 | tf_op jit(solution)/shard_map/line_7/ppermute | solution.py:208
  36.8 2.5 %collective-permute-start.8 = (f32[256,256]{1,0:T(8,128)S(1)}, f32[256,256]{1,0:T(8,128)S(1)}, u32[]{:S(2)}, u32[]{:S(2)}) collective-permute-start(f32[256,256]{1,0:T(8,128)S(1)} %shard_map.84), channel_id=1, source_target_pairs={{0,1},{4,0},{1,2},{5,4},{2,3},{6,5},{3,7},{7,6},{8,9},{12,8},{9,10... | collective-permute-start | bytes 786440 | tf_op jit(solution)/shard_map/line_6/ppermute | solution.py:208
  40.5 2.5 %collective-permute-start.11 = (f32[256,256]{1,0:T(8,128)S(1)}, f32[256,256]{1,0:T(8,128)S(1)}, u32[]{:S(2)}, u32[]{:S(2)}) collective-permute-start(f32[256,256]{1,0:T(8,128)S(1)} %shard_map.87), channel_id=1, source_target_pairs={{0,1},{4,0},{1,2},{5,4},{2,3},{6,5},{3,7},{7,6},{8,9},{12,8},{9,10... | collective-permute-start | bytes 786440 | tf_op jit(solution)/shard_map/line_9/ppermute | solution.py:208
  43.3 2.5 %collective-permute-start.10 = (f32[256,256]{1,0:T(8,128)S(1)}, f32[256,256]{1,0:T(8,128)S(1)}, u32[]{:S(2)}, u32[]{:S(2)}) collective-permute-start(f32[256,256]{1,0:T(8,128)S(1)} %shard_map.86), channel_id=1, source_target_pairs={{0,1},{4,0},{1,2},{5,4},{2,3},{6,5},{3,7},{7,6},{8,9},{12,8},{9,10... | collective-permute-start | bytes 786440 | tf_op jit(solution)/shard_map/line_8/ppermute | solution.py:208
  45.8 2.2 %shard_map.89.refs_4_.again_ref = f32[1024,256]{1,0:T(8,128)S(1)} custom-call(bf16[1024,1024]{1,0:T(8,128)(2,1)S(1)} %get-tuple-element.21.high_ref, bf16[1024,1024]{1,0:T(8,128)(2,1)S(1)} %get-tuple-element.22.low_ref, f32[4,128,256]{2,1,0:T(8,128)S(1)} %add.29.mine_ref.users_ref, f32[4,128,256]{2,1,0:T(8,128)S(1)} %collective-permute-done.15.other_ref), custom_call_target="tpu_custom_call" | custom-call | flops 1610612736 | bytes 6291456 | tf_op jit(solution)/shard_map/pallas_call | solution.py:189
  48.1 1.6 %collective-permute-done.10.refs_0_.rest_4_ = f32[256,256]{1,0:T(8,128)S(1)} collective-permute-done((f32[256,256]{1,0:T(8,128)S(1)}, f32[256,256]{1,0:T(8,128)S(1)}, u32[]{:S(2)}, u32[]{:S(2)}) %collective-permute-start.10) | collective-permute-done | bytes 262176 | tf_op jit(solution)/shard_map/line_8/ppermute | solution.py:208
  50.7 1.7 %collective-permute-start.18 = (f32[256,256]{1,0:T(8,128)S(1)}, f32[256,256]{1,0:T(8,128)S(1)}, u32[]{:S(2)}, u32[]{:S(2)}) collective-permute-start(f32[256,256]{1,0:T(8,128)S(1)} %shard_map.91), channel_id=1, source_target_pairs={{0,1},{4,0},{1,2},{5,4},{2,3},{6,5},{3,7},{7,6},{8,9},{12,8},{9,10... | collective-permute-start | bytes 786440 | tf_op jit(solution)/shard_map/line_11/ppermute | solution.py:208
  54.1 2.3 %collective-permute-done.18.rest_7_.refs_0_ = f32[256,256]{1,0:T(8,128)S(1)} collective-permute-done((f32[256,256]{1,0:T(8,128)S(1)}, f32[256,256]{1,0:T(8,128)S(1)}, u32[]{:S(2)}, u32[]{:S(2)}) %collective-permute-start.18) | collective-permute-done | bytes 262176 | tf_op jit(solution)/shard_map/line_11/ppermute | solution.py:208
  56.4 2.8 %collective-permute-done.17.rest_6_.refs_0_ = f32[256,256]{1,0:T(8,128)S(1)} collective-permute-done((f32[256,256]{1,0:T(8,128)S(1)}, f32[256,256]{1,0:T(8,128)S(1)}, u32[]{:S(2)}, u32[]{:S(2)}) %collective-permute-start.17) | collective-permute-done | bytes 262176 | tf_op jit(solution)/shard_map/line_10/ppermute | solution.py:208
  59.2 2.1 %shard_map.92 = (f32[4,128,256]{2,1,0:T(8,128)S(1)}, f32[4,128,256]{2,1,0:T(8,128)S(1)}, f32[256,256]{1,0:T(8,128)S(1)}) custom-call(f32[1024,256]{1,0:T(8,128)} %user_cot_hbm.1, f32[1024,256]{1,0:T(8,128)} %item_cot_hbm.1, bf16[1024,1024]{1,0:T(8,128)(2,1)S(1)} %get-tuple-element.21.high_ref, bf16[1024,1024]{1,0:T(8,128)(2,1)S(1)} %get-tuple-element.22.low_ref, ...), custom_call_target="tpu_custom_call" | custom-call | flops 1610612736 | bytes 6291456 | tf_op jit(solution)/shard_map/pallas_call | solution.py:189
  61.6 2.5 %collective-permute-start.25 = (f32[256,256]{1,0:T(8,128)S(1)}, f32[256,256]{1,0:T(8,128)S(1)}, u32[]{:S(2)}, u32[]{:S(2)}) collective-permute-start(f32[256,256]{1,0:T(8,128)S(1)} %shard_map.95), channel_id=1, source_target_pairs={{0,1},{4,0},{1,2},{5,4},{2,3},{6,5},{3,7},{7,6},{8,9},{12,8},{9,10... | collective-permute-start | bytes 786440 | tf_op jit(solution)/shard_map/line_12/ppermute | solution.py:208
  64.1 1.6 %collective-permute-start.23 = (f32[256,256]{1,0:T(8,128)S(1)}, f32[256,256]{1,0:T(8,128)S(1)}, u32[]{:S(2)}, u32[]{:S(2)}) collective-permute-start(f32[256,256]{1,0:T(8,128)S(1)} %shard_map.93), channel_id=1, source_target_pairs={{0,1},{4,0},{1,2},{5,4},{2,3},{6,5},{3,7},{7,6},{8,9},{12,8},{9,10... | collective-permute-start | bytes 786440 | tf_op jit(solution)/shard_map/line_13/ppermute | solution.py:208
  65.7 2.3 %collective-permute-done.25.refs_0_ = f32[256,256]{1,0:T(8,128)S(1)} collective-permute-done((f32[256,256]{1,0:T(8,128)S(1)}, f32[256,256]{1,0:T(8,128)S(1)}, u32[]{:S(2)}, u32[]{:S(2)}) %collective-permute-start.25) | collective-permute-done | bytes 262176 | tf_op jit(solution)/shard_map/line_12/ppermute | solution.py:208
  68.0 2.5 %collective-permute-start.26 = (f32[256,256]{1,0:T(8,128)S(1)}, f32[256,256]{1,0:T(8,128)S(1)}, u32[]{:S(2)}, u32[]{:S(2)}) collective-permute-start(f32[256,256]{1,0:T(8,128)S(1)} %shard_map.96), channel_id=1, source_target_pairs={{0,1},{4,0},{1,2},{5,4},{2,3},{6,5},{3,7},{7,6},{8,9},{12,8},{9,10... | collective-permute-start | bytes 786440 | tf_op jit(solution)/shard_map/line_14/ppermute | solution.py:208
  74.2 1.6 %collective-permute-start.24 = (f32[256,256]{1,0:T(8,128)S(1)}, f32[256,256]{1,0:T(8,128)S(1)}, u32[]{:S(2)}, u32[]{:S(2)}) collective-permute-start(f32[256,256]{1,0:T(8,128)S(1)} %shard_map.94), channel_id=1, source_target_pairs={{0,1},{4,0},{1,2},{5,4},{2,3},{6,5},{3,7},{7,6},{8,9},{12,8},{9,10... | collective-permute-start | bytes 786440 | tf_op jit(solution)/shard_map/line_15/ppermute | solution.py:208
  (59 shorter events, 20.3 us)
Async XLA Ops:
  10.2 9.8 %collective-permute-start.13 = (f32[4,128,256]{2,1,0:T(8,128)S(1)}, f32[4,128,256]{2,1,0:T(8,128)S(1)}, u32[]{:S(2)}, u32[]{:S(2)}) collective-permute-start(f32[4,128,256]{2,1,0:T(8,128)S(1)} %add.27), channel_id=1, source_target_pairs={{0,8},{4,20},{8,0},{12,28},{16,24},{20,4},{24,16},{28,12},{1,9},{5... | collective-permute-start | bytes 1572872 | tf_op jit(solution)/shard_map/users_0/ppermute | solution.py:213
  12.9 7.2 %collective-permute-start.3 = (f32[256,256]{1,0:T(8,128)S(1)}, f32[256,256]{1,0:T(8,128)S(1)}, u32[]{:S(2)}, u32[]{:S(2)}) collective-permute-start(f32[256,256]{1,0:T(8,128)S(1)} %shard_map.79), channel_id=1, source_target_pairs={{0,1},{4,0},{1,2},{5,4},{2,3},{6,5},{3,7},{7,6},{8,9},{12,8},{9,10... | collective-permute-start | bytes 786440 | tf_op jit(solution)/shard_map/line_1/ppermute | solution.py:208
  15.3 8.3 %collective-permute-start.2 = (f32[256,256]{1,0:T(8,128)S(1)}, f32[256,256]{1,0:T(8,128)S(1)}, u32[]{:S(2)}, u32[]{:S(2)}) collective-permute-start(f32[256,256]{1,0:T(8,128)S(1)} %shard_map.78), channel_id=1, source_target_pairs={{0,1},{4,0},{1,2},{5,4},{2,3},{6,5},{3,7},{7,6},{8,9},{12,8},{9,10... | collective-permute-start | bytes 786440 | tf_op jit(solution)/shard_map/line_0/ppermute | solution.py:208
  20.1 12.9 %collective-permute-start.14 = (f32[4,128,256]{2,1,0:T(8,128)S(1)}, f32[4,128,256]{2,1,0:T(8,128)S(1)}, u32[]{:S(2)}, u32[]{:S(2)}) collective-permute-start(f32[4,128,256]{2,1,0:T(8,128)S(1)} %add.28), channel_id=1, source_target_pairs={{0,16},{4,12},{8,24},{12,4},{16,0},{20,28},{24,8},{28,20},{1,17},{... | collective-permute-start | bytes 1572872 | tf_op jit(solution)/shard_map/users_1/ppermute | solution.py:213
  22.2 5.3 %collective-permute-start.5 = (f32[256,256]{1,0:T(8,128)S(1)}, f32[256,256]{1,0:T(8,128)S(1)}, u32[]{:S(2)}, u32[]{:S(2)}) collective-permute-start(f32[256,256]{1,0:T(8,128)S(1)} %shard_map.81), channel_id=1, source_target_pairs={{0,1},{4,0},{1,2},{5,4},{2,3},{6,5},{3,7},{7,6},{8,9},{12,8},{9,10... | collective-permute-start | bytes 786440 | tf_op jit(solution)/shard_map/line_3/ppermute | solution.py:208
  23.7 6.7 %collective-permute-start.4 = (f32[256,256]{1,0:T(8,128)S(1)}, f32[256,256]{1,0:T(8,128)S(1)}, u32[]{:S(2)}, u32[]{:S(2)}) collective-permute-start(f32[256,256]{1,0:T(8,128)S(1)} %shard_map.80), channel_id=1, source_target_pairs={{0,1},{4,0},{1,2},{5,4},{2,3},{6,5},{3,7},{7,6},{8,9},{12,8},{9,10... | collective-permute-start | bytes 786440 | tf_op jit(solution)/shard_map/line_2/ppermute | solution.py:208
  27.6 6.4 %collective-permute-start.7 = (f32[256,256]{1,0:T(8,128)S(1)}, f32[256,256]{1,0:T(8,128)S(1)}, u32[]{:S(2)}, u32[]{:S(2)}) collective-permute-start(f32[256,256]{1,0:T(8,128)S(1)} %shard_map.83), channel_id=1, source_target_pairs={{0,1},{4,0},{1,2},{5,4},{2,3},{6,5},{3,7},{7,6},{8,9},{12,8},{9,10... | collective-permute-start | bytes 786440 | tf_op jit(solution)/shard_map/line_5/ppermute | solution.py:208
  30.4 6.4 %collective-permute-start.6 = (f32[256,256]{1,0:T(8,128)S(1)}, f32[256,256]{1,0:T(8,128)S(1)}, u32[]{:S(2)}, u32[]{:S(2)}) collective-permute-start(f32[256,256]{1,0:T(8,128)S(1)} %shard_map.82), channel_id=1, source_target_pairs={{0,1},{4,0},{1,2},{5,4},{2,3},{6,5},{3,7},{7,6},{8,9},{12,8},{9,10... | collective-permute-start | bytes 786440 | tf_op jit(solution)/shard_map/line_4/ppermute | solution.py:208
  33.0 12.8 %collective-permute-start.15 = (f32[4,128,256]{2,1,0:T(8,128)S(1)}, f32[4,128,256]{2,1,0:T(8,128)S(1)}, u32[]{:S(2)}, u32[]{:S(2)}) collective-permute-start(f32[4,128,256]{2,1,0:T(8,128)S(1)} %add.29.mine_ref.users_ref), channel_id=1, source_target_pairs={{0,4},{4,0},{8,12},{12,8},{16,20},{20,16},{24,28},{28,24},{1,5},{5... | collective-permute-start | bytes 1572872 | tf_op jit(solution)/shard_map/ppermute | solution.py:213
  34.0 6.4 %collective-permute-start.9 = (f32[256,256]{1,0:T(8,128)S(1)}, f32[256,256]{1,0:T(8,128)S(1)}, u32[]{:S(2)}, u32[]{:S(2)}) collective-permute-start(f32[256,256]{1,0:T(8,128)S(1)} %shard_map.85), channel_id=1, source_target_pairs={{0,1},{4,0},{1,2},{5,4},{2,3},{6,5},{3,7},{7,6},{8,9},{12,8},{9,10... | collective-permute-start | bytes 786440 | tf_op jit(solution)/shard_map/line_7/ppermute | solution.py:208
  36.8 6.4 %collective-permute-start.8 = (f32[256,256]{1,0:T(8,128)S(1)}, f32[256,256]{1,0:T(8,128)S(1)}, u32[]{:S(2)}, u32[]{:S(2)}) collective-permute-start(f32[256,256]{1,0:T(8,128)S(1)} %shard_map.84), channel_id=1, source_target_pairs={{0,1},{4,0},{1,2},{5,4},{2,3},{6,5},{3,7},{7,6},{8,9},{12,8},{9,10... | collective-permute-start | bytes 786440 | tf_op jit(solution)/shard_map/line_6/ppermute | solution.py:208
  40.5 7.6 %collective-permute-start.11 = (f32[256,256]{1,0:T(8,128)S(1)}, f32[256,256]{1,0:T(8,128)S(1)}, u32[]{:S(2)}, u32[]{:S(2)}) collective-permute-start(f32[256,256]{1,0:T(8,128)S(1)} %shard_map.87), channel_id=1, source_target_pairs={{0,1},{4,0},{1,2},{5,4},{2,3},{6,5},{3,7},{7,6},{8,9},{12,8},{9,10... | collective-permute-start | bytes 786440 | tf_op jit(solution)/shard_map/line_9/ppermute | solution.py:208
  43.3 6.4 %collective-permute-start.10 = (f32[256,256]{1,0:T(8,128)S(1)}, f32[256,256]{1,0:T(8,128)S(1)}, u32[]{:S(2)}, u32[]{:S(2)}) collective-permute-start(f32[256,256]{1,0:T(8,128)S(1)} %shard_map.86), channel_id=1, source_target_pairs={{0,1},{4,0},{1,2},{5,4},{2,3},{6,5},{3,7},{7,6},{8,9},{12,8},{9,10... | collective-permute-start | bytes 786440 | tf_op jit(solution)/shard_map/line_8/ppermute | solution.py:208
  49.8 4.3 %collective-permute-start.12 = (f32[1024,256]{1,0:T(8,128)S(1)}, f32[1024,256]{1,0:T(8,128)S(1)}, u32[]{:S(2)}, u32[]{:S(2)}) collective-permute-start(f32[1024,256]{1,0:T(8,128)S(1)} %shard_map.88), channel_id=1, source_target_pairs={{0,4},{4,0},{8,12},{12,8},{16,20},{20,16},{24,28},{28,24},{1,5},{5... | collective-permute-start | bytes 3145736 | tf_op jit(solution)/shard_map/ppermute | solution.py:213
  50.7 5.6 %collective-permute-start.18 = (f32[256,256]{1,0:T(8,128)S(1)}, f32[256,256]{1,0:T(8,128)S(1)}, u32[]{:S(2)}, u32[]{:S(2)}) collective-permute-start(f32[256,256]{1,0:T(8,128)S(1)} %shard_map.91), channel_id=1, source_target_pairs={{0,1},{4,0},{1,2},{5,4},{2,3},{6,5},{3,7},{7,6},{8,9},{12,8},{9,10... | collective-permute-start | bytes 786440 | tf_op jit(solution)/shard_map/line_11/ppermute | solution.py:208
  52.5 6.7 %collective-permute-start.17 = (f32[256,256]{1,0:T(8,128)S(1)}, f32[256,256]{1,0:T(8,128)S(1)}, u32[]{:S(2)}, u32[]{:S(2)}) collective-permute-start(f32[256,256]{1,0:T(8,128)S(1)} %shard_map.90), channel_id=1, source_target_pairs={{0,1},{4,0},{1,2},{5,4},{2,3},{6,5},{3,7},{7,6},{8,9},{12,8},{9,10... | collective-permute-start | bytes 786440 | tf_op jit(solution)/shard_map/line_10/ppermute | solution.py:208
  61.3 9.2 %collective-permute-start.19 = (f32[4,128,256]{2,1,0:T(8,128)S(1)}, f32[4,128,256]{2,1,0:T(8,128)S(1)}, u32[]{:S(2)}, u32[]{:S(2)}) collective-permute-start(f32[4,128,256]{2,1,0:T(8,128)S(1)} %get-tuple-element.38), channel_id=1, source_target_pairs={{0,4},{4,0},{8,12},{12,8},{16,20},{20,16},{24,28},{28,24},{1,5},{5... | collective-permute-start | bytes 1572872 | tf_op jit(solution)/shard_map/ppermute | solution.py:213
  61.6 6.4 %collective-permute-start.25 = (f32[256,256]{1,0:T(8,128)S(1)}, f32[256,256]{1,0:T(8,128)S(1)}, u32[]{:S(2)}, u32[]{:S(2)}) collective-permute-start(f32[256,256]{1,0:T(8,128)S(1)} %shard_map.95), channel_id=1, source_target_pairs={{0,1},{4,0},{1,2},{5,4},{2,3},{6,5},{3,7},{7,6},{8,9},{12,8},{9,10... | collective-permute-start | bytes 786440 | tf_op jit(solution)/shard_map/line_12/ppermute | solution.py:208
  64.1 10.1 %collective-permute-start.23 = (f32[256,256]{1,0:T(8,128)S(1)}, f32[256,256]{1,0:T(8,128)S(1)}, u32[]{:S(2)}, u32[]{:S(2)}) collective-permute-start(f32[256,256]{1,0:T(8,128)S(1)} %shard_map.93), channel_id=1, source_target_pairs={{0,1},{4,0},{1,2},{5,4},{2,3},{6,5},{3,7},{7,6},{8,9},{12,8},{9,10... | collective-permute-start | bytes 786440 | tf_op jit(solution)/shard_map/line_13/ppermute | solution.py:208
  68.0 7.8 %collective-permute-start.26 = (f32[256,256]{1,0:T(8,128)S(1)}, f32[256,256]{1,0:T(8,128)S(1)}, u32[]{:S(2)}, u32[]{:S(2)}) collective-permute-start(f32[256,256]{1,0:T(8,128)S(1)} %shard_map.96), channel_id=1, source_target_pairs={{0,1},{4,0},{1,2},{5,4},{2,3},{6,5},{3,7},{7,6},{8,9},{12,8},{9,10... | collective-permute-start | bytes 786440 | tf_op jit(solution)/shard_map/line_14/ppermute | solution.py:208
  70.6 6.0 %collective-permute-start.20 = (f32[128,256]{1,0:T(8,128)S(1)}, f32[128,256]{1,0:T(8,128)S(1)}, u32[]{:S(2)}, u32[]{:S(2)}) collective-permute-start(f32[128,256]{1,0:T(8,128)S(1)} %get-tuple-element.40), channel_id=1, source_target_pairs={{0,24},{4,28},{8,16},{12,20},{16,8},{20,12},{24,0},{28,4},{1,25},{... | collective-permute-start | bytes 393224 | tf_op jit(solution)/shard_map/ppermute | solution.py:213
  72.1 5.8 %collective-permute-start.21 = (f32[128,256]{1,0:T(8,128)S(1)}, f32[128,256]{1,0:T(8,128)S(1)}, u32[]{:S(2)}, u32[]{:S(2)}) collective-permute-start(f32[128,256]{1,0:T(8,128)S(1)} %get-tuple-element.42), channel_id=1, source_target_pairs={{0,16},{4,20},{8,24},{12,28},{16,0},{20,4},{24,8},{28,12},{1,17},{... | collective-permute-start | bytes 393224 | tf_op jit(solution)/shard_map/ppermute | solution.py:213
  73.6 5.0 %collective-permute-start.22 = (f32[128,256]{1,0:T(8,128)S(1)}, f32[128,256]{1,0:T(8,128)S(1)}, u32[]{:S(2)}, u32[]{:S(2)}) collective-permute-start(f32[128,256]{1,0:T(8,128)S(1)} %get-tuple-element.41), channel_id=1, source_target_pairs={{0,8},{4,12},{8,0},{12,4},{16,24},{20,28},{24,16},{28,20},{1,9},{5... | collective-permute-start | bytes 393224 | tf_op jit(solution)/shard_map/ppermute | solution.py:213
  74.2 5.5 %collective-permute-start.24 = (f32[256,256]{1,0:T(8,128)S(1)}, f32[256,256]{1,0:T(8,128)S(1)}, u32[]{:S(2)}, u32[]{:S(2)}) collective-permute-start(f32[256,256]{1,0:T(8,128)S(1)} %shard_map.94), channel_id=1, source_target_pairs={{0,1},{4,0},{1,2},{5,4},{2,3},{6,5},{3,7},{7,6},{8,9},{12,8},{9,10... | collective-permute-start | bytes 786440 | tf_op jit(solution)/shard_map/line_15/ppermute | solution.py:208
  (4 other events, 11.9 us)

commit v5 on v4

--- a/solution.py
+++ b/solution.py
@@ -57,8 +57,8 @@
 
 
 def first_kernel(count_ref, rows_hbm, cols_hbm, tiles_hbm, users_hbm, items_hbm, *rest):
-    high_ref, low_ref, sums_ref, mine_ref, other_ref = rest[:5]
-    whole_ref, full_ref, tiles_ref, users_ref, items_ref, rows_ref, cols_ref, sems = rest[5:]
+    high_ref, low_ref, users_ref, mine_ref, other_ref = rest[:5]
+    whole_ref, full_ref, tiles_ref, items_ref, rows_ref, cols_ref, sems = rest[5:]
     index_copies = [
         pltpu.make_async_copy(source, target, sems.at[COPIES + 2 + k])
         for k, (source, target) in enumerate(((rows_hbm, rows_ref), (cols_hbm, cols_ref)))
@@ -86,11 +86,14 @@
 
     for here in blocks_of(whole_ref.shape[0]):
         high_ref[here, :], low_ref[here, :] = halves(whole_ref[here, :])
-    users_copy.wait()
-    item_product(high_ref, low_ref, users_ref[...] * THIRD, sums_ref)
     items_copy.wait()
     user_product(high_ref, low_ref, halves(items_ref[...] * THIRD), full_ref)
     user_blocks(full_ref, mine_ref, other_ref, 0)
+    users_copy.wait()
+
+
+def sums_kernel(high_ref, low_ref, users_ref, sums_ref):
+    item_product(high_ref, low_ref, users_ref[...] * THIRD, sums_ref)
 
 
 def items_kernel(high_ref, low_ref, mine_ref, other_ref, sums_ref, users_ref):
@@ -237,18 +240,19 @@
 
     arguments = (tile_rows, tile_cols, tile_vals, user_cot, item_cot)
     pinned = [pltpu.with_memory_space_constraint(array, pltpu.HBM) for array in arguments]
-    high, low, sums, mine, other = call(
+    high, low, held, mine, other = call(
         first_kernel,
-        [b16(n_user, n_item), b16(n_user, n_item), items] + blocks,
+        [b16(n_user, n_item), b16(n_user, n_item), f32(n_user, feature)] + blocks,
         (tile_count, *pinned),
         [space(n_user, n_item), space(n_user, feature), space(*tile_vals.shape[2:])]
-        + [space(n_user, feature), space(n_item, feature)]
+        + [space(n_item, feature)]
         + [pltpu.SMEM(array.shape, jnp.int32) for array in arguments[:2]]
         + [pltpu.SemaphoreType.DMA((COPIES + 4,))],
         [pltpu.SMEM] + [pltpu.HBM] * 5,
         **cost,
     )
 
+    (sums,) = call(sums_kernel, [items], (high, low, held), **cost)
     users = mine + swap(other)
     sources = [swap(after(sums, users)), sums]
     rounds = (chips - 1).bit_length()

time: 80.6 us -> 79.2 us (0.983)
  waiting for transfers between devices: 22.6 us -> 21.1 us
    ppermute x12, waiting for transfers between devices: 8.2 us -> 6.74 us  [across_panel(): lax.ppermute(values, 'panel', [(i, i ^ bits[i & 1]) for i in range(count)])]
    pallas_call x20 -> x21, Pallas kernels: 10.9 us -> 11 us  [call(): pl.pallas_call(kernel, out_shape=out_shape, in_specs=[pl.BlockSpec(memory...]
  transfers between devices with their start and end apart: 28 -> 28, of which waited for: 17 -> 16; matrix products, arithmetic and copies ran while one was open for 1% -> 1% of each run, Pallas kernels for 3% -> 6%
where the time goes in v5:
time: 79.2 us; the launch traced here: 79 us
  starting transfers between devices  43.7 us (55%)
  waiting for transfers between devices  21.1 us (27%)
  Pallas kernels  11 us (14%)
  other arithmetic  1.72 us (2%)
  between operations  1.52 us (2%)
    ppermute x16, starting transfers between devices, along_line(): return lax.ppermute(values, ('panel', 'rep'), pairs)  34 us
    ppermute x16, waiting for transfers between devices, along_line(): return lax.ppermute(values, ('panel', 'rep'), pairs)  14.4 us
    pallas_call x21, Pallas kernels, call(): pl.pallas_call(kernel, out_shape=out_shape, in_specs=[pl.BlockSpec(memory...  11 us
    ppermute x12, starting transfers between devices, across_panel(): lax.ppermute(values, 'panel', [(i, i ^ bits[i & 1]) for i in range(count)])  9.7 us
    ppermute x12, waiting for transfers between devices, across_panel(): lax.ppermute(values, 'panel', [(i, i ^ bits[i & 1]) for i in range(count)])  6.74 us
  transfers between devices with their start and end apart: 28, of which 16 were waited for; matrix products, arithmetic and copies ran while one was open for 1% of the time, Pallas kernels for 6%

profile of v5, /device:TPU:0, one launch (start us, length us, event | category | flops | bytes accessed | tf_op | source)
XLA Modules:
  0.0 79.0 jit_solution(4569002893585558595)
XLA Ops:
  1.3 4.3 %shard_map.77 = (bf16[1024,1024]{1,0:T(8,128)(2,1)S(1)}, bf16[1024,1024]{1,0:T(8,128)(2,1)S(1)}, f32[1024,256]{1,0:T(8,128)S(1)}, f32[4,128,256]{2,1,0:T(8,128)S(1)}, f32[4,128,256]{2,1,0:T(8,128)S(1)}) custom-call(s32[1,1]{1,0:T(1,128)S(6)} %copy.8.count_ref, s32[1,1,40]{2,1,0:T(1,128)} %rows_hbm.1, s32[1,1,40]{2,1,0:T(1,128)} %cols_hbm.1, ...), custom_call_target="tpu_custom_call" | custom-call | flops 1610612736 | bytes 6291456 | tf_op jit(solution)/shard_map/pallas_call | solution.py:192
  6.2 2.0 %shard_map.78.refs_2_.sums_ref = f32[1024,256]{1,0:T(8,128)S(1)} custom-call(bf16[1024,1024]{1,0:T(8,128)(2,1)S(1)} %get-tuple-element.21.high_ref, bf16[1024,1024]{1,0:T(8,128)(2,1)S(1)} %get-tuple-element.22.low_ref, f32[1024,256]{1,0:T(8,128)S(1)} %get-tuple-element.23.users_ref), custom_call_target="tpu_custom_call" | custom-call | flops 1610612736 | bytes 6291456 | tf_op jit(solution)/shard_map/pallas_call | solution.py:192
  8.3 2.9 %collective-permute-start.13 = (f32[4,128,256]{2,1,0:T(8,128)S(1)}, f32[4,128,256]{2,1,0:T(8,128)S(1)}, u32[]{:S(2)}, u32[]{:S(2)}) collective-permute-start(f32[4,128,256]{2,1,0:T(8,128)S(1)} %add.27), channel_id=1, source_target_pairs={{0,8},{4,20},{8,0},{12,28},{16,24},{20,4},{24,16},{28,12},{1,9},{5... | collective-permute-start | bytes 1572872 | tf_op jit(solution)/shard_map/users_0/ppermute | solution.py:216
  11.3 2.4 %collective-permute-start.3 = (f32[256,256]{1,0:T(8,128)S(1)}, f32[256,256]{1,0:T(8,128)S(1)}, u32[]{:S(2)}, u32[]{:S(2)}) collective-permute-start(f32[256,256]{1,0:T(8,128)S(1)} %shard_map.80), channel_id=1, source_target_pairs={{0,1},{4,0},{1,2},{5,4},{2,3},{6,5},{3,7},{7,6},{8,9},{12,8},{9,10... | collective-permute-start | bytes 786440 | tf_op jit(solution)/shard_map/line_1/ppermute | solution.py:211
  15.3 3.1 %collective-permute-done.13 = f32[4,128,256]{2,1,0:T(8,128)S(1)} collective-permute-done((f32[4,128,256]{2,1,0:T(8,128)S(1)}, f32[4,128,256]{2,1,0:T(8,128)S(1)}, u32[]{:S(2)}, u32[]{:S(2)}) %collective-permute-start.13) | collective-permute-done | bytes 524320 | tf_op jit(solution)/shard_map/users_0/ppermute | solution.py:216
  18.5 2.1 %collective-permute-start.14 = (f32[4,128,256]{2,1,0:T(8,128)S(1)}, f32[4,128,256]{2,1,0:T(8,128)S(1)}, u32[]{:S(2)}, u32[]{:S(2)}) collective-permute-start(f32[4,128,256]{2,1,0:T(8,128)S(1)} %add.28), channel_id=1, source_target_pairs={{0,16},{4,12},{8,24},{12,4},{16,0},{20,28},{24,8},{28,20},{1,17},{... | collective-permute-start | bytes 1572872 | tf_op jit(solution)/shard_map/users_1/ppermute | solution.py:216
  20.6 1.6 %collective-permute-start.5 = (f32[256,256]{1,0:T(8,128)S(1)}, f32[256,256]{1,0:T(8,128)S(1)}, u32[]{:S(2)}, u32[]{:S(2)}) collective-permute-start(f32[256,256]{1,0:T(8,128)S(1)} %shard_map.82), channel_id=1, source_target_pairs={{0,1},{4,0},{1,2},{5,4},{2,3},{6,5},{3,7},{7,6},{8,9},{12,8},{9,10... | collective-permute-start | bytes 786440 | tf_op jit(solution)/shard_map/line_3/ppermute | solution.py:211
  22.3 1.6 %collective-permute-start.4 = (f32[256,256]{1,0:T(8,128)S(1)}, f32[256,256]{1,0:T(8,128)S(1)}, u32[]{:S(2)}, u32[]{:S(2)}) collective-permute-start(f32[256,256]{1,0:T(8,128)S(1)} %shard_map.81), channel_id=1, source_target_pairs={{0,1},{4,0},{1,2},{5,4},{2,3},{6,5},{3,7},{7,6},{8,9},{12,8},{9,10... | collective-permute-start | bytes 786440 | tf_op jit(solution)/shard_map/line_2/ppermute | solution.py:211
  23.9 2.2 %collective-permute-done.5.refs_0_.refs_3_ = f32[256,256]{1,0:T(8,128)S(1)} collective-permute-done((f32[256,256]{1,0:T(8,128)S(1)}, f32[256,256]{1,0:T(8,128)S(1)}, u32[]{:S(2)}, u32[]{:S(2)}) %collective-permute-start.5) | collective-permute-done | bytes 262176 | tf_op jit(solution)/shard_map/line_3/ppermute | solution.py:211
  26.2 2.5 %collective-permute-start.7 = (f32[256,256]{1,0:T(8,128)S(1)}, f32[256,256]{1,0:T(8,128)S(1)}, u32[]{:S(2)}, u32[]{:S(2)}) collective-permute-start(f32[256,256]{1,0:T(8,128)S(1)} %shard_map.84), channel_id=1, source_target_pairs={{0,1},{4,0},{1,2},{5,4},{2,3},{6,5},{3,7},{7,6},{8,9},{12,8},{9,10... | collective-permute-start | bytes 786440 | tf_op jit(solution)/shard_map/line_5/ppermute | solution.py:211
  29.0 2.5 %collective-permute-start.6 = (f32[256,256]{1,0:T(8,128)S(1)}, f32[256,256]{1,0:T(8,128)S(1)}, u32[]{:S(2)}, u32[]{:S(2)}) collective-permute-start(f32[256,256]{1,0:T(8,128)S(1)} %shard_map.83), channel_id=1, source_target_pairs={{0,1},{4,0},{1,2},{5,4},{2,3},{6,5},{3,7},{7,6},{8,9},{12,8},{9,10... | collective-permute-start | bytes 786440 | tf_op jit(solution)/shard_map/line_4/ppermute | solution.py:211
  32.6 2.5 %collective-permute-start.9 = (f32[256,256]{1,0:T(8,128)S(1)}, f32[256,256]{1,0:T(8,128)S(1)}, u32[]{:S(2)}, u32[]{:S(2)}) collective-permute-start(f32[256,256]{1,0:T(8,128)S(1)} %shard_map.86), channel_id=1, source_target_pairs={{0,1},{4,0},{1,2},{5,4},{2,3},{6,5},{3,7},{7,6},{8,9},{12,8},{9,10... | collective-permute-start | bytes 786440 | tf_op jit(solution)/shard_map/line_7/ppermute | solution.py:211
  35.4 2.5 %collective-permute-start.8 = (f32[256,256]{1,0:T(8,128)S(1)}, f32[256,256]{1,0:T(8,128)S(1)}, u32[]{:S(2)}, u32[]{:S(2)}) collective-permute-start(f32[256,256]{1,0:T(8,128)S(1)} %shard_map.85), channel_id=1, source_target_pairs={{0,1},{4,0},{1,2},{5,4},{2,3},{6,5},{3,7},{7,6},{8,9},{12,8},{9,10... | collective-permute-start | bytes 786440 | tf_op jit(solution)/shard_map/line_6/ppermute | solution.py:211
  39.0 2.5 %collective-permute-start.11 = (f32[256,256]{1,0:T(8,128)S(1)}, f32[256,256]{1,0:T(8,128)S(1)}, u32[]{:S(2)}, u32[]{:S(2)}) collective-permute-start(f32[256,256]{1,0:T(8,128)S(1)} %shard_map.88), channel_id=1, source_target_pairs={{0,1},{4,0},{1,2},{5,4},{2,3},{6,5},{3,7},{7,6},{8,9},{12,8},{9,10... | collective-permute-start | bytes 786440 | tf_op jit(solution)/shard_map/line_9/ppermute | solution.py:211
  41.8 2.5 %collective-permute-start.10 = (f32[256,256]{1,0:T(8,128)S(1)}, f32[256,256]{1,0:T(8,128)S(1)}, u32[]{:S(2)}, u32[]{:S(2)}) collective-permute-start(f32[256,256]{1,0:T(8,128)S(1)} %shard_map.87), channel_id=1, source_target_pairs={{0,1},{4,0},{1,2},{5,4},{2,3},{6,5},{3,7},{7,6},{8,9},{12,8},{9,10... | collective-permute-start | bytes 786440 | tf_op jit(solution)/shard_map/line_8/ppermute | solution.py:211
  44.4 2.2 %shard_map.90.refs_4_.again_ref = f32[1024,256]{1,0:T(8,128)S(1)} custom-call(bf16[1024,1024]{1,0:T(8,128)(2,1)S(1)} %get-tuple-element.21.high_ref, bf16[1024,1024]{1,0:T(8,128)(2,1)S(1)} %get-tuple-element.22.low_ref, f32[4,128,256]{2,1,0:T(8,128)S(1)} %add.29.mine_ref.users_ref, f32[4,128,256]{2,1,0:T(8,128)S(1)} %collective-permute-done.15.other_ref), custom_call_target="tpu_custom_call" | custom-call | flops 1610612736 | bytes 6291456 | tf_op jit(solution)/shard_map/pallas_call | solution.py:192
  46.7 1.6 %collective-permute-done.10.refs_0_.rest_4_ = f32[256,256]{1,0:T(8,128)S(1)} collective-permute-done((f32[256,256]{1,0:T(8,128)S(1)}, f32[256,256]{1,0:T(8,128)S(1)}, u32[]{:S(2)}, u32[]{:S(2)}) %collective-permute-start.10) | collective-permute-done | bytes 262176 | tf_op jit(solution)/shard_map/line_8/ppermute | solution.py:211
  49.3 1.7 %collective-permute-start.18 = (f32[256,256]{1,0:T(8,128)S(1)}, f32[256,256]{1,0:T(8,128)S(1)}, u32[]{:S(2)}, u32[]{:S(2)}) collective-permute-start(f32[256,256]{1,0:T(8,128)S(1)} %shard_map.92), channel_id=1, source_target_pairs={{0,1},{4,0},{1,2},{5,4},{2,3},{6,5},{3,7},{7,6},{8,9},{12,8},{9,10... | collective-permute-start | bytes 786440 | tf_op jit(solution)/shard_map/line_11/ppermute | solution.py:211
  52.7 2.3 %collective-permute-done.18.rest_7_.refs_0_ = f32[256,256]{1,0:T(8,128)S(1)} collective-permute-done((f32[256,256]{1,0:T(8,128)S(1)}, f32[256,256]{1,0:T(8,128)S(1)}, u32[]{:S(2)}, u32[]{:S(2)}) %collective-permute-start.18) | collective-permute-done | bytes 262176 | tf_op jit(solution)/shard_map/line_11/ppermute | solution.py:211
  55.0 2.8 %collective-permute-done.17.rest_6_.refs_0_ = f32[256,256]{1,0:T(8,128)S(1)} collective-permute-done((f32[256,256]{1,0:T(8,128)S(1)}, f32[256,256]{1,0:T(8,128)S(1)}, u32[]{:S(2)}, u32[]{:S(2)}) %collective-permute-start.17) | collective-permute-done | bytes 262176 | tf_op jit(solution)/shard_map/line_10/ppermute | solution.py:211
  57.8 2.1 %shard_map.93 = (f32[4,128,256]{2,1,0:T(8,128)S(1)}, f32[4,128,256]{2,1,0:T(8,128)S(1)}, f32[256,256]{1,0:T(8,128)S(1)}) custom-call(f32[1024,256]{1,0:T(8,128)} %user_cot_hbm.1, f32[1024,256]{1,0:T(8,128)} %item_cot_hbm.1, bf16[1024,1024]{1,0:T(8,128)(2,1)S(1)} %get-tuple-element.21.high_ref, bf16[1024,1024]{1,0:T(8,128)(2,1)S(1)} %get-tuple-element.22.low_ref, ...), custom_call_target="tpu_custom_call" | custom-call | flops 1610612736 | bytes 6291456 | tf_op jit(solution)/shard_map/pallas_call | solution.py:192
  60.1 2.5 %collective-permute-start.25 = (f32[256,256]{1,0:T(8,128)S(1)}, f32[256,256]{1,0:T(8,128)S(1)}, u32[]{:S(2)}, u32[]{:S(2)}) collective-permute-start(f32[256,256]{1,0:T(8,128)S(1)} %shard_map.96), channel_id=1, source_target_pairs={{0,1},{4,0},{1,2},{5,4},{2,3},{6,5},{3,7},{7,6},{8,9},{12,8},{9,10... | collective-permute-start | bytes 786440 | tf_op jit(solution)/shard_map/line_12/ppermute | solution.py:211
  64.3 2.3 %collective-permute-done.25.refs_0_ = f32[256,256]{1,0:T(8,128)S(1)} collective-permute-done((f32[256,256]{1,0:T(8,128)S(1)}, f32[256,256]{1,0:T(8,128)S(1)}, u32[]{:S(2)}, u32[]{:S(2)}) %collective-permute-start.25) | collective-permute-done | bytes 262176 | tf_op jit(solution)/shard_map/line_12/ppermute | solution.py:211
  66.6 2.5 %collective-permute-start.26 = (f32[256,256]{1,0:T(8,128)S(1)}, f32[256,256]{1,0:T(8,128)S(1)}, u32[]{:S(2)}, u32[]{:S(2)}) collective-permute-start(f32[256,256]{1,0:T(8,128)S(1)} %shard_map.97), channel_id=1, source_target_pairs={{0,1},{4,0},{1,2},{5,4},{2,3},{6,5},{3,7},{7,6},{8,9},{12,8},{9,10... | collective-permute-start | bytes 786440 | tf_op jit(solution)/shard_map/line_14/ppermute | solution.py:211
  (60 shorter events, 20.0 us)
Async XLA Ops:
  8.3 10.1 %collective-permute-start.13 = (f32[4,128,256]{2,1,0:T(8,128)S(1)}, f32[4,128,256]{2,1,0:T(8,128)S(1)}, u32[]{:S(2)}, u32[]{:S(2)}) collective-permute-start(f32[4,128,256]{2,1,0:T(8,128)S(1)} %add.27), channel_id=1, source_target_pairs={{0,8},{4,20},{8,0},{12,28},{16,24},{20,4},{24,16},{28,12},{1,9},{5... | collective-permute-start | bytes 1572872 | tf_op jit(solution)/shard_map/users_0/ppermute | solution.py:216
  11.3 7.2 %collective-permute-start.3 = (f32[256,256]{1,0:T(8,128)S(1)}, f32[256,256]{1,0:T(8,128)S(1)}, u32[]{:S(2)}, u32[]{:S(2)}) collective-permute-start(f32[256,256]{1,0:T(8,128)S(1)} %shard_map.80), channel_id=1, source_target_pairs={{0,1},{4,0},{1,2},{5,4},{2,3},{6,5},{3,7},{7,6},{8,9},{12,8},{9,10... | collective-permute-start | bytes 786440 | tf_op jit(solution)/shard_map/line_1/ppermute | solution.py:211
  13.7 8.6 %collective-permute-start.2 = (f32[256,256]{1,0:T(8,128)S(1)}, f32[256,256]{1,0:T(8,128)S(1)}, u32[]{:S(2)}, u32[]{:S(2)}) collective-permute-start(f32[256,256]{1,0:T(8,128)S(1)} %shard_map.79), channel_id=1, source_target_pairs={{0,1},{4,0},{1,2},{5,4},{2,3},{6,5},{3,7},{7,6},{8,9},{12,8},{9,10... | collective-permute-start | bytes 786440 | tf_op jit(solution)/shard_map/line_0/ppermute | solution.py:211
  18.5 13.0 %collective-permute-start.14 = (f32[4,128,256]{2,1,0:T(8,128)S(1)}, f32[4,128,256]{2,1,0:T(8,128)S(1)}, u32[]{:S(2)}, u32[]{:S(2)}) collective-permute-start(f32[4,128,256]{2,1,0:T(8,128)S(1)} %add.28), channel_id=1, source_target_pairs={{0,16},{4,12},{8,24},{12,4},{16,0},{20,28},{24,8},{28,20},{1,17},{... | collective-permute-start | bytes 1572872 | tf_op jit(solution)/shard_map/users_1/ppermute | solution.py:216
  20.6 5.5 %collective-permute-start.5 = (f32[256,256]{1,0:T(8,128)S(1)}, f32[256,256]{1,0:T(8,128)S(1)}, u32[]{:S(2)}, u32[]{:S(2)}) collective-permute-start(f32[256,256]{1,0:T(8,128)S(1)} %shard_map.82), channel_id=1, source_target_pairs={{0,1},{4,0},{1,2},{5,4},{2,3},{6,5},{3,7},{7,6},{8,9},{12,8},{9,10... | collective-permute-start | bytes 786440 | tf_op jit(solution)/shard_map/line_3/ppermute | solution.py:211
  22.3 6.7 %collective-permute-start.4 = (f32[256,256]{1,0:T(8,128)S(1)}, f32[256,256]{1,0:T(8,128)S(1)}, u32[]{:S(2)}, u32[]{:S(2)}) collective-permute-start(f32[256,256]{1,0:T(8,128)S(1)} %shard_map.81), channel_id=1, source_target_pairs={{0,1},{4,0},{1,2},{5,4},{2,3},{6,5},{3,7},{7,6},{8,9},{12,8},{9,10... | collective-permute-start | bytes 786440 | tf_op jit(solution)/shard_map/line_2/ppermute | solution.py:211
  26.2 6.4 %collective-permute-start.7 = (f32[256,256]{1,0:T(8,128)S(1)}, f32[256,256]{1,0:T(8,128)S(1)}, u32[]{:S(2)}, u32[]{:S(2)}) collective-permute-start(f32[256,256]{1,0:T(8,128)S(1)} %shard_map.84), channel_id=1, source_target_pairs={{0,1},{4,0},{1,2},{5,4},{2,3},{6,5},{3,7},{7,6},{8,9},{12,8},{9,10... | collective-permute-start | bytes 786440 | tf_op jit(solution)/shard_map/line_5/ppermute | solution.py:211
  29.0 6.4 %collective-permute-start.6 = (f32[256,256]{1,0:T(8,128)S(1)}, f32[256,256]{1,0:T(8,128)S(1)}, u32[]{:S(2)}, u32[]{:S(2)}) collective-permute-start(f32[256,256]{1,0:T(8,128)S(1)} %shard_map.83), channel_id=1, source_target_pairs={{0,1},{4,0},{1,2},{5,4},{2,3},{6,5},{3,7},{7,6},{8,9},{12,8},{9,10... | collective-permute-start | bytes 786440 | tf_op jit(solution)/shard_map/line_4/ppermute | solution.py:211
  31.6 12.8 %collective-permute-start.15 = (f32[4,128,256]{2,1,0:T(8,128)S(1)}, f32[4,128,256]{2,1,0:T(8,128)S(1)}, u32[]{:S(2)}, u32[]{:S(2)}) collective-permute-start(f32[4,128,256]{2,1,0:T(8,128)S(1)} %add.29.mine_ref.users_ref), channel_id=1, source_target_pairs={{0,4},{4,0},{8,12},{12,8},{16,20},{20,16},{24,28},{28,24},{1,5},{5... | collective-permute-start | bytes 1572872 | tf_op jit(solution)/shard_map/ppermute | solution.py:216
  32.6 6.4 %collective-permute-start.9 = (f32[256,256]{1,0:T(8,128)S(1)}, f32[256,256]{1,0:T(8,128)S(1)}, u32[]{:S(2)}, u32[]{:S(2)}) collective-permute-start(f32[256,256]{1,0:T(8,128)S(1)} %shard_map.86), channel_id=1, source_target_pairs={{0,1},{4,0},{1,2},{5,4},{2,3},{6,5},{3,7},{7,6},{8,9},{12,8},{9,10... | collective-permute-start | bytes 786440 | tf_op jit(solution)/shard_map/line_7/ppermute | solution.py:211
  35.4 6.4 %collective-permute-start.8 = (f32[256,256]{1,0:T(8,128)S(1)}, f32[256,256]{1,0:T(8,128)S(1)}, u32[]{:S(2)}, u32[]{:S(2)}) collective-permute-start(f32[256,256]{1,0:T(8,128)S(1)} %shard_map.85), channel_id=1, source_target_pairs={{0,1},{4,0},{1,2},{5,4},{2,3},{6,5},{3,7},{7,6},{8,9},{12,8},{9,10... | collective-permute-start | bytes 786440 | tf_op jit(solution)/shard_map/line_6/ppermute | solution.py:211
  39.0 7.6 %collective-permute-start.11 = (f32[256,256]{1,0:T(8,128)S(1)}, f32[256,256]{1,0:T(8,128)S(1)}, u32[]{:S(2)}, u32[]{:S(2)}) collective-permute-start(f32[256,256]{1,0:T(8,128)S(1)} %shard_map.88), channel_id=1, source_target_pairs={{0,1},{4,0},{1,2},{5,4},{2,3},{6,5},{3,7},{7,6},{8,9},{12,8},{9,10... | collective-permute-start | bytes 786440 | tf_op jit(solution)/shard_map/line_9/ppermute | solution.py:211
  41.8 6.4 %collective-permute-start.10 = (f32[256,256]{1,0:T(8,128)S(1)}, f32[256,256]{1,0:T(8,128)S(1)}, u32[]{:S(2)}, u32[]{:S(2)}) collective-permute-start(f32[256,256]{1,0:T(8,128)S(1)} %shard_map.87), channel_id=1, source_target_pairs={{0,1},{4,0},{1,2},{5,4},{2,3},{6,5},{3,7},{7,6},{8,9},{12,8},{9,10... | collective-permute-start | bytes 786440 | tf_op jit(solution)/shard_map/line_8/ppermute | solution.py:211
  48.4 4.3 %collective-permute-start.12 = (f32[1024,256]{1,0:T(8,128)S(1)}, f32[1024,256]{1,0:T(8,128)S(1)}, u32[]{:S(2)}, u32[]{:S(2)}) collective-permute-start(f32[1024,256]{1,0:T(8,128)S(1)} %shard_map.89), channel_id=1, source_target_pairs={{0,4},{4,0},{8,12},{12,8},{16,20},{20,16},{24,28},{28,24},{1,5},{5... | collective-permute-start | bytes 3145736 | tf_op jit(solution)/shard_map/ppermute | solution.py:216
  49.3 5.6 %collective-permute-start.18 = (f32[256,256]{1,0:T(8,128)S(1)}, f32[256,256]{1,0:T(8,128)S(1)}, u32[]{:S(2)}, u32[]{:S(2)}) collective-permute-start(f32[256,256]{1,0:T(8,128)S(1)} %shard_map.92), channel_id=1, source_target_pairs={{0,1},{4,0},{1,2},{5,4},{2,3},{6,5},{3,7},{7,6},{8,9},{12,8},{9,10... | collective-permute-start | bytes 786440 | tf_op jit(solution)/shard_map/line_11/ppermute | solution.py:211
  51.1 6.7 %collective-permute-start.17 = (f32[256,256]{1,0:T(8,128)S(1)}, f32[256,256]{1,0:T(8,128)S(1)}, u32[]{:S(2)}, u32[]{:S(2)}) collective-permute-start(f32[256,256]{1,0:T(8,128)S(1)} %shard_map.91), channel_id=1, source_target_pairs={{0,1},{4,0},{1,2},{5,4},{2,3},{6,5},{3,7},{7,6},{8,9},{12,8},{9,10... | collective-permute-start | bytes 786440 | tf_op jit(solution)/shard_map/line_10/ppermute | solution.py:211
  59.9 9.2 %collective-permute-start.19 = (f32[4,128,256]{2,1,0:T(8,128)S(1)}, f32[4,128,256]{2,1,0:T(8,128)S(1)}, u32[]{:S(2)}, u32[]{:S(2)}) collective-permute-start(f32[4,128,256]{2,1,0:T(8,128)S(1)} %get-tuple-element.38), channel_id=1, source_target_pairs={{0,4},{4,0},{8,12},{12,8},{16,20},{20,16},{24,28},{28,24},{1,5},{5... | collective-permute-start | bytes 1572872 | tf_op jit(solution)/shard_map/ppermute | solution.py:216
  60.1 6.4 %collective-permute-start.25 = (f32[256,256]{1,0:T(8,128)S(1)}, f32[256,256]{1,0:T(8,128)S(1)}, u32[]{:S(2)}, u32[]{:S(2)}) collective-permute-start(f32[256,256]{1,0:T(8,128)S(1)} %shard_map.96), channel_id=1, source_target_pairs={{0,1},{4,0},{1,2},{5,4},{2,3},{6,5},{3,7},{7,6},{8,9},{12,8},{9,10... | collective-permute-start | bytes 786440 | tf_op jit(solution)/shard_map/line_12/ppermute | solution.py:211
  62.7 10.1 %collective-permute-start.23 = (f32[256,256]{1,0:T(8,128)S(1)}, f32[256,256]{1,0:T(8,128)S(1)}, u32[]{:S(2)}, u32[]{:S(2)}) collective-permute-start(f32[256,256]{1,0:T(8,128)S(1)} %shard_map.94), channel_id=1, source_target_pairs={{0,1},{4,0},{1,2},{5,4},{2,3},{6,5},{3,7},{7,6},{8,9},{12,8},{9,10... | collective-permute-start | bytes 786440 | tf_op jit(solution)/shard_map/line_13/ppermute | solution.py:211
  66.6 7.8 %collective-permute-start.26 = (f32[256,256]{1,0:T(8,128)S(1)}, f32[256,256]{1,0:T(8,128)S(1)}, u32[]{:S(2)}, u32[]{:S(2)}) collective-permute-start(f32[256,256]{1,0:T(8,128)S(1)} %shard_map.97), channel_id=1, source_target_pairs={{0,1},{4,0},{1,2},{5,4},{2,3},{6,5},{3,7},{7,6},{8,9},{12,8},{9,10... | collective-permute-start | bytes 786440 | tf_op jit(solution)/shard_map/line_14/ppermute | solution.py:211
  69.2 6.0 %collective-permute-start.20 = (f32[128,256]{1,0:T(8,128)S(1)}, f32[128,256]{1,0:T(8,128)S(1)}, u32[]{:S(2)}, u32[]{:S(2)}) collective-permute-start(f32[128,256]{1,0:T(8,128)S(1)} %get-tuple-element.40), channel_id=1, source_target_pairs={{0,24},{4,28},{8,16},{12,20},{16,8},{20,12},{24,0},{28,4},{1,25},{... | collective-permute-start | bytes 393224 | tf_op jit(solution)/shard_map/ppermute | solution.py:216
  70.7 5.8 %collective-permute-start.21 = (f32[128,256]{1,0:T(8,128)S(1)}, f32[128,256]{1,0:T(8,128)S(1)}, u32[]{:S(2)}, u32[]{:S(2)}) collective-permute-start(f32[128,256]{1,0:T(8,128)S(1)} %get-tuple-element.42), channel_id=1, source_target_pairs={{0,16},{4,20},{8,24},{12,28},{16,0},{20,4},{24,8},{28,12},{1,17},{... | collective-permute-start | bytes 393224 | tf_op jit(solution)/shard_map/ppermute | solution.py:216
  72.2 5.0 %collective-permute-start.22 = (f32[128,256]{1,0:T(8,128)S(1)}, f32[128,256]{1,0:T(8,128)S(1)}, u32[]{:S(2)}, u32[]{:S(2)}) collective-permute-start(f32[128,256]{1,0:T(8,128)S(1)} %get-tuple-element.41), channel_id=1, source_target_pairs={{0,8},{4,12},{8,0},{12,4},{16,24},{20,28},{24,16},{28,20},{1,9},{5... | collective-permute-start | bytes 393224 | tf_op jit(solution)/shard_map/ppermute | solution.py:216
  72.8 5.5 %collective-permute-start.24 = (f32[256,256]{1,0:T(8,128)S(1)}, f32[256,256]{1,0:T(8,128)S(1)}, u32[]{:S(2)}, u32[]{:S(2)}) collective-permute-start(f32[256,256]{1,0:T(8,128)S(1)} %shard_map.95), channel_id=1, source_target_pairs={{0,1},{4,0},{1,2},{5,4},{2,3},{6,5},{3,7},{7,6},{8,9},{12,8},{9,10... | collective-permute-start | bytes 786440 | tf_op jit(solution)/shard_map/line_15/ppermute | solution.py:211
  (4 other events, 12.2 us)
